TPU v7x, 32 devices: a whole 2x2x4 slice. The times are simulated.
32 devices in a mesh: dp: 8 (over y, x, core), tensor: 4 (over z).
Axes of the slice: x: 2, y: 2, z: 4, core: 2. Of those that a mesh axis runs over, the one named last changes fastest.
Arguments:
- tokens: bfloat16 [25088, 1024], P(('dp', 'tensor')), may hold values from -6 to 6
- cotangent: bfloat16 [25088, 1024], P(('dp', 'tensor')), may hold values from -6 to 6
- norm_first: float32 [1024], replicated, may hold values from 0.1 to 1.9
- norm_second: float32 [1024], replicated, may hold values from 0.1 to 1.9
- entry_weight: bfloat16 [1024, 3, 1024], P('dp', None, 'tensor'), may hold values from -0.1875 to 0.1875
- output_weight: bfloat16 [1024, 1024], P('dp', 'tensor'), may hold values from -4 to 4
- expand_weight: bfloat16 [1024, 4096], P('dp', 'tensor'), may hold values from -0.1875 to 0.1875
- shrink_weight: bfloat16 [1024, 4096], P('dp', 'tensor'), may hold values from -0.09375 to 0.09375
- entry_down: bfloat16 [8, 1024, 16], replicated, may hold values from -0.1875 to 0.1875
- entry_up: bfloat16 [8, 16, 3, 1024], P(None, None, None, 'tensor'), may hold values from -1 to 1
- output_down: bfloat16 [8, 1024, 16], P(None, 'tensor'), may hold values from -4 to 4
- output_up: bfloat16 [8, 16, 1024], replicated, may hold values from -1.5 to 1.5
- expand_down: bfloat16 [8, 1024, 16], replicated, may hold values from -0.1875 to 0.1875
- expand_up: bfloat16 [8, 16, 4096], P(None, None, 'tensor'), may hold values from -1 to 1
- shrink_down: bfloat16 [8, 4096, 16], P(None, 'tensor'), may hold values from -0.09375 to 0.09375
- shrink_up: bfloat16 [8, 16, 1024], replicated, may hold values from -1 to 1
- adapter_choice: int32 [16], P('dp'), may hold values from 0 to 7
- clip_count: int32 [8], P('dp'), may hold values from 1 to 2, as said below
Outputs:
- mixed: bfloat16 [25088, 1024], P(('dp', 'tensor'))
- token_grad: bfloat16 [25088, 1024], P(('dp', 'tensor'))
- entry_down_grad: float32 [8, 1024, 16], replicated
- entry_up_grad: float32 [8, 16, 3, 1024], P(None, None, None, 'tensor')
- output_down_grad: float32 [8, 1024, 16], P(None, 'tensor')
- output_up_grad: float32 [8, 16, 1024], replicated
- expand_down_grad: float32 [8, 1024, 16], replicated
- expand_up_grad: float32 [8, 16, 4096], P(None, None, 'tensor')
- shrink_down_grad: float32 [8, 4096, 16], P(None, 'tensor')
- shrink_up_grad: float32 [8, 16, 1024], replicated
Inputs may be any that keep to these rules, and one draw needn't show every extreme that they name: The first clip_count[i] of the 2 slots of dp index i hold clips, the rest are empty; some index has all 2 slots live.
All inputs are finite; a program needn't handle non-finite values.
Results may differ from a plain program's by a relative error of at most 0.02.
Values may be sent and summed in bfloat16 or wider, within the bound.
A program may use at most 256 MiB of HBM per device.

v0:
```python
import jax
import jax.numpy as jnp
from jax import lax
from jax.sharding import PartitionSpec as P

HEAD_DIM = 64


highest_precision = lax.Precision.HIGHEST


def normalize(values):
    centre = jnp.mean(values, axis=-1, keepdims=True)
    shifted = values - centre
    spread = jnp.mean(shifted * shifted, axis=-1, keepdims=True)
    return shifted * lax.rsqrt(spread + 1e-05)


def scaled_norm(values, gain):
    return normalize(values) * gain


def exact_gelu(values):
    return jax.nn.gelu(values, approximate=False)


def select(onehot_low, table):
    return jnp.einsum("cn,n...->c...", onehot_low, table, preferred_element_type=jnp.float32)


def per_adapter(onehot_float, per_clip):
    return jnp.einsum("cn,c...->n...", onehot_float, per_clip, precision=highest_precision)


def local(
    tokens,
    cotangent,
    norm_first,
    norm_second,
    entry_weight,
    output_weight,
    expand_weight,
    shrink_weight,
    entry_down,
    entry_up,
    output_down,
    output_up,
    expand_down,
    expand_up,
    shrink_down,
    shrink_up,
    adapter_choice,
    clip_count,
):
    capacity = adapter_choice.shape[0]
    local_rows, model_width = tokens.shape
    total_rows = local_rows * lax.axis_size("tensor")
    length = total_rows // capacity
    adapters_count = entry_down.shape[0]
    head_dim = HEAD_DIM
    local_width = entry_weight.shape[2]
    local_heads = local_width // head_dim
    hidden_width = expand_weight.shape[1]
    score_scale = head_dim ** (-0.5)
    row_start = lax.axis_index("tensor") * local_rows
    row_index = row_start + lax.iota(jnp.int32, local_rows)
    alive_rows = (row_index // length < clip_count[0]).astype(jnp.float32)[:, None]
    onehot = adapter_choice[:, None] == lax.iota(jnp.int32, adapters_count)[None, :]
    onehot_low = onehot.astype(jnp.bfloat16)
    onehot_float = onehot.astype(jnp.float32)
    select_entry_down = select(onehot_low, entry_down)
    select_entry_up = select(onehot_low, entry_up)
    select_output_down = select(onehot_low, output_down)
    select_output_up = select(onehot_low, output_up)
    select_expand_down = select(onehot_low, expand_down)
    select_expand_up = select(onehot_low, expand_up)
    select_shrink_down = select(onehot_low, shrink_down)
    select_shrink_up = select(onehot_low, shrink_up)
    full_entry, full_output, full_expand, full_shrink = (
        lax.all_gather(entry_weight, "dp", axis=0, tiled=True),
        lax.all_gather(output_weight, "dp", axis=0, tiled=True),
        lax.all_gather(expand_weight, "dp", axis=0, tiled=True),
        lax.all_gather(shrink_weight, "dp", axis=0, tiled=True),
    )
    inputs = tokens.astype(jnp.float32)
    normed_local = scaled_norm(inputs, norm_first).astype(jnp.bfloat16)
    normed_full = lax.all_gather(normed_local, "tensor", axis=0, tiled=True)
    normed_clips = normed_full.reshape(capacity, length, model_width)
    entry_lowrank_path = jnp.einsum(
        "hza,haj->hzj",
        normed_clips,
        select_entry_down.astype(jnp.bfloat16),
        preferred_element_type=jnp.float32,
    )
    projected_rows = jnp.einsum(
        "td,dje->tje", normed_full, full_entry, preferred_element_type=jnp.float32
    ).reshape(capacity, length, 3, local_width)
    projected_rows = (
        projected_rows
        + jnp.einsum(
            "ftz,fzqx->ftqx", entry_lowrank_path, select_entry_up, precision=highest_precision
        )
    ).astype(jnp.bfloat16)
    queries = projected_rows[:, :, 0].reshape(capacity, length, local_heads, head_dim)
    keys_all = projected_rows[:, :, 1].reshape(capacity, length, local_heads, head_dim)
    values_all = projected_rows[:, :, 2].reshape(capacity, length, local_heads, head_dim)

    def attend(clip_parts):
        query_clip, key_clip, value_clip = clip_parts
        scores = (
            jnp.einsum("qhd,khd->hqk", query_clip, key_clip, preferred_element_type=jnp.float32)
            * score_scale
        )
        row_top = jnp.max(scores, axis=-1, keepdims=True)
        exponent = jnp.exp(scores - row_top)
        row_total = jnp.sum(exponent, axis=-1, keepdims=True)
        probs_low = (exponent / row_total).astype(jnp.bfloat16)
        result = jnp.einsum(
            "hqk,khd->qhd", probs_low, value_clip, preferred_element_type=jnp.float32
        )
        return (result.astype(jnp.bfloat16), (row_top + jnp.log(row_total))[..., 0])

    attended, logsum = lax.map(attend, (queries, keys_all, values_all))
    attended_flat = attended.reshape(capacity, length, local_width)
    output_lowrank_path = jnp.einsum(
        "ktx,kxg->ktg",
        attended_flat,
        select_output_down.astype(jnp.bfloat16),
        preferred_element_type=jnp.float32,
    )
    branch = jnp.einsum(
        "ti,oi->to",
        attended_flat.reshape(total_rows, local_width),
        full_output,
        preferred_element_type=jnp.float32,
    )
    branch = branch + jnp.einsum(
        "htu,hud->htd", output_lowrank_path, select_output_up, precision=highest_precision
    ).reshape(total_rows, model_width)
    middle = inputs + lax.psum_scatter(
        branch.astype(jnp.bfloat16), "tensor", scatter_dimension=0, tiled=True
    ).astype(jnp.float32)
    second_local = scaled_norm(middle, norm_second).astype(jnp.bfloat16)
    second_full = lax.all_gather(second_local, "tensor", axis=0, tiled=True)
    second_clips = second_full.reshape(capacity, length, model_width)
    expand_lowrank_path = jnp.einsum(
        "hza,haj->hzj",
        second_clips,
        select_expand_down.astype(jnp.bfloat16),
        preferred_element_type=jnp.float32,
    )
    hidden_activation = jnp.dot(
        second_full, full_expand, preferred_element_type=jnp.float32
    ).reshape(capacity, length, hidden_width)
    hidden_activation = hidden_activation + jnp.einsum(
        "ujb,ubk->ujk", expand_lowrank_path, select_expand_up, precision=highest_precision
    )
    activated = exact_gelu(hidden_activation).astype(jnp.bfloat16)
    shrink_lowrank_path = jnp.einsum(
        "omh,ohq->omq",
        activated,
        select_shrink_down.astype(jnp.bfloat16),
        preferred_element_type=jnp.float32,
    )
    branch_two = jnp.einsum(
        "tf,of->to",
        activated.reshape(total_rows, hidden_width),
        full_shrink,
        preferred_element_type=jnp.float32,
    )
    branch_two = branch_two + jnp.einsum(
        "htu,hud->htd", shrink_lowrank_path, select_shrink_up, precision=highest_precision
    ).reshape(total_rows, model_width)
    output_rows = middle + lax.psum_scatter(
        branch_two.astype(jnp.bfloat16), "tensor", scatter_dimension=0, tiled=True
    ).astype(jnp.float32)
    mixed = (alive_rows * output_rows).astype(jnp.bfloat16)
    grad_out = alive_rows * cotangent.astype(jnp.float32)
    branch_grad = lax.all_gather(grad_out.astype(jnp.bfloat16), "tensor", axis=0, tiled=True)
    branch_clips = branch_grad.reshape(capacity, length, model_width)
    shrink_pullback_fn = jnp.einsum(
        "uaq,uiq->uai",
        branch_clips,
        select_shrink_up.astype(jnp.bfloat16),
        preferred_element_type=jnp.float32,
    )
    activated_grad = jnp.dot(branch_grad, full_shrink, preferred_element_type=jnp.float32).reshape(
        capacity, length, hidden_width
    )
    activated_grad = activated_grad + jnp.einsum(
        "igh,ieh->ige", shrink_pullback_fn, select_shrink_down, precision=highest_precision
    )
    shrink_down_clip = jnp.einsum(
        "fko,fkl->fol",
        activated,
        shrink_pullback_fn,
        preferred_element_type=jnp.float32,
        precision=highest_precision,
    )
    shrink_up_clip = jnp.einsum(
        "iez,iej->izj",
        shrink_lowrank_path,
        branch_clips,
        preferred_element_type=jnp.float32,
        precision=highest_precision,
    )
    _, gelu_back = jax.vjp(exact_gelu, hidden_activation)
    hidden_grad = gelu_back(activated_grad)[0].astype(jnp.bfloat16)
    expand_pullback_fn = jnp.einsum(
        "yud,ynd->yun",
        hidden_grad,
        select_expand_up.astype(jnp.bfloat16),
        preferred_element_type=jnp.float32,
    )
    second_grad = jnp.einsum(
        "tf,df->td",
        hidden_grad.reshape(total_rows, hidden_width),
        full_expand,
        preferred_element_type=jnp.float32,
    )
    second_grad = second_grad + jnp.einsum(
        "jpg,jhg->jph", expand_pullback_fn, select_expand_down, precision=highest_precision
    ).reshape(total_rows, model_width)
    expand_up_clip = jnp.einsum(
        "npw,npj->nwj",
        expand_lowrank_path,
        hidden_grad,
        preferred_element_type=jnp.float32,
        precision=highest_precision,
    )
    expand_down_clip = jnp.einsum(
        "spm,spt->smt",
        second_clips,
        expand_pullback_fn,
        preferred_element_type=jnp.float32,
        precision=highest_precision,
    )
    second_local_grad = lax.psum_scatter(
        second_grad.astype(jnp.bfloat16), "tensor", scatter_dimension=0, tiled=True
    ).astype(jnp.float32)
    _, second_back = jax.vjp(scaled_norm, middle, norm_second)
    middle_grad = grad_out + second_back(second_local_grad)[0]
    first_branch = lax.all_gather(middle_grad.astype(jnp.bfloat16), "tensor", axis=0, tiled=True)
    first_clips = first_branch.reshape(capacity, length, model_width)
    output_pullback_fn = jnp.einsum(
        "uaq,uiq->uai",
        first_clips,
        select_output_up.astype(jnp.bfloat16),
        preferred_element_type=jnp.float32,
    )
    attended_grad = jnp.dot(first_branch, full_output, preferred_element_type=jnp.float32).reshape(
        capacity, length, local_width
    )
    attended_grad = attended_grad + jnp.einsum(
        "ynm,ykm->ynk", output_pullback_fn, select_output_down, precision=highest_precision
    )
    output_down_clip = jnp.einsum(
        "mkx,mka->mxa",
        attended_flat,
        output_pullback_fn,
        preferred_element_type=jnp.float32,
        precision=highest_precision,
    )
    output_up_clip = jnp.einsum(
        "iez,iej->izj",
        output_lowrank_path,
        first_clips,
        preferred_element_type=jnp.float32,
        precision=highest_precision,
    )
    attended_low = attended_grad.astype(jnp.bfloat16).reshape(
        capacity, length, local_heads, head_dim
    )

    def attend_back(clip_parts):
        query_clip, key_clip, value_clip, grad_clip, logsum_clip = clip_parts
        scores = (
            jnp.einsum("qhd,khd->hqk", query_clip, key_clip, preferred_element_type=jnp.float32)
            * score_scale
        )
        probs = jnp.exp(scores - logsum_clip[..., None])
        probs_low = probs.astype(jnp.bfloat16)
        value_grad = jnp.einsum(
            "hqk,qhd->khd", probs_low, grad_clip, preferred_element_type=jnp.float32
        )
        prob_grad = jnp.einsum(
            "qhd,khd->hqk", grad_clip, value_clip, preferred_element_type=jnp.float32
        )
        score_grad = (
            probs * (prob_grad - jnp.sum(probs * prob_grad, axis=-1, keepdims=True))
        ).astype(jnp.bfloat16)
        query_grad = (
            jnp.einsum("hqk,khd->qhd", score_grad, key_clip, preferred_element_type=jnp.float32)
            * score_scale
        )
        key_grad = (
            jnp.einsum("hqk,qhd->khd", score_grad, query_clip, preferred_element_type=jnp.float32)
            * score_scale
        )
        return jnp.stack([query_grad, key_grad, value_grad], axis=1).astype(jnp.bfloat16)

    projected_grad = lax.map(
        attend_back, (queries, keys_all, values_all, attended_low, logsum)
    ).reshape(capacity, length, 3, local_width)
    entry_pullback_fn = jnp.einsum(
        "tvkb,tgkb->tvg",
        projected_grad,
        select_entry_up.astype(jnp.bfloat16),
        preferred_element_type=jnp.float32,
    )
    first_grad = jnp.einsum(
        "tje,dje->td",
        projected_grad.reshape(total_rows, 3, local_width),
        full_entry,
        preferred_element_type=jnp.float32,
    )
    first_grad = first_grad + jnp.einsum(
        "jpg,jhg->jph", entry_pullback_fn, select_entry_down, precision=highest_precision
    ).reshape(total_rows, model_width)
    entry_up_clip = jnp.einsum(
        "tqn,tqxa->tnxa",
        entry_lowrank_path,
        projected_grad,
        preferred_element_type=jnp.float32,
        precision=highest_precision,
    )
    entry_down_clip = jnp.einsum(
        "spm,spt->smt",
        normed_clips,
        entry_pullback_fn,
        preferred_element_type=jnp.float32,
        precision=highest_precision,
    )
    first_local_grad = lax.psum_scatter(
        first_grad.astype(jnp.bfloat16), "tensor", scatter_dimension=0, tiled=True
    ).astype(jnp.float32)
    _, first_back = jax.vjp(scaled_norm, inputs, norm_first)
    token_grad = (middle_grad + first_back(first_local_grad)[0]).astype(jnp.bfloat16)
    entry_up_grad, output_down_grad, expand_up_grad, shrink_down_grad = (
        lax.psum(per_adapter(onehot_float, entry_up_clip).astype(jnp.bfloat16), "dp").astype(
            jnp.float32
        ),
        lax.psum(per_adapter(onehot_float, output_down_clip).astype(jnp.bfloat16), "dp").astype(
            jnp.float32
        ),
        lax.psum(per_adapter(onehot_float, expand_up_clip).astype(jnp.bfloat16), "dp").astype(
            jnp.float32
        ),
        lax.psum(per_adapter(onehot_float, shrink_down_clip).astype(jnp.bfloat16), "dp").astype(
            jnp.float32
        ),
    )
    entry_down_grad, output_up_grad, expand_down_grad, shrink_up_grad = lax.psum(
        (
            per_adapter(onehot_float, entry_down_clip),
            per_adapter(onehot_float, output_up_clip),
            per_adapter(onehot_float, expand_down_clip),
            per_adapter(onehot_float, shrink_up_clip),
        ),
        ("dp", "tensor"),
    )
    return (
        mixed,
        token_grad,
        entry_down_grad,
        entry_up_grad,
        output_down_grad,
        output_up_grad,
        expand_down_grad,
        expand_up_grad,
        shrink_down_grad,
        shrink_up_grad,
    )


def solution(mesh):
    in_specs = (
        P(("dp", "tensor"), None),
        P(("dp", "tensor"), None),
        P(),
        P(),
        P("dp", None, "tensor"),
        P("dp", "tensor"),
        P("dp", "tensor"),
        P("dp", "tensor"),
        P(),
        P(None, None, None, "tensor"),
        P(None, "tensor", None),
        P(),
        P(),
        P(None, None, "tensor"),
        P(None, "tensor", None),
        P(),
        P("dp"),
        P("dp"),
    )
    out_specs = (
        P(("dp", "tensor"), None),
        P(("dp", "tensor"), None),
        P(),
        P(None, None, None, "tensor"),
        P(None, "tensor", None),
        P(),
        P(),
        P(None, None, "tensor"),
        P(None, "tensor", None),
        P(),
    )
    return jax.shard_map(local, mesh=mesh, in_specs=in_specs, out_specs=out_specs, check_vma=False)
```

profile of v0, /device:TPU:0, one launch (start us, length us, event | category | flops | bytes accessed | tf_op | source)
XLA Modules:
  0.0 1845.9 jit_solution(6975274509266592190)
XLA Ops:
  31.7 103.5 %all-gather.8.cloned.1.call-done = bf16[3136,1024]{1,0:T(8,128)(2,1)} async-done(((bf16[784,1024]{1,0:T(8,128)(2,1)}), bf16[3136,1024]{1,0:T(8,128)(2,1)}) %all-gather.8.cloned.1.call-update) | async-done | bytes 6422544 | tf_op jit(solution)/shard_map/all_gather | solution.py:87
  139.9 21.3 %all-gather.10.cloned.1.call-done = bf16[1024,3,256]{2,0,1:T(8,128)(2,1)} async-done(((bf16[128,3,256]{2,0,1:T(8,128)(2,1)}), bf16[1024,3,256]{2,0,1:T(8,128)(2,1)}) %all-gather.10.cloned.1.call-update) | async-done | bytes 1572880 | tf_op jit(solution)/shard_map/all_gather | solution.py:80
  189.7 106.2 %while.22 = (s32[]{:T(128)}, bf16[2,1568,4,64]{1,3,2,0:T(8,128)(2,1)}, f32[2,4,1568]{2,1,0:T(4,128)}, bf16[2,1568,4,64]{1,3,2,0:T(8,128)(2,1)}, bf16[2,1568,4,64...) while((s32[]{:T(128)}, bf16[2,1568,4,64]{1,3,2,0:T(8,128)(2,1)}, ...), condition=%wide.region_5.6_spmd, body=%wide.region_2.5_spmd.sunk | while | flops 2606536704 | bytes 124034640 | solution.py:123
  326.7 109.5 %reduce-scatter.5.cloned.1.call-done = bf16[784,1024]{1,0:T(8,128)(2,1)} async-done(((bf16[3136,1024]{1,0:T(8,128)(2,1)}), bf16[784,1024]{1,0:T(8,128)(2,1)}) %reduce-scatter.5.cloned.1.call-update) | async-done | bytes 1605648 | tf_op jit(solution)/shard_map/reduce_scatter | solution.py:140
  450.8 105.4 %all-gather.18.cloned.1.call-done = bf16[3136,1024]{1,0:T(8,128)(2,1)} async-done(((bf16[784,1024]{1,0:T(8,128)(2,1)}), bf16[3136,1024]{1,0:T(8,128)(2,1)}) %all-gather.18.cloned.1.call-update) | async-done | bytes 6422544 | tf_op jit(solution)/shard_map/all_gather | solution.py:179
  561.5 22.6 %all-gather.16.cloned.1.call-done = bf16[1024,1024]{1,0:T(8,128)(2,1)} async-done(((bf16[128,1024]{1,0:T(8,128)(2,1)}), bf16[1024,1024]{1,0:T(8,128)(2,1)}) %all-gather.16.cloned.1.call-update) | async-done | bytes 2097168 | tf_op jit(solution)/shard_map/all_gather | solution.py:83
  597.0 106.6 %all-gather.12.cloned.1.call-done = bf16[3136,1024]{1,0:T(8,128)(2,1)} async-done(((bf16[784,1024]{1,0:T(8,128)(2,1)}), bf16[3136,1024]{1,0:T(8,128)(2,1)}) %all-gather.12.cloned.1.call-update) | async-done | bytes 6422544 | tf_op jit(solution)/shard_map/all_gather | solution.py:144
  708.9 22.8 %all-gather.14.cloned.1.call-done = bf16[1024,1024]{1,0:T(8,128)(2,1)} async-done(((bf16[128,1024]{1,0:T(8,128)(2,1)}), bf16[1024,1024]{1,0:T(8,128)(2,1)}) %all-gather.14.cloned.1.call-update) | async-done | bytes 2097168 | tf_op jit(solution)/shard_map/all_gather | solution.py:82
  744.7 20.6 %fusion.70 = (u8[1568,1024]{1,0:T(8,128)(4,1)S(1)}, u8[1568,1024]{1,0:T(8,128)(4,1)S(1)}, f32[2,1568,1024]{2,1,0:T(8,128)}) fusion(f32[2,1568,1024]{2,1,0:T(8,128)} %bitcast.273, f32[2,1568,16]{1,2,0:T(8,128)S(1)} %copy-done.22, f32[2,16,1024]{2,0,1:T(2,128)S(1)} %copy-done.43), kind=kOutput, calls=%fused_computation.113 | convolution fusion | flops 658309120 | bytes 29233152 | tf_op jit(solution)/shard_map/ujb,ubk->ujk/dot_general | solution.py:155
  765.3 31.9 %multiply_convert_fusion.1 = (bf16[2,1568,1024]{2,1,0:T(8,128)(2,1)}, f32[2,1568,1024]{2,1,0:T(8,128)}) fusion(f32[2,1568,1024]{2,1,0:T(8,128)} %get-tuple-element.170, u8[1568,1024]{1,0:T(8,128)(4,1)S(1)} %get-tuple-element.117, u8[1568,1024]{1,0:T(8,128)(4,1)S(1)} %get-tuple-element.116), kind=kLoop, calls=%fused_computation.70 | loop fusion | flops 224788480 | bytes 35323904 | tf_op jit(solution)/shard_map/convert_element_type | solution.py:158
  797.2 21.8 %add_convert_fusion = bf16[2,1568,1024]{2,1,0:T(8,128)(2,1)} fusion(f32[2,1568,1024]{2,1,0:T(8,128)} %get-tuple-element.155, f32[2,1568,1024]{2,1,0:T(8,128)} %bitcast.272, f32[2,1568,1024]{2,1,0:T(8,128)} %get-tuple-element.170, f32[2,1568,16]{1,2,0:T(8,128)S(1)} %copy-done.29, f32[2,1024,16]{1,0,2:T(2,128)S(1)} %copy-done.42), kind=kOutput, calls=%fused_computation.69 | convolution fusion | flops 664731648 | bytes 45289472 | tf_op jit(solution)/shard_map/igh,ieh->ige/dot_general | solution.py:190
  880.5 81.8 %reduce-scatter.9.cloned.1.call-done = bf16[784,1024]{1,0:T(8,128)(2,1)} async-done(((bf16[3136,1024]{1,0:T(8,128)(2,1)}), bf16[784,1024]{1,0:T(8,128)(2,1)}) %reduce-scatter.9.cloned.1.call-update) | async-done | bytes 1605648 | tf_op jit(solution)/shard_map/reduce_scatter | solution.py:238
  964.7 113.3 %reduce-scatter.7.cloned.1.call-done = bf16[784,1024]{1,0:T(8,128)(2,1)} async-done(((bf16[3136,1024]{1,0:T(8,128)(2,1)}), bf16[784,1024]{1,0:T(8,128)(2,1)}) %reduce-scatter.7.cloned.1.call-update) | async-done | bytes 1605648 | tf_op jit(solution)/shard_map/reduce_scatter | solution.py:174
  1107.3 97.1 %all-gather.20.cloned.1.call-done = bf16[3136,1024]{1,0:T(8,128)(2,1)} async-done(((bf16[784,1024]{1,0:T(8,128)(2,1)}), bf16[3136,1024]{1,0:T(8,128)(2,1)}) %all-gather.20.cloned.1.call-update) | async-done | bytes 6422544 | tf_op jit(solution)/shard_map/all_gather | solution.py:243
  1224.3 247.5 %while.23 = (s32[]{:T(128)}, bf16[2,1568,3,4,64]{1,4,3,2,0:T(8,128)(2,1)}, bf16[2,1568,4,64]{1,3,2,0:T(8,128)(2,1)S(1)}, bf16[2,1568,4,64]{1,3,2,0:T(8,128)(2,1)...) while((s32[]{:T(128)}, ...), condition=%wide.region_15.16_spmd, body=%wide.region_13.15_spmd.sunk | while | flops 6381979648 | bytes 323803296 | solution.py:302
  1225.2 20.9 %fusion.264 = f32[4,1568,1568]{1,2,0:T(8,128)} fusion(bf16[2,1568,4,64]{1,3,2,0:T(8,128)(2,1)} %get-tuple-element.312, s32[]{:T(128)S(6)} %copy.238, bf16[2,1568,4,64]{1,3,2,0:T(8,128)(2,1)} %get-tuple-element.311), kind=kOutput, calls=%fused_computation.33.clone.1 | convolution fusion | flops 1258815488 | bytes 41042944 | tf_op jit(solution)/shard_map/while/body/eval_jaxpr/qhd,khd->hqk/dot_general | solution.py:286
  1246.1 27.1 %multiply_reduce_fusion.7 = (f32[4,1568]{1,0:T(4,128)S(1)}, f32[4,1568,1568]{1,2,0:T(8,128)}) fusion(f32[4,1568,1568]{1,2,0:T(8,128)} %fusion.264, f32[4,1568]{1,0:T(4,128)S(1)} %dynamic-slice_bitcast_fusion.2, bf16[2,1568,4,64]{1,3,2,0:T(8,128)(2,1)S(1)} %get-tuple-element.308, s32[]{:T(128)S(6)} %copy.238, bf16[2,1568,4,64]{1,3,2,0:T(8,128)(2,1)S(1)} %copy-done.6), kind=kOutput, calls=%fused_computation.20.clone.1 | convolution fusion | flops 1298147200 | bytes 80432640 | tf_op jit(solution)/shard_map/while/body/eval_jaxpr/qhd,khd->hqk/dot_general | solution.py:278
  1273.2 33.5 %multiply_convert_fusion.5 = bf16[4,1568,1568]{1,2,0:T(8,128)(2,1)} fusion(f32[4,1568,1568]{1,2,0:T(8,128)} %get-tuple-element.267, f32[4,1568,1568]{1,2,0:T(8,128)} %fusion.264, f32[4,1568]{1,0:T(4,128)S(1)} %get-tuple-element.268), kind=kLoop, calls=%fused_computation.19.clone.1 | loop fusion | flops 29503488 | bytes 98370048 | tf_op jit(solution)/shard_map/while/body/eval_jaxpr/convert_element_type | solution.py:291
  1348.9 20.9 %fusion.264 = f32[4,1568,1568]{1,2,0:T(8,128)} fusion(bf16[2,1568,4,64]{1,3,2,0:T(8,128)(2,1)} %get-tuple-element.312, s32[]{:T(128)S(6)} %copy.238, bf16[2,1568,4,64]{1,3,2,0:T(8,128)(2,1)} %get-tuple-element.311), kind=kOutput, calls=%fused_computation.33.clone.1 | convolution fusion | flops 1258815488 | bytes 41042944 | tf_op jit(solution)/shard_map/while/body/eval_jaxpr/qhd,khd->hqk/dot_general | solution.py:286
  1369.8 27.1 %multiply_reduce_fusion.7 = (f32[4,1568]{1,0:T(4,128)S(1)}, f32[4,1568,1568]{1,2,0:T(8,128)}) fusion(f32[4,1568,1568]{1,2,0:T(8,128)} %fusion.264, f32[4,1568]{1,0:T(4,128)S(1)} %dynamic-slice_bitcast_fusion.2, bf16[2,1568,4,64]{1,3,2,0:T(8,128)(2,1)S(1)} %get-tuple-element.308, s32[]{:T(128)S(6)} %copy.238, bf16[2,1568,4,64]{1,3,2,0:T(8,128)(2,1)S(1)} %copy-done.6), kind=kOutput, calls=%fused_computation.20.clone.1 | convolution fusion | flops 1298147200 | bytes 80432640 | tf_op jit(solution)/shard_map/while/body/eval_jaxpr/qhd,khd->hqk/dot_general | solution.py:278
  1396.8 33.5 %multiply_convert_fusion.5 = bf16[4,1568,1568]{1,2,0:T(8,128)(2,1)} fusion(f32[4,1568,1568]{1,2,0:T(8,128)} %get-tuple-element.267, f32[4,1568,1568]{1,2,0:T(8,128)} %fusion.264, f32[4,1568]{1,0:T(4,128)S(1)} %get-tuple-element.268), kind=kLoop, calls=%fused_computation.19.clone.1 | loop fusion | flops 29503488 | bytes 98370048 | tf_op jit(solution)/shard_map/while/body/eval_jaxpr/convert_element_type | solution.py:291
  1536.9 39.5 %all-reduce.7.cloned.1.call-done = (bf16[8,16,3,256]{3,0,2,1:T(8,128)(2,1)}, bf16[8,256,16]{1,0,2:T(8,128)(2,1)}, bf16[8,16,1024]{2,0,1:T(8,128)(2,1)}, bf16[8,1024,16]{1,0,2:T(8,128)(2,1)}) async-done(((bf16[8,16,3,256]{3,0,2,1:T(8,128)(2,1)}, bf16[8,256,16]{1,0,2:T(8,128)(2,1)}, bf16[8,16,1024]{2,0,1:T(8,128)(2,1)}, bf16[8,1024,16]{1,0,2:T(8,128)(2,1)}), (bf16[8,16,3,256]{3,0,2,1:T(8,128)(2,1)}, ...) | async-done | bytes 786448 | tf_op jit(solution)/shard_map/psum | solution.py:340
  1583.6 133.6 %all-reduce.5.cloned.1.call-done = (f32[8,1024,16]{1,0,2:T(8,128)}, f32[8,16,1024]{2,0,1:T(8,128)}, f32[8,1024,16]{1,0,2:T(8,128)}, f32[8,16,1024]{2,0,1:T(8,128)}) async-done(((f32[8,1024,16]{1,0,2:T(8,128)}, f32[8,16,1024]{2,0,1:T(8,128)}, f32[8,1024,16]{1,0,2:T(8,128)}, f32[8,16,1024]{2,0,1:T(8,128)}), (f32[8,1024,16]{1,0,2:T(8,128)}, f32[8,16,1024]{2,0,1:T(8,128)}, f32[8,1024,16]{1,0,2:T(8,128)}, ...) | async-done | bytes 2097168 | tf_op jit(solution)/shard_map/psum | solution.py:353
  1725.9 105.5 %reduce-scatter.11.cloned.1.call-done = bf16[784,1024]{1,0:T(8,128)(2,1)} async-done(((bf16[3136,1024]{1,0:T(8,128)(2,1)}), bf16[784,1024]{1,0:T(8,128)(2,1)}) %reduce-scatter.11.cloned.1.call-update) | async-done | bytes 1605648 | tf_op jit(solution)/shard_map/reduce_scatter | solution.py:334
  (283 shorter events, 529.8 us)
Async XLA Ops:
  7.2 128.0 %all-gather.8.cloned.1.call-start = ((), (), s32[]{:S(2)}) async-start(), calls=%async_computation.4 | async-start | bytes 8028160 | tf_op jit(solution)/shard_map/all_gather | solution.py:87
  14.9 146.2 %all-gather.10.cloned.1.call-start = ((), (), s32[]{:S(2)}) async-start(), calls=%async_computation.5 | async-start | bytes 1769472 | tf_op jit(solution)/shard_map/all_gather | solution.py:80
  15.7 420.5 %reduce-scatter.5.cloned.1.call-start = ((), (), s32[]{:S(2)}) async-start(), calls=%async_computation.6 | async-start | bytes 8028160 | tf_op jit(solution)/shard_map/reduce_scatter | solution.py:140
  323.2 117.2 %copy-start.59 = (f32[1024]{0:T(1024)S(1)}, f32[1024]{0:T(1024)}, u32[]{:S(2)}) copy-start(f32[1024]{0:T(1024)} %param.25) | copy-start | bytes 12292
  323.2 233.1 %all-gather.18.cloned.1.call-start = ((), (), s32[]{:S(2)}) async-start(), calls=%async_computation.11 | async-start | bytes 8028160 | tf_op jit(solution)/shard_map/all_gather | solution.py:179
  324.6 758.3 %copy-start.47 = (f32[784]{0:T(1024)}, f32[784]{0:T(1024)S(1)}, u32[]{:S(2)}) copy-start(f32[784]{0:T(1024)S(1)} %fusion.131) | copy-start | bytes 9412
  326.1 258.0 %all-gather.16.cloned.1.call-start = ((), (), s32[]{:S(2)}) async-start(), calls=%async_computation.9 | async-start | bytes 2359296 | tf_op jit(solution)/shard_map/all_gather | solution.py:83
  326.7 116.4 %copy-start.45 = (s32[2]{0:T(128)S(1)}, s32[2]{0:T(128)}, u32[]{:S(2)}) copy-start(s32[2]{0:T(128)} %param.38) | copy-start | bytes 28
  326.7 377.0 %all-gather.12.cloned.1.call-start = ((), (), s32[]{:S(2)}) async-start(), calls=%async_computation.7 | async-start | bytes 8028160 | tf_op jit(solution)/shard_map/all_gather | solution.py:144
  442.3 289.4 %all-gather.14.cloned.1.call-start = ((), (), s32[]{:S(2)}) async-start(), calls=%async_computation.8 | async-start | bytes 2359296 | tf_op jit(solution)/shard_map/all_gather | solution.py:82
  443.0 519.2 %reduce-scatter.9.cloned.1.call-start = ((), (), s32[]{:S(2)}) async-start(), calls=%async_computation.12 | async-start | bytes 8028160 | tf_op jit(solution)/shard_map/reduce_scatter | solution.py:238
  849.2 228.8 %reduce-scatter.7.cloned.1.call-start = ((), (), s32[]{:S(2)}) async-start(), calls=%async_computation.10 | async-start | bytes 8028160 | tf_op jit(solution)/shard_map/reduce_scatter | solution.py:174
  880.4 323.9 %all-gather.20.cloned.1.call-start = ((), (), s32[]{:S(2)}) async-start(), calls=%async_computation.13 | async-start | bytes 8028160 | tf_op jit(solution)/shard_map/all_gather | solution.py:243
  1086.2 490.2 %all-reduce.7.cloned.1.call-start = ((), (), s32[]{:S(2)}) async-start(), calls=%async_computation.16 | async-start | bytes 1572864 | tf_op jit(solution)/shard_map/psum | solution.py:340
  1522.1 195.0 %all-reduce.5.cloned.1.call-start = ((), (), s32[]{:S(2)}) async-start(), calls=%async_computation.15 | async-start | bytes 4194304 | tf_op jit(solution)/shard_map/psum | solution.py:353
  1524.8 306.5 %reduce-scatter.11.cloned.1.call-start = ((), (), s32[]{:S(2)}) async-start(), calls=%async_computation.14 | async-start | bytes 8028160 | tf_op jit(solution)/shard_map/reduce_scatter | solution.py:334
  1536.9 294.5 %copy-start.3 = (bf16[784,1024]{1,0:T(8,128)(2,1)S(1)}, bf16[784,1024]{1,0:T(8,128)(2,1)}, u32[]{:S(2)}) copy-start(bf16[784,1024]{1,0:T(8,128)(2,1)} %param.22) | copy-start | bytes 4816900
  1536.9 294.5 %copy-start.40 = (f32[784]{0:T(1024)S(1)}, f32[784]{0:T(1024)}, u32[]{:S(2)}) copy-start(f32[784]{0:T(1024)} %copy-done.39) | copy-start | bytes 9412
  1536.9 294.5 %copy-start.49 = (f32[1024]{0:T(1024)S(1)}, f32[1024]{0:T(1024)}, u32[]{:S(2)}) copy-start(f32[1024]{0:T(1024)} %param.24) | copy-start | bytes 12292
  1536.9 296.8 %copy-start.58 = (f32[784]{0:T(1024)S(1)}, f32[784]{0:T(1024)}, u32[]{:S(2)}) copy-start(f32[784]{0:T(1024)} %copy-done.57) | copy-start | bytes 9412
  1536.9 296.9 %copy-start.51 = (f32[784]{0:T(1024)S(1)}, f32[784]{0:T(1024)}, u32[]{:S(2)}) copy-start(f32[784]{0:T(1024)} %copy-done.50) | copy-start | bytes 9412
  1577.9 258.5 %copy-start.15 = (bf16[784,1024]{1,0:T(8,128)(2,1)S(1)}, bf16[784,1024]{1,0:T(8,128)(2,1)}, u32[]{:S(2)}) copy-start(bf16[784,1024]{1,0:T(8,128)(2,1)} %param.23) | copy-start | bytes 4816900
  1577.9 258.5 %copy-start.48 = (f32[784]{0:T(1024)S(1)}, f32[784]{0:T(1024)}, u32[]{:S(2)}) copy-start(f32[784]{0:T(1024)} %copy-done.47) | copy-start | bytes 9412
  1577.9 258.5 %copy-start.56 = (f32[784]{0:T(1024)S(1)}, f32[784]{0:T(1024)}, u32[]{:S(2)}) copy-start(f32[784]{0:T(1024)} %copy-done.55) | copy-start | bytes 9412
  (62 other events, 982.3 us)
Sparse Core Ops, SparseCore 0:
  15.0 120.1 all-gather.7
  137.2 23.9 all-gather.9
  323.3 112.8 reduce-scatter.4
  438.2 118.0 all-gather.17
  558.0 26.1 all-gather.15
  586.1 117.4 all-gather.11
  705.5 26.1 all-gather.13
  849.3 112.8 reduce-scatter.8
  964.6 113.3 reduce-scatter.6
  1086.3 118.0 all-gather.19
  1522.2 54.1 all-reduce.6
  1583.1 133.9 all-reduce.4
  1719.6 111.7 reduce-scatter.10
where the time goes:
time: 1860 us; the launch traced here: 1850 us
  waiting for transfers between devices  1060 us (57%)
  matrix products  514 us (28%)
  other arithmetic  171 us (9%)
  local copies, waits for them, and re-layouts  67.1 us (4%)
    psum x1, waiting for transfers between devices, local(): lax.psum((per_adapter(onehot_float, entry_down_clip), per_adapter(onehot_...  134 us
    reduce_scatter x1, waiting for transfers between devices, local(): lax.psum_scatter(branch_two.astype(jnp.bfloat16), 'tensor', scatter_dimen...  113 us
    reduce_scatter x1, waiting for transfers between devices, local(): lax.psum_scatter(branch.astype(jnp.bfloat16), 'tensor', scatter_dimension...  109 us
    all_gather x1, waiting for transfers between devices, local(): second_full = lax.all_gather(second_local, 'tensor', axis=0, tiled=True)  107 us
    reduce_scatter x1, waiting for transfers between devices, local(): lax.psum_scatter(first_grad.astype(jnp.bfloat16), 'tensor', scatter_dimen...  106 us
    all_gather x1, waiting for transfers between devices, local(): lax.all_gather(grad_out.astype(jnp.bfloat16), 'tensor', axis=0, tiled=True)  105 us
    all_gather x1, waiting for transfers between devices, local(): normed_full = lax.all_gather(normed_local, 'tensor', axis=0, tiled=True)  104 us
    all_gather x1, waiting for transfers between devices, local(): lax.all_gather(middle_grad.astype(jnp.bfloat16), 'tensor', axis=0, tiled=...  97.1 us
  transfers between devices with their start and end apart: 13, of which 13 were waited for; matrix products, arithmetic and copies ran while one was open for 7% of the time, Pallas kernels for 0%

commit v1 on v0

v1 whole, which is shorter than its diff:
```python
import functools

import jax
import jax.numpy as jnp
from jax import lax
from jax.experimental import pallas as pl
from jax.experimental.pallas import tpu as pltpu
from jax.sharding import PartitionSpec as P

HEAD_DIM = 64
PAIR = 2 * HEAD_DIM
RANK = 16
LOG2E = 1.4426950408889634
LN2 = 0.6931471805599453
F32, BF = jnp.float32, jnp.bfloat16
VMEM_LIMIT = 60 * 2**20


def dot(a, b, ca, cb):
    return lax.dot_general(a, b, (((ca,), (cb,)), ((), ())), preferred_element_type=F32)


def params(**more):
    return pltpu.CompilerParams(vmem_limit_bytes=VMEM_LIMIT, **more)


def merge_rows(block):
    return block.reshape(block.shape[0] * block.shape[1], block.shape[2])


def norm_parts(values):
    centre = jnp.mean(values, axis=-1, keepdims=True)
    shifted = values - centre
    scale = lax.rsqrt(jnp.mean(shifted * shifted, axis=-1, keepdims=True) + 1e-05)
    return shifted * scale, scale


def norm_back(hat, scale, gain, grad):
    inner = grad * gain
    mean_one = jnp.mean(inner, axis=-1, keepdims=True)
    mean_two = jnp.mean(inner * hat, axis=-1, keepdims=True)
    return scale * (inner - mean_one - hat * mean_two)


def entry_kernel(
    tok_ref, gain_ref, w_ref, down_ref, up_ref, q_ref, k_ref, v_ref, normed_ref, inner_t_ref, inner_ref
):
    @pl.when(pl.program_id(0) == 0)
    def _():
        hat, _ = norm_parts(tok_ref[...].astype(F32))
        normed = (hat * gain_ref[...]).astype(BF)
        normed_ref[...] = normed
        inner_ref[...] = dot(normed, down_ref[...], 1, 1).astype(BF)
        inner_t_ref[...] = dot(down_ref[...], normed, 1, 1).astype(BF)

    normed = normed_ref[...]
    inner = inner_ref[...]
    for which, (out, scale) in enumerate(((q_ref, HEAD_DIM**-0.5 * LOG2E), (k_ref, None), (v_ref, None))):
        part = dot(normed, merge_rows(w_ref[:, which]), 1, 0) + dot(inner, up_ref[which], 1, 0)
        if scale is not None:
            part = part * scale
        out[...] = part.astype(BF)


def entry_forward(tok, gain, w, down, up):
    rows, width = tok.shape
    n_dp, n_t, _, depth, cols = w.shape
    whole = lambda shape: pl.BlockSpec(shape, lambda i: (0,) * len(shape))
    return pl.pallas_call(
        entry_kernel,
        grid=(n_t,),
        in_specs=[
            whole((rows, width)),
            whole((1, width)),
            pl.BlockSpec((n_dp, None, 3, depth, cols), lambda i: (0, i, 0, 0, 0)),
            whole((RANK, width)),
            pl.BlockSpec((None, 3, RANK, cols), lambda i: (i, 0, 0, 0)),
        ],
        out_specs=[pl.BlockSpec((rows, cols), lambda i: (0, i))] * 3
        + [whole((rows, width)), whole((RANK, rows))],
        out_shape=[jax.ShapeDtypeStruct((rows, width), BF)] * 4 + [jax.ShapeDtypeStruct((RANK, rows), BF)],
        scratch_shapes=[pltpu.VMEM((rows, RANK), BF)],
        compiler_params=params(),
        name="entry_forward",
    )(tok, gain, w, down, up)


def head_masks(shape):
    lane = lax.broadcasted_iota(jnp.int32, shape, 1)
    return lane < HEAD_DIM, lane >= HEAD_DIM


def ones_lanes(rows, count):
    lane = lax.broadcasted_iota(jnp.int32, (rows, PAIR), 1)
    return jnp.where(lane < count, 1.0, 0.0).astype(BF)


def attend_kernel(q_ref, k_ref, v_ref, o_ref, lse_ref):
    rows = q_ref.shape[0]
    keys = k_ref[...]
    length = keys.shape[0]
    values = jnp.concatenate([v_ref[...], ones_lanes(length, 1)], axis=1)
    queries = q_ref[...]
    zero = jnp.zeros_like(queries)
    outs, sums = [], []
    for mask in head_masks(queries.shape):
        scores = dot(jnp.where(mask, queries, zero), keys, 1, 1)
        top = jnp.max(scores, axis=1, keepdims=True)
        probs = jnp.exp2(scores - top).astype(BF)
        mixed = dot(probs, values, 1, 0)
        total = mixed[:, PAIR : PAIR + 1]
        outs.append(mixed[:, :PAIR] / total)
        sums.append(top + jnp.log2(total))
    first, _ = head_masks((rows, PAIR))
    o_ref[...] = jnp.where(first, outs[0], outs[1]).astype(BF)
    lse_ref[...] = jnp.where(first, sums[0], sums[1])


def attention_forward(q, k, v):
    rows, width = q.shape
    length = k.shape[0]
    pair = lambda n: pl.BlockSpec((n, PAIR), lambda h: (0, h))
    return pl.pallas_call(
        attend_kernel,
        grid=(width // PAIR,),
        in_specs=[pair(rows), pair(length), pair(length)],
        out_specs=[pair(rows), pair(rows)],
        out_shape=[jax.ShapeDtypeStruct((rows, width), BF), jax.ShapeDtypeStruct((rows, width), F32)],
        compiler_params=params(),
        name="attention_forward",
    )(q, k, v)


def split_lanes(column):
    column = -column
    high = column.astype(BF)
    rest = column - high.astype(F32)
    mid = rest.astype(BF)
    low = (rest - mid.astype(F32)).astype(BF)
    lane = lax.broadcasted_iota(jnp.int32, (column.shape[0], PAIR), 1)
    zero = jnp.zeros((column.shape[0], PAIR), BF)
    return jnp.where(lane == 0, high, jnp.where(lane == 1, mid, jnp.where(lane == 2, low, zero)))


def attend_back_kernel(q_ref, k_ref, v_ref, o_ref, lse_ref, do_ref, dq_ref, dk_ref, dv_ref):
    rows = q_ref.shape[0]
    keys = k_ref[...]
    length = keys.shape[0]
    ones = ones_lanes(length, 3)
    keys_more = jnp.concatenate([keys, ones], axis=1)
    values_more = jnp.concatenate([v_ref[...], ones], axis=1)
    queries, grad = q_ref[...], do_ref[...]
    zero = jnp.zeros_like(queries)
    product = grad.astype(F32) * o_ref[...].astype(F32)
    d_queries, d_keys, d_values = [], 0.0, 0.0
    for head, mask in enumerate(head_masks(queries.shape)):
        query = jnp.where(mask, queries, zero)
        grad_head = jnp.where(mask, grad, zero)
        lse = lse_ref[:, head * HEAD_DIM : head * HEAD_DIM + 1]
        delta = jnp.sum(jnp.where(mask, product, 0.0), axis=1, keepdims=True)
        probs = jnp.exp2(dot(jnp.concatenate([query, split_lanes(lse)], axis=1), keys_more, 1, 1))
        slope = dot(jnp.concatenate([grad_head, split_lanes(delta)], axis=1), values_more, 1, 1)
        score_grad = (probs * slope).astype(BF)
        d_queries.append(dot(score_grad, keys, 1, 0))
        d_values = d_values + dot(grad_head, probs.astype(BF), 0, 0)
        d_keys = d_keys + dot(query, score_grad, 0, 0)
    first, _ = head_masks((rows, PAIR))
    dq_ref[...] = (jnp.where(first, d_queries[0], d_queries[1]) * HEAD_DIM**-0.5).astype(BF)
    dk_ref[...] = (d_keys * LN2).T.astype(BF)
    dv_ref[...] = d_values.T.astype(BF)


def attention_backward(q, k, v, o, lse, do):
    rows, width = q.shape
    length = k.shape[0]
    pair = lambda n: pl.BlockSpec((n, PAIR), lambda h: (0, h))
    return pl.pallas_call(
        attend_back_kernel,
        grid=(width // PAIR,),
        in_specs=[pair(rows), pair(length), pair(length), pair(rows), pair(rows), pair(rows)],
        out_specs=[pair(rows), pair(length), pair(length)],
        out_shape=[
            jax.ShapeDtypeStruct((rows, width), BF),
            jax.ShapeDtypeStruct((length, width), BF),
            jax.ShapeDtypeStruct((length, width), BF),
        ],
        compiler_params=params(),
        name="attention_backward",
    )(q, k, v, o, lse, do)


def gelu_parts(hidden):
    share = 0.5 * (1.0 + lax.erf(hidden * 0.7071067811865476))
    density = jnp.exp(-0.5 * hidden * hidden) * 0.3989422804014327
    return hidden * share, share + hidden * density


def middle_kernel(
    alive_ref, x_ref, att_ref, cot_ref, gain_ref, wo_ref, we_ref, ws_ref,
    o_down_ref, o_up_ref, e_down_ref, e_up_ref, s_down_ref, s_up_ref,
    mixed_ref, mgrad_ref, agrad_ref, od_g_ref, ou_g_ref, ed_g_ref, eu_g_ref, sd_g_ref, su_g_ref,
    middle_ref, second_ref, dy_ref, acc2_ref, acc3_ref, einner_ref, einner_t_ref, sback_ref, sback_t_ref,
    sinner_ref, eback_ref, oinner_ref,
):
    step = pl.program_id(0)
    alive = alive_ref[0]
    n_t = wo_ref.shape[1]
    cols = wo_ref.shape[3]

    @pl.when(step == 0)
    def _():
        branch, inner = 0.0, 0.0
        for t in range(n_t):
            att = att_ref[:, t * cols : (t + 1) * cols]
            branch = branch + dot(att, merge_rows(wo_ref[:, t]), 1, 1)
            inner = inner + dot(att, o_down_ref[t], 1, 1)
        inner = inner.astype(BF)
        oinner_ref[...] = inner
        middle = x_ref[...].astype(F32) + (branch + dot(inner, o_up_ref[...], 1, 0))
        middle_ref[...] = middle
        hat, _ = norm_parts(middle)
        second = (hat * gain_ref[...]).astype(BF)
        second_ref[...] = second
        dy = (cot_ref[...].astype(F32) * alive).astype(BF)
        dy_ref[...] = dy
        einner_ref[...] = dot(second, e_down_ref[...], 1, 1).astype(BF)
        einner_t_ref[...] = dot(e_down_ref[...], second, 1, 1).astype(BF)
        sback_ref[...] = dot(dy, s_up_ref[...], 1, 1).astype(BF)
        sback_t_ref[...] = dot(s_up_ref[...], dy, 1, 1).astype(BF)
        acc2_ref[...] = jnp.zeros_like(acc2_ref)
        acc3_ref[...] = jnp.zeros_like(acc3_ref)
        sinner_ref[...] = jnp.zeros_like(sinner_ref)
        eback_ref[...] = jnp.zeros_like(eback_ref)

    we, ws = merge_rows(we_ref[...]), merge_rows(ws_ref[...])
    e_up, s_down = e_up_ref[...], s_down_ref[...]
    hidden = dot(second_ref[...], we, 1, 0) + dot(einner_ref[...], e_up, 1, 0)
    value, slope = gelu_parts(hidden)
    act = value.astype(BF)
    acc2_ref[...] += dot(act, ws, 1, 1)
    sinner_ref[...] += dot(act, s_down, 1, 1)
    act_grad = dot(dy_ref[...], ws, 1, 0) + dot(sback_ref[...], s_down, 1, 0)
    hid_grad = (act_grad * slope).astype(BF)
    acc3_ref[...] += dot(hid_grad, we, 1, 1)
    eback_ref[...] += dot(hid_grad, e_up, 1, 1)
    sd_g_ref[...] = dot(sback_t_ref[...], act, 1, 0)
    eu_g_ref[...] = dot(einner_t_ref[...], hid_grad, 1, 0)

    @pl.when(step == pl.num_programs(0) - 1)
    def _():
        s_inner, e_back = sinner_ref[...].astype(BF), eback_ref[...].astype(BF)
        middle = middle_ref[...]
        mixed_ref[...] = (alive * (middle + (acc2_ref[...] + dot(s_inner, s_up_ref[...], 1, 0)))).astype(BF)
        su_g_ref[...] = dot(s_inner, dy_ref[...], 0, 0)
        ed_g_ref[...] = dot(e_back, second_ref[...], 0, 0)
        second_grad = acc3_ref[...] + dot(e_back, e_down_ref[...], 1, 0)
        hat, scale = norm_parts(middle)
        mgrad = cot_ref[...].astype(F32) * alive + norm_back(hat, scale, gain_ref[...], second_grad)
        mgrad_ref[...] = mgrad
        low = mgrad.astype(BF)
        o_back = dot(low, o_up_ref[...], 1, 1).astype(BF)
        for t in range(n_t):
            agrad_ref[:, t * cols : (t + 1) * cols] = (
                dot(low, merge_rows(wo_ref[:, t]), 1, 0) + dot(o_back, o_down_ref[t], 1, 0)
            ).astype(BF)
        od_g_ref[...] = dot(o_back, att_ref[...], 0, 0)
        ou_g_ref[...] = dot(oinner_ref[...], low, 0, 0)


def middle_both_ways(alive, x, att, cot, gain, wo, we, ws, o_down, o_up, e_down, e_up, s_down, s_up):
    rows, width = x.shape
    n_dp, n_t, depth, hid = we.shape
    sub = max(1, hid // 512)
    step_cols = hid // sub
    whole = lambda shape: pl.BlockSpec(shape, lambda i: (0,) * len(shape))
    chunk = pl.BlockSpec((n_dp, None, depth, step_cols), lambda i: (0, i // sub, 0, i % sub))
    thin = pl.BlockSpec((None, RANK, step_cols), lambda i: (i // sub, 0, i % sub))
    ff = n_t * hid
    return pl.pallas_call(
        middle_kernel,
        grid=(n_t * sub,),
        in_specs=[
            pl.BlockSpec(memory_space=pltpu.SMEM),
            whole((rows, width)), whole((rows, width)), whole((rows, width)), whole((1, width)),
            whole(wo.shape), chunk, chunk,
            whole(o_down.shape), whole((RANK, width)), whole((RANK, width)), thin, thin, whole((RANK, width)),
        ],
        out_specs=[
            whole((rows, width)), whole((rows, width)), whole((rows, width)),
            whole((RANK, width)), whole((RANK, width)), whole((RANK, width)),
            pl.BlockSpec((RANK, step_cols), lambda i: (0, i)), pl.BlockSpec((RANK, step_cols), lambda i: (0, i)),
            whole((RANK, width)),
        ],
        out_shape=[
            jax.ShapeDtypeStruct((rows, width), BF), jax.ShapeDtypeStruct((rows, width), F32),
            jax.ShapeDtypeStruct((rows, width), BF),
            jax.ShapeDtypeStruct((RANK, width), F32), jax.ShapeDtypeStruct((RANK, width), F32),
            jax.ShapeDtypeStruct((RANK, width), F32), jax.ShapeDtypeStruct((RANK, ff), F32),
            jax.ShapeDtypeStruct((RANK, ff), F32), jax.ShapeDtypeStruct((RANK, width), F32),
        ],
        scratch_shapes=[
            pltpu.VMEM((rows, width), F32), pltpu.VMEM((rows, width), BF), pltpu.VMEM((rows, width), BF),
            pltpu.VMEM((rows, width), F32), pltpu.VMEM((rows, width), F32),
            pltpu.VMEM((rows, RANK), BF), pltpu.VMEM((RANK, rows), BF),
            pltpu.VMEM((rows, RANK), BF), pltpu.VMEM((RANK, rows), BF),
            pltpu.VMEM((rows, RANK), F32), pltpu.VMEM((rows, RANK), F32), pltpu.VMEM((rows, RANK), BF),
        ],
        compiler_params=params(),
        name="middle_both_ways",
    )(alive, x, att, cot, gain, wo, we, ws, o_down, o_up, e_down, e_up, s_down, s_up)


def entry_back_kernel(
    tok_ref, gain_ref, mgrad_ref, normed_ref, inner_t_ref, dq_ref, dk_ref, dv_ref, dk2_ref, dv2_ref,
    w_ref, down_ref, up_ref, tgrad_ref, down_g_ref, up_g_ref, acc_ref, back_ref,
):
    @pl.when(pl.program_id(0) == 0)
    def _():
        acc_ref[...] = jnp.zeros_like(acc_ref)
        back_ref[...] = jnp.zeros_like(back_ref)

    acc, back = acc_ref[...], back_ref[...]
    add = lambda a, b: (a[...].astype(F32) + b[...].astype(F32)).astype(BF)
    for which, grad in enumerate((dq_ref[...], add(dk_ref, dk2_ref), add(dv_ref, dv2_ref))):
        acc = acc + dot(grad, merge_rows(w_ref[:, which]), 1, 1)
        back = back + dot(grad, up_ref[which], 1, 1)
        up_g_ref[which] = dot(inner_t_ref[...], grad, 1, 0)
    acc_ref[...] = acc
    back_ref[...] = back

    @pl.when(pl.program_id(0) == pl.num_programs(0) - 1)
    def _():
        back = back_ref[...].astype(BF)
        first_grad = acc_ref[...] + dot(back, down_ref[...], 1, 0)
        down_g_ref[...] = dot(back, normed_ref[...], 0, 0)
        hat, scale = norm_parts(tok_ref[...].astype(F32))
        tgrad_ref[...] = (mgrad_ref[...] + norm_back(hat, scale, gain_ref[...], first_grad)).astype(BF)


def entry_backward(tok, gain, mgrad, normed, inner_t, dq, dk, dv, dk2, dv2, w, down, up):
    rows, width = tok.shape
    n_dp, n_t, _, depth, cols = w.shape
    whole = lambda shape: pl.BlockSpec(shape, lambda i: (0,) * len(shape))
    return pl.pallas_call(
        entry_back_kernel,
        grid=(n_t,),
        in_specs=[
            whole((rows, width)), whole((1, width)), whole((rows, width)), whole((rows, width)),
            whole((RANK, rows)),
            *[pl.BlockSpec((rows, cols), lambda i: (0, i))] * 5,
            pl.BlockSpec((n_dp, None, 3, depth, cols), lambda i: (0, i, 0, 0, 0)),
            whole((RANK, width)),
            pl.BlockSpec((None, 3, RANK, cols), lambda i: (i, 0, 0, 0)),
        ],
        out_specs=[
            whole((rows, width)), whole((RANK, width)),
            pl.BlockSpec((None, 3, RANK, cols), lambda i: (i, 0, 0, 0)),
        ],
        out_shape=[
            jax.ShapeDtypeStruct((rows, width), BF), jax.ShapeDtypeStruct((RANK, width), F32),
            jax.ShapeDtypeStruct((n_t, 3, RANK, cols), F32),
        ],
        scratch_shapes=[pltpu.VMEM((rows, width), F32), pltpu.VMEM((rows, RANK), F32)],
        compiler_params=params(),
        name="entry_backward",
    )(tok, gain, mgrad, normed, inner_t, dq, dk, dv, dk2, dv2, w, down, up)


class Places:
    def __init__(self, n_dp, n_t, cap):
        self.n_dp, self.n_t, self.cap = n_dp, n_t, cap
        self.group = n_t // cap
        self.half = self.group // 2

    def swapped(self, dp, t):
        core, slot, j = dp % 2, t // self.group, t % self.group
        return dp - core + j // self.half, slot * self.group + core * self.half + j % self.half

    def swap_pairs(self):
        pairs = []
        for dp in range(self.n_dp):
            for t in range(self.n_t):
                to = self.swapped(dp, t)
                pairs.append((dp * self.n_t + t, to[0] * self.n_t + to[1]))
        return pairs

    def mate(self, dp, t, shift):
        core, j = dp % 2, t % self.group
        block = (core * self.half + j % self.half + shift) % self.group
        return dp - core + block // self.half, t - j % self.half + block % self.half

    def mate_pairs(self, shift):
        pairs = []
        for dp in range(self.n_dp):
            for t in range(self.n_t):
                to = self.mate(dp, t, shift)
                pairs.append((dp * self.n_t + t, to[0] * self.n_t + to[1]))
        return pairs

    def owner(self, dp, t):
        return self.swapped(dp, t)[0] * self.cap + t // self.group


BOTH = ("dp", "tensor")


def local(
    tokens, cotangent, norm_first, norm_second, entry_weight, output_weight, expand_weight, shrink_weight,
    entry_down, entry_up, output_down, output_up, expand_down, expand_up, shrink_down, shrink_up,
    adapter_choice, clip_count,
):
    n_dp, n_t, cap = lax.axis_size("dp"), lax.axis_size("tensor"), adapter_choice.shape[0]
    dp, t = lax.axis_index("dp"), lax.axis_index("tensor")
    places = Places(n_dp, n_t, cap)
    rows, width = tokens.shape
    adapters = entry_down.shape[0]
    cols, hid = output_weight.shape[1], expand_weight.shape[1]

    choices = lax.all_gather(adapter_choice, "dp", axis=0, tiled=True)
    counts = lax.all_gather(clip_count, "dp", axis=0, tiled=True)
    owner = places.owner(dp, t)
    mine = choices[owner]
    alive = (owner % cap < counts[owner // cap]).astype(F32).reshape(1)

    tok = lax.ppermute(tokens, BOTH, places.swap_pairs())
    cot = lax.ppermute(cotangent, BOTH, places.swap_pairs())
    gather = lambda w: lax.all_gather(w, BOTH, axis=0).reshape(n_dp, n_t, *w.shape)
    full_entry = gather(entry_weight.transpose(1, 0, 2))
    full_output = gather(output_weight)
    full_expand = gather(expand_weight)
    full_shrink = gather(shrink_weight)

    thin = jnp.concatenate(
        [
            entry_up.transpose(0, 2, 1, 3).reshape(adapters, 3 * RANK, cols).reshape(adapters, 3, RANK, cols)[:, 0],
            entry_up[:, :, 1],
            entry_up[:, :, 2],
            output_down.transpose(0, 2, 1),
            expand_up,
            shrink_down.transpose(0, 2, 1),
        ],
        axis=2,
    )
    owners = jnp.stack([places.owner(dp, jnp.int32(other)) for other in range(n_t)])
    sent = thin[choices[owners]]
    got = lax.all_to_all(sent, "tensor", 0, 0)
    up_entry = jnp.stack([got[:, :, i * cols : (i + 1) * cols] for i in range(3)], axis=1)
    down_output = got[:, :, 3 * cols : 4 * cols]
    up_expand = got[:, :, 4 * cols : 4 * cols + hid]
    down_shrink = got[:, :, 4 * cols + hid :]
    pick = lambda table: lax.dynamic_index_in_dim(table, mine, 0, keepdims=False)
    down_entry, up_output = pick(entry_down.transpose(0, 2, 1)), pick(output_up)
    down_expand, up_shrink = pick(expand_down.transpose(0, 2, 1)), pick(shrink_up)
    gain_first, gain_second = norm_first.reshape(1, width), norm_second.reshape(1, width)

    q, k, v, normed, inner_t = entry_forward(tok, gain_first, full_entry, down_entry, up_entry)
    shifts = range(1, places.group)
    k_all = jnp.concatenate([k] + [lax.ppermute(k, BOTH, places.mate_pairs(s)) for s in shifts], axis=0)
    v_all = jnp.concatenate([v] + [lax.ppermute(v, BOTH, places.mate_pairs(s)) for s in shifts], axis=0)
    att, lse = attention_forward(q, k_all, v_all)
    mixed, mgrad, agrad, od_g, ou_g, ed_g, eu_g, sd_g, su_g = middle_both_ways(
        alive, tok, att, cot, gain_second, full_output, full_expand, full_shrink,
        down_output, up_output, down_expand, up_expand, down_shrink, up_shrink,
    )
    dq, dk, dv = attention_backward(q, k_all, v_all, att, lse, agrad)

    def returned(grad):
        total = 0.0
        for s in shifts:
            part = lax.ppermute(grad[s * rows : (s + 1) * rows], BOTH, places.mate_pairs(places.group - s))
            total = total + part.astype(F32) if places.group > 2 else part
        return total.astype(BF)

    tgrad, edn_g, eup_g = entry_backward(
        tok, gain_first, mgrad, normed, inner_t, dq, dk[:rows], dv[:rows], returned(dk), returned(dv),
        full_entry, down_entry, up_entry,
    )
    mixed = lax.ppermute(mixed, BOTH, places.swap_pairs())
    token_grad = lax.ppermute(tgrad, BOTH, places.swap_pairs())

    all_owner = jnp.array([places.owner(d, o) for d in range(n_dp) for o in range(n_t)], jnp.int32)
    onehot = (choices[all_owner][:, None] == lax.iota(jnp.int32, adapters)[None]).astype(F32)
    whole = jnp.stack([edn_g, ou_g, ed_g, su_g])
    whole = lax.all_gather(whole.astype(BF), BOTH, axis=0)
    whole = jnp.einsum("sa,sgrd->gard", onehot.astype(BF), whole, preferred_element_type=F32)
    thin_g = jnp.concatenate(
        [
            eup_g[:, 0],
            eup_g[:, 1],
            eup_g[:, 2],
            od_g.reshape(RANK, n_t, cols).transpose(1, 0, 2),
            eu_g.reshape(RANK, n_t, hid).transpose(1, 0, 2),
            sd_g.reshape(RANK, n_t, hid).transpose(1, 0, 2),
        ],
        axis=2,
    )
    thin_g = lax.all_to_all(thin_g.astype(BF), "tensor", 0, 0)
    here = lax.dynamic_slice_in_dim(onehot, dp * n_t, n_t, 0).astype(BF)
    thin_g = jnp.einsum("sa,src->arc", here, thin_g, preferred_element_type=F32)
    thin_g = lax.psum(thin_g.astype(BF), "dp").astype(F32)
    entry_up_grad = jnp.stack([thin_g[:, :, i * cols : (i + 1) * cols] for i in range(3)], axis=2)
    return (
        mixed,
        token_grad,
        whole[0].transpose(0, 2, 1),
        entry_up_grad,
        thin_g[:, :, 3 * cols : 4 * cols].transpose(0, 2, 1),
        whole[1],
        whole[2].transpose(0, 2, 1),
        thin_g[:, :, 4 * cols : 4 * cols + hid],
        thin_g[:, :, 4 * cols + hid :].transpose(0, 2, 1),
        whole[3],
    )


def solution(mesh):
    in_specs = (
        P(BOTH, None), P(BOTH, None), P(), P(),
        P("dp", None, "tensor"), P("dp", "tensor"), P("dp", "tensor"), P("dp", "tensor"),
        P(), P(None, None, None, "tensor"), P(None, "tensor", None), P(),
        P(), P(None, None, "tensor"), P(None, "tensor", None), P(), P("dp"), P("dp"),
    )
    out_specs = (
        P(BOTH, None), P(BOTH, None), P(), P(None, None, None, "tensor"), P(None, "tensor", None), P(),
        P(), P(None, None, "tensor"), P(None, "tensor", None), P(),
    )
    return jax.shard_map(local, mesh=mesh, in_specs=in_specs, out_specs=out_specs, check_vma=False)
```

time: 1860 us -> 609 us (0.33)
  waiting for transfers between devices: 1060 us -> 309 us
  matrix products: 514 us -> 5.86 us
  Pallas kernels: 0 us -> 179 us
  other arithmetic: 171 us -> 5.69 us
  starting transfers between devices: 0.53 us -> 28.6 us
  local copies, waits for them, and re-layouts: 67.1 us -> 42.6 us
    dot_general x62 -> x2, matrix products: 514 us -> 5.86 us  [the longest x1 4.54 us: local(): jnp.einsum('sa,sgrd->gard', onehot.astype(BF), whole, preferred_element_t...]
    reduce_scatter x4 -> x0, waiting for transfers between devices: 410 us -> none  [the longest x1 113 us: local(): lax.psum_scatter(branch_two.astype(jnp.bfloat16), 'tensor', scatter_dimen...]
    all_gather x7 -> x5, waiting for transfers between devices: 479 us -> 224 us  [the longest x4 165 us: local(): lax.all_gather(w, BOTH, axis=0).reshape(n_dp, n_t, *w.shape)]
    pallas_call x0 -> x5, Pallas kernels: none -> 179 us  [the longest x1 55.9 us: attention_backward(): pl.pallas_call(attend_back_kernel, grid=(width // PAIR,), in_specs=[pair(...]
    psum x2 -> x1, waiting for transfers between devices: 173 us -> 48.9 us  [local(): thin_g = lax.psum(thin_g.astype(BF), 'dp').astype(F32)]
    convert_element_type x9 -> x2, other arithmetic: 110 us -> 1.28 us  [the longest x1 1.28 us: local(): thin_g = lax.psum(thin_g.astype(BF), 'dp').astype(F32)]
    reduce_sum x10 -> x0, other arithmetic: 53.9 us -> none  [the longest x2 33.7 us: attend(): row_total = jnp.sum(exponent, axis=-1, keepdims=True)]
    all_to_all x0 -> x2, waiting for transfers between devices: none -> 32.3 us  [the longest x1 20.1 us: local(): got = lax.all_to_all(sent, 'tensor', 0, 0)]
  transfers between devices with their start and end apart: 13 -> 16, of which waited for: 13 -> 8; matrix products, arithmetic and copies ran while one was open for 7% -> 5% of each run, Pallas kernels for 0% -> 9%
where the time goes in v1:
time: 609 us; the launch traced here: 600 us
  waiting for transfers between devices  309 us (51%)
  Pallas kernels  179 us (29%)
  local copies, waits for them, and re-layouts  42.6 us (7%)
  starting transfers between devices  28.6 us (5%)
  between operations  18.9 us (3%)
  blocking collectives  10.5 us (2%)
    all_gather x4, waiting for transfers between devices, local(): lax.all_gather(w, BOTH, axis=0).reshape(n_dp, n_t, *w.shape)  165 us
    all_gather x1, waiting for transfers between devices, local(): whole = lax.all_gather(whole.astype(BF), BOTH, axis=0)  59.6 us
    pallas_call x1, Pallas kernels, attention_backward(): pl.pallas_call(attend_back_kernel, grid=(width // PAIR,), in_specs=[pair(...  55.9 us
    pallas_call x1, Pallas kernels, middle_both_ways(): pl.pallas_call(middle_kernel, grid=(n_t * sub,), in_specs=[pl.BlockSpec(m...  55.6 us
    psum x1, waiting for transfers between devices, local(): thin_g = lax.psum(thin_g.astype(BF), 'dp').astype(F32)  48.9 us
    pallas_call x1, Pallas kernels, attention_forward(): pl.pallas_call(attend_kernel, grid=(width // PAIR,), in_specs=[pair(rows)...  39.6 us
    unnamed x63, local copies, waits for them, and re-layouts  22.5 us
    all_to_all x1, waiting for transfers between devices, local(): got = lax.all_to_all(sent, 'tensor', 0, 0)  20.1 us
  transfers between devices with their start and end apart: 16, of which 8 were waited for; matrix products, arithmetic and copies ran while one was open for 5% of the time, Pallas kernels for 9%

profile of v1, /device:TPU:0, one launch (start us, length us, event | category | flops | bytes accessed | tf_op | source)
XLA Modules:
  0.0 599.7 jit_solution(41242860609838251)
XLA Ops:
  14.2 2.1 collective-permute-start
  16.2 10.5 %all-reduce.2 = (s32[8]{0:T(128)S(1)}, s32[16]{0:T(128)S(1)}) all-reduce(s32[8]{0:T(128)S(1)} %dynamic-update-slice, s32[16]{0:T(128)S(1)} %dynamic-update-slice.1), channel_id=1, replica_groups=mesh['dp'=8,'tensor'=4] {'dp'}, use_global_device_ids=true, to_apply=%add | all-reduce | flops 24 | bytes 192
  29.9 3.9 all-to-all-start
  36.9 20.1 %all-to-all-done = bf16[4,16,3072]{2,1,0:T(8,128)(2,1)S(1)} async-done(((bf16[4,16,3072]{2,1,0:T(8,128)(2,1)}), bf16[4,16,3072]{2,1,0:T(8,128)(2,1)S(1)}, u32[]{:S(2)}, u32[]{:S(2)}) %all-to-all-start) | async-done | bytes 393248 | tf_op jit(solution)/shard_map/all_to_all | solution.py:446
  58.3 27.0 %all-gather.12.cloned.1.call-done = bf16[96,128,256]{2,1,0:T(8,128)(2,1)} async-done(((bf16[3,128,256]{2,1,0:T(8,128)(2,1)}), bf16[96,128,256]{2,1,0:T(8,128)(2,1)}) %all-gather.12.cloned.1.call-update) | async-done | bytes 6291472 | tf_op jit(solution)/shard_map/all_gather | solution.py:427
  85.2 11.7 %entry_forward.1 = (bf16[784,1024]{1,0:T(8,128)(2,1)}, bf16[784,1024]{1,0:T(8,128)(2,1)}, bf16[784,1024]{1,0:T(8,128)(2,1)}, bf16[784,1024]{1,0:T(8,128)(2,1)}, bf16[16,784]{1,0:T(8,128)(2,1)}) custom-call(bf16[784,1024]{1,0:T(8,128)(2,1)} %copy-done.4, f32[1,1024]{1,0:T(1,128)} %bitcast.151, bf16[8,4,3,128,256]{4,3,2,1,0:T(8,128)(2,1)} %bitcast.141, ...), custom_call_target="tpu_custom_call" | custom-call | tf_op jit(solution)/shard_map/entry_forward/pallas_call | solution.py:69
  97.4 13.8 %collective-permute-start.3 = (bf16[784,1024]{1,0:T(8,128)(2,1)}, bf16[784,1024]{1,0:T(8,128)(2,1)}, u32[]{:S(2)}, u32[]{:S(2)}) collective-permute-start(bf16[784,1024]{1,0:T(8,128)(2,1)} %param.20), channel_id=1, source_target_pairs={{0,0},{1,4},{2,2},{3,6},{4,1},{5,5},{6,3},{7,7},{8,8},{9,12},{10,1... | collective-permute-start | bytes 4816904 | tf_op jit(solution)/shard_map/ppermute | solution.py:426
  116.0 2.2 constant_dynamic-update-slice_fusion.2
  119.8 2.7 constant_dynamic-update-slice_fusion.1.k_ref
  124.2 39.6 %attention_forward.1 = (bf16[784,1024]{1,0:T(8,128)(2,1)}, f32[784,1024]{1,0:T(8,128)}) custom-call(bf16[784,1024]{1,0:T(8,128)(2,1)} %get-tuple-element.32.q_ref, bf16[1568,1024]{1,0:T(8,128)(2,1)} %copy-done.2, bf16[1568,1024]{1,0:T(8,128)(2,1)} %copy-done.3), custom_call_target="tpu_custom_call" | custom-call | tf_op jit(solution)/shard_map/attention_forward/pallas_call | solution.py:123
  163.8 58.8 %all-gather.16.cloned.1.call-done = bf16[4096,1024]{1,0:T(8,128)(2,1)} async-done(((bf16[128,1024]{1,0:T(8,128)(2,1)}), bf16[4096,1024]{1,0:T(8,128)(2,1)}) %all-gather.16.cloned.1.call-update) | async-done | bytes 8388624 | tf_op jit(solution)/shard_map/all_gather | solution.py:427
  222.6 78.8 %all-gather.18.cloned.1.call-done = bf16[4096,1024]{1,0:T(8,128)(2,1)} async-done(((bf16[128,1024]{1,0:T(8,128)(2,1)}), bf16[4096,1024]{1,0:T(8,128)(2,1)}) %all-gather.18.cloned.1.call-update) | async-done | bytes 8388624 | tf_op jit(solution)/shard_map/all_gather | solution.py:427
  301.4 55.6 %middle_both_ways.1 = (bf16[784,1024]{1,0:T(8,128)(2,1)}, f32[784,1024]{1,0:T(8,128)}, bf16[784,1024]{1,0:T(8,128)(2,1)}, f32[16,1024]{1,0:T(8,128)}, f32[16,102...) custom-call(f32[1]{0:T(128)} %bitcast.2.alive_ref, ...), custom_call_target="tpu_custom_call" | custom-call | tf_op jit(solution)/shard_map/middle_both_ways/pallas_call | solution.py:279
  357.0 55.9 %attention_backward.1 = (bf16[784,1024]{1,0:T(8,128)(2,1)}, bf16[1568,1024]{1,0:T(8,128)(2,1)}, bf16[1568,1024]{1,0:T(8,128)(2,1)}) custom-call(bf16[784,1024]{1,0:T(8,128)(2,1)} %get-tuple-element.32.q_ref, bf16[1568,1024]{1,0:T(8,128)(2,1)} %copy-done.2, bf16[1568,1024]{1,0:T(8,128)(2,1)} %copy-done.3, bf16[784,1024]{1,0:T(8,128)(2,1)} %get-tuple-element.35.att_ref.o_ref, ...), custom_call_target="tpu_custom_call" | custom-call | tf_op jit(solution)/shard_map/attention_backward/pallas_call | solution.py:177
  412.9 4.1 fusion.25
  417.3 2.0 fusion.24
  424.2 16.1 %entry_backward.1 = (bf16[784,1024]{1,0:T(8,128)(2,1)}, f32[16,1024]{1,0:T(8,128)}, f32[4,3,16,256]{3,2,1,0:T(8,128)}) custom-call(bf16[784,1024]{1,0:T(8,128)(2,1)} %copy-done.4, f32[1,1024]{1,0:T(1,128)} %bitcast.152, f32[784,1024]{1,0:T(8,128)} %get-tuple-element.37.mgrad_ref, bf16[784,1024]{1,0:T(8,128)(2,1)} %get-tuple-element.38.normed_ref, ...), custom_call_target="tpu_custom_call" | custom-call | tf_op jit(solution)/shard_map/entry_backward/pallas_call | solution.py:344
  445.1 3.5 all-to-all-start.1
  448.6 12.2 %all-to-all-done.1 = bf16[4,16,3072]{2,1,0:T(8,128)(2,1)S(1)} async-done(((bf16[4,16,3072]{2,1,0:T(8,128)(2,1)}), bf16[4,16,3072]{2,1,0:T(8,128)(2,1)S(1)}, u32[]{:S(2)}, u32[]{:S(2)}) %all-to-all-start.1) | async-done | bytes 393248 | tf_op jit(solution)/shard_map/all_to_all | solution.py:497
  463.0 2.1 collective-permute-start.4
  465.1 2.1 collective-permute-start.7
  467.2 48.9 %all-reduce.5.cloned.1.call-done = bf16[8,16,3072]{2,0,1:T(8,128)(2,1)} async-done(((bf16[8,16,3072]{2,0,1:T(8,128)(2,1)}), bf16[8,16,3072]{2,0,1:T(8,128)(2,1)}) %all-reduce.5.cloned.1.call-update) | async-done | bytes 786448 | tf_op jit(solution)/shard_map/psum | solution.py:500
  521.3 59.6 %all-gather.10.cloned.1.call-done = bf16[32,4,16,1024]{3,2,1,0:T(8,128)(2,1)} async-done(((bf16[1,4,16,1024]{3,2,1,0:T(8,128)(2,1)}), bf16[32,4,16,1024]{3,2,1,0:T(8,128)(2,1)}) %all-gather.10.cloned.1.call-update) | async-done | bytes 4194320 | tf_op jit(solution)/shard_map/all_gather | solution.py:484
  580.9 4.5 fusion.2
  (123 shorter events, 43.1 us)
Async XLA Ops:
  7.2 29.1 %copy-start = (bf16[8,1024,16]{1,2,0:T(8,128)(2,1)S(1)}, bf16[8,1024,16]{1,2,0:T(8,128)(2,1)}, u32[]{:S(2)}) copy-start(bf16[8,1024,16]{1,2,0:T(8,128)(2,1)} %param.27) | copy-start | bytes 786436
  7.2 21.3 %copy-start.16 = (bf16[8,256,16]{1,2,0:T(8,128)(2,1)S(1)}, bf16[8,256,16]{1,2,0:T(8,128)(2,1)}, u32[]{:S(2)}) copy-start(bf16[8,256,16]{1,2,0:T(8,128)(2,1)} %param.29) | copy-start | bytes 196612
  7.2 21.3 %copy-start.9 = (bf16[8,16,1024]{2,1,0:T(8,128)(2,1)S(1)}, bf16[8,16,1024]{2,1,0:T(8,128)(2,1)}, u32[]{:S(2)}) copy-start(bf16[8,16,1024]{2,1,0:T(8,128)(2,1)} %param.32) | copy-start | bytes 786436
  7.2 21.3 %copy-start.10 = (bf16[8,1024,16]{1,2,0:T(8,128)(2,1)S(1)}, bf16[8,1024,16]{1,2,0:T(8,128)(2,1)}, u32[]{:S(2)}) copy-start(bf16[8,1024,16]{1,2,0:T(8,128)(2,1)} %param.33) | copy-start | bytes 786436
  7.2 78.0 %all-gather.12.cloned.1.call-start = ((), (), s32[]{:S(2)}) async-start(), calls=%async_computation.4 | async-start | bytes 6488064 | tf_op jit(solution)/shard_map/all_gather | solution.py:427
  8.0 155.8 %all-gather.14.cloned.1.call-start = ((), (), s32[]{:S(2)}) async-start(), calls=%async_computation.5 | async-start | bytes 2162688 | tf_op jit(solution)/shard_map/all_gather | solution.py:427
  8.7 213.9 %all-gather.16.cloned.1.call-start = ((), (), s32[]{:S(2)}) async-start(), calls=%async_computation.6 | async-start | bytes 8650752 | tf_op jit(solution)/shard_map/all_gather | solution.py:427
  9.4 291.9 %all-gather.18.cloned.1.call-start = ((), (), s32[]{:S(2)}) async-start(), calls=%async_computation.7 | async-start | bytes 8650752 | tf_op jit(solution)/shard_map/all_gather | solution.py:427
  14.2 44.1 %collective-permute-start = (bf16[784,1024]{1,0:T(8,128)(2,1)}, bf16[784,1024]{1,0:T(8,128)(2,1)S(1)}, u32[]{:S(2)}, u32[]{:S(2)}) collective-permute-start(bf16[784,1024]{1,0:T(8,128)(2,1)} %param.19), channel_id=1, source_target_pairs={{0,0},{1,4},{2,2},{3,6},{4,1},{5,5},{6,3},{7,7},{8,8},{9,12},{10,1... | collective-permute-start | bytes 4816904 | tf_op jit(solution)/shard_map/ppermute | solution.py:425
  29.9 27.1 %all-to-all-start = ((bf16[4,16,3072]{2,1,0:T(8,128)(2,1)}), bf16[4,16,3072]{2,1,0:T(8,128)(2,1)S(1)}, u32[]{:S(2)}, u32[]{:S(2)}) async-start(bf16[4,16,3072]{2,1,0:T(8,128)(2,1)} %gather_fusion.1), calls=%async_computation | async-start | bytes 786432 | tf_op jit(solution)/shard_map/all_to_all | solution.py:446
  58.3 27.0 %copy-start.4 = (bf16[784,1024]{1,0:T(8,128)(2,1)}, bf16[784,1024]{1,0:T(8,128)(2,1)S(1)}, u32[]{:S(2)}) copy-start(bf16[784,1024]{1,0:T(8,128)(2,1)S(1)} %collective-permute-done.tok_ref.x_ref) | copy-start | bytes 4816900
  96.9 21.3 %collective-permute-start.2 = (bf16[784,1024]{1,0:T(8,128)(2,1)}, bf16[784,1024]{1,0:T(8,128)(2,1)}, u32[]{:S(2)}, u32[]{:S(2)}) collective-permute-start(bf16[784,1024]{1,0:T(8,128)(2,1)} %get-tuple-element.34), channel_id=1, source_target_pairs={{0,4},{1,5},{2,6},{3,7},{4,0},{5,1},{6,2},{7,3},{8,12},{9,13},{10,... | collective-permute-start | bytes 4816904 | tf_op jit(solution)/shard_map/ppermute | solution.py:459
  97.2 22.6 %collective-permute-start.1 = (bf16[784,1024]{1,0:T(8,128)(2,1)}, bf16[784,1024]{1,0:T(8,128)(2,1)}, u32[]{:S(2)}, u32[]{:S(2)}) collective-permute-start(bf16[784,1024]{1,0:T(8,128)(2,1)} %get-tuple-element.33), channel_id=1, source_target_pairs={{0,4},{1,5},{2,6},{3,7},{4,0},{5,1},{6,2},{7,3},{8,12},{9,13},{10,... | collective-permute-start | bytes 4816904 | tf_op jit(solution)/shard_map/ppermute | solution.py:458
  97.4 66.3 %collective-permute-start.3 = (bf16[784,1024]{1,0:T(8,128)(2,1)}, bf16[784,1024]{1,0:T(8,128)(2,1)}, u32[]{:S(2)}, u32[]{:S(2)}) collective-permute-start(bf16[784,1024]{1,0:T(8,128)(2,1)} %param.20), channel_id=1, source_target_pairs={{0,0},{1,4},{2,2},{3,6},{4,1},{5,5},{6,3},{7,7},{8,8},{9,12},{10,1... | collective-permute-start | bytes 4816904 | tf_op jit(solution)/shard_map/ppermute | solution.py:426
  417.0 5.2 collective-permute-start.5
  419.3 3.7 collective-permute-start.6
  440.3 8.4 %copy-start.12 = (f32[16,1024]{1,0:T(8,128)S(1)}, f32[16,1024]{1,0:T(8,128)}, u32[]{:S(2)}) copy-start(f32[16,1024]{1,0:T(8,128)} %get-tuple-element.48) | copy-start | bytes 196612
  444.4 17.9 %copy-start.11 = (f32[16,1024]{1,0:T(8,128)S(1)}, f32[16,1024]{1,0:T(8,128)}, u32[]{:S(2)}) copy-start(f32[16,1024]{1,0:T(8,128)} %get-tuple-element.47) | copy-start | bytes 196612
  444.4 17.9 %copy-start.14 = (f32[16,1024]{1,0:T(8,128)S(1)}, f32[16,1024]{1,0:T(8,128)}, u32[]{:S(2)}) copy-start(f32[16,1024]{1,0:T(8,128)} %get-tuple-element.46) | copy-start | bytes 196612
  445.1 15.8 %all-to-all-start.1 = ((bf16[4,16,3072]{2,1,0:T(8,128)(2,1)}), bf16[4,16,3072]{2,1,0:T(8,128)(2,1)S(1)}, u32[]{:S(2)}, u32[]{:S(2)}) async-start(bf16[4,16,3072]{2,1,0:T(8,128)(2,1)} %fusion.6), calls=%async_computation.1 | async-start | bytes 786432 | tf_op jit(solution)/shard_map/all_to_all | solution.py:497
  448.5 67.6 %all-reduce.5.cloned.1.call-start = ((), (), s32[]{:S(2)}) async-start(), calls=%async_computation.3 | async-start | bytes 1572864 | tf_op jit(solution)/shard_map/psum | solution.py:500
  462.2 118.7 %all-gather.10.cloned.1.call-start = ((), (), s32[]{:S(2)}) async-start(), calls=%async_computation.2 | async-start | bytes 4325376 | tf_op jit(solution)/shard_map/all_gather | solution.py:484
  463.0 4.2 collective-permute-start.4
  465.1 56.2 %collective-permute-start.7 = (bf16[784,1024]{1,0:T(8,128)(2,1)}, bf16[784,1024]{1,0:T(8,128)(2,1)S(1)}, u32[]{:S(2)}, u32[]{:S(2)}) collective-permute-start(bf16[784,1024]{1,0:T(8,128)(2,1)} %get-tuple-element.45), channel_id=1, source_target_pairs={{0,0},{1,4},{2,2},{3,6},{4,1},{5,5},{6,3},{7,7},{8,8},{9,12},{10,1... | collective-permute-start | bytes 4816904 | tf_op jit(solution)/shard_map/ppermute | solution.py:479
  (10 other events, 29.7 us)
Sparse Core Ops, SparseCore 0:
  10.9 74.2 all-gather.11
  88.2 55.1 all-gather.13
  146.3 76.2 all-gather.15
  225.4 75.9 all-gather.17
  462.3 53.7 all-reduce.4
  519.5 61.3 all-gather.9

commit v2 on v1

v2 whole, which is shorter than its diff:
```python
import functools

import jax
import jax.numpy as jnp
from jax import lax
from jax.experimental import pallas as pl
from jax.experimental.pallas import tpu as pltpu
from jax.sharding import PartitionSpec as P

HEAD_DIM = 64
PAIR = 2 * HEAD_DIM
RANK = 16
LOG2E = 1.4426950408889634
LN2 = 0.6931471805599453
F32, BF = jnp.float32, jnp.bfloat16
VMEM_LIMIT = 60 * 2**20


def dot(a, b, ca, cb):
    return lax.dot_general(a, b, (((ca,), (cb,)), ((), ())), preferred_element_type=F32)


def params(**more):
    return pltpu.CompilerParams(vmem_limit_bytes=VMEM_LIMIT, **more)


def merge_rows(block):
    return block.reshape(block.shape[0] * block.shape[1], block.shape[2])


def norm_parts(values):
    centre = jnp.mean(values, axis=-1, keepdims=True)
    shifted = values - centre
    scale = lax.rsqrt(jnp.mean(shifted * shifted, axis=-1, keepdims=True) + 1e-05)
    return shifted * scale, scale


def norm_back(hat, scale, gain, grad):
    inner = grad * gain
    mean_one = jnp.mean(inner, axis=-1, keepdims=True)
    mean_two = jnp.mean(inner * hat, axis=-1, keepdims=True)
    return scale * (inner - mean_one - hat * mean_two)


MESH = pl.DeviceIdType.MESH
BOTH = ("dp", "tensor")
ANY = pl.BlockSpec(memory_space=pl.ANY)
IN_VMEM = pl.BlockSpec(memory_space=pltpu.VMEM)
IN_SMEM = pl.BlockSpec(memory_space=pltpu.SMEM)
DMA = pltpu.SemaphoreType.DMA


class Place:
    def __init__(self, n_dp, n_t, cap):
        self.n_dp, self.n_t, self.cap = n_dp, n_t, cap
        self.dp, self.t = lax.axis_index("dp"), lax.axis_index("tensor")
        self.core, self.q = self.dp % 2, self.dp // 2
        self.n_q, self.n_hi = n_dp // 2, n_dp // 4
        self.lo, self.hi = self.q % 2, self.q // 2
        self.group = n_t // cap
        self.half = self.group // 2
        self.slot, block = self.t // self.group, self.t % self.group
        self.high, self.low = block // self.half, block % self.half
        self.stays = self.core == self.high
        self.sibling = (self.dp + 1 - 2 * self.core, self.t)
        self.partner = (self.dp - self.core + self.high, self.t - block + self.core * self.half + self.low)

    def along(self, d):
        return (self.t + d) % self.n_t

    def column(self, d, cols):
        return pl.ds(pl.multiple_of(((self.t + self.n_t - d) % self.n_t) * cols, cols), cols)

    def lo_q(self):
        return self.q + 1 - 2 * self.lo

    def hi_q(self, m, lo=None):
        return ((self.hi + m) % self.n_hi) * 2 + (self.lo if lo is None else lo)

    def device(self, q, core=None, t=None):
        return (q * 2 + (self.core if core is None else core), self.t if t is None else t)

    def mate(self, shift):
        block = (self.core * self.half + self.low + shift) % self.group
        return (self.dp - self.core + block // self.half, self.t - self.low + block % self.half)

    def gather_peers(self):
        return (
            [(self.dp, self.along(d)) for d in range(1, self.n_t)]
            + [self.sibling, self.device(self.lo_q())]
            + [self.device(self.hi_q(m)) for m in range(1, self.n_hi)]
        )

    def other_core_peers(self):
        return [(self.sibling[0], self.along(d)) for d in range(1, self.n_t)]


def greet(peers):
    barrier = pltpu.get_barrier_semaphore()
    for peer in peers:
        pl.semaphore_signal(barrier, inc=1, device_id=peer, device_id_type=MESH)
    pl.semaphore_wait(barrier, len(peers))


def remote(src, dst, send, recv, device):
    return pltpu.make_async_remote_copy(
        src_ref=src, dst_ref=dst, send_sem=send, recv_sem=recv, device_id=device, device_id_type=MESH
    )


class Gather:
    @staticmethod
    def keys(n_hi, ds):
        found = []
        for d in ds:
            found += [("z", d)] if d else []
            found += [("x", d), ("s", d)]
            for m in range(1, n_hi):
                found += [("y", m, d), ("dy", m, d), ("dx", m, d)]
        return found

    @staticmethod
    def scratch(n_dp, ds):
        count = len(Gather.keys(n_dp // 4, ds))
        return [DMA((count,)), DMA((count,)), DMA((1,))]

    def __init__(self, place, source, full, ds, sems, spread=None, by_rows=True):
        self.place, self.source, self.full, self.ds = place, source, full, list(ds)
        self.send, self.recv, self.own = sems
        self.index = {k: i for i, k in enumerate(Gather.keys(place.n_hi, self.ds))}
        self.spread, self.by_rows = spread, by_rows
        self.ms = range(1, place.n_hi)

    def block(self, d, q, half=None):
        ref = self.full.at[self.ds.index(d), q, self.place.core]
        if half is None:
            return ref
        rows, cols = self.full.shape[-2:]
        if self.by_rows:
            return ref.at[pl.ds(half * (rows // 2), rows // 2)]
        first = cols // 2 // 128 * 128
        return ref.at[:, pl.ds(half * first, cols - first if half else first)]

    def copy(self, key):
        p, kind, d = self.place, key[0], key[-1]
        i = self.index[key]
        if kind == "z":
            src = self.source if self.spread is None else self.spread(d)
            dst, device = self.block(d, p.q), (p.dp, p.along(d))
        elif kind == "s":
            src = dst = self.full.at[self.ds.index(d), :, p.core]
            device = p.sibling
        elif kind in "xy":
            src = self.source if d == 0 else self.block(d, p.q)
            dst = self.block(d, p.q)
            device = p.device(p.lo_q() if kind == "x" else p.hi_q(key[1]))
        elif kind == "dy":
            src = dst = self.block(d, p.lo_q(), 0)
            device = p.device(p.hi_q(key[1]))
        else:
            src = dst = self.block(d, p.hi_q(p.n_hi - key[1]), 1)
            device = p.device(p.lo_q())
        return remote(src, dst, self.send.at[i], self.recv.at[i], device)

    def own_copy(self):
        return pltpu.make_async_copy(self.source, self.block(0, self.place.q), self.own.at[0])

    def start(self):
        for d in self.ds:
            if d:
                self.copy(("z", d)).start()
        if 0 in self.ds:
            self.relay(0)
            self.own_copy().start()

    def relay(self, d):
        if d:
            self.copy(("z", d)).wait_recv()
        self.copy(("x", d)).start()
        for m in self.ms:
            self.copy(("y", m, d)).start()

    def diag(self, d):
        self.copy(("x", d)).wait_recv()
        for m in self.ms:
            self.copy(("dy", m, d)).start()
        for m in self.ms:
            self.copy(("y", m, d)).wait_recv()
            self.copy(("dx", m, d)).start()

    def share(self, d):
        if d == 0:
            self.own_copy().wait()
        for m in self.ms:
            self.copy(("dy", m, d)).wait_recv()
            self.copy(("dx", m, d)).wait_recv()
        self.copy(("s", d)).start()

    def done(self, d):
        self.copy(("s", d)).wait_recv()

    def finish(self):
        for key in self.index:
            self.copy(key).wait_send()


def move(place, source, target, sems, kind, rows=None):
    if rows is not None:
        source, target = source.at[rows], target.at[rows]

    @pl.when(place.stays)
    def _():
        here = pltpu.make_async_copy(source, target, sems[2])
        here.start() if kind == "start" else here.wait()

    @pl.when(jnp.logical_not(place.stays))
    def _():
        there = remote(source, target, sems[0], sems[1], place.partner)
        there.start() if kind == "start" else there.wait()


def first_kernel(
    n_dp, n_t, cap,
    choice_ref, count_ref, tokens_ref, w_ref, gain_ref, ed_tab, ou_tab, xd_tab, su_tab, eu_tab, od_tab, xu_tab, sd_tab,
    q_ref, k_ref, v_ref, normed_ref, inner_t_ref, thin_ref, rep_ref, tok_out, k_far, v_far, w_full,
    tok, thin, thin_send, rep, stage, inner,
    g_send, g_recv, g_own, tok_sems, thin_sends, thin_recvs, rep_sems, stage_sems, kv_sends, kv_recvs, out_sem,
):
    p = Place(n_dp, n_t, cap)
    cols, hid = od_tab.shape[-1], xu_tab.shape[-1]
    greet(p.gather_peers() + p.other_core_peers())
    gather = Gather(p, w_ref, w_full, range(n_t), (g_send, g_recv, g_own))
    gather.start()
    swap_sems = [tok_sems.at[i] for i in range(3)]
    move(p, tokens_ref, tok, swap_sems, "start")

    for s in range(cap):
        a = choice_ref[s]
        for i in range(3):
            thin_send[s, :, i * cols : (i + 1) * cols] = eu_tab[a, i]
        thin_send[s, :, 3 * cols : 4 * cols] = od_tab[a]
        thin_send[s, :, 4 * cols : 4 * cols + hid] = xu_tab[a]
        thin_send[s, :, 4 * cols + hid :] = sd_tab[a]
    for s in range(cap):
        for low in range(p.half):
            to = s * p.group + p.core * p.half + low
            d = (to + n_t - p.t) % n_t
            for core in range(2):
                i = (s * p.half + low) * 2 + core
                mine = jnp.logical_and(core == p.core, to == p.t)

                @pl.when(jnp.logical_not(mine))
                def _():
                    remote(
                        thin_send.at[s], thin.at[d], thin_sends.at[i], thin_recvs.at[d], (p.dp - p.core + core, to)
                    ).start()

    @pl.when(p.stays)
    def _():
        a = choice_ref[p.slot]
        for i, table in enumerate((ed_tab, ou_tab, xd_tab, su_tab)):
            rep[i * RANK : (i + 1) * RANK] = table[a]
        row = lax.broadcasted_iota(jnp.int32, (RANK, rep.shape[1]), 0)
        alive = jnp.where(p.slot < count_ref[0], 1.0, 0.0)
        rep[4 * RANK :] = jnp.where(row < RANK // 2, alive, a.astype(F32)).astype(BF)
        remote(rep, rep, rep_sems.at[0], rep_sems.at[1], p.sibling).start()
        thin[0] = thin_send[p.slot]

    gather.diag(0)
    gather.relay(1)
    gather.share(0)
    for d in range(1, n_t - 1):
        gather.diag(d)
        gather.relay(d + 1)
        gather.share(d)

    @pl.when(jnp.logical_not(p.stays))
    def _():
        remote(rep, rep, rep_sems.at[0], rep_sems.at[1], p.sibling).wait_recv()
        remote(thin_send.at[0], thin.at[0], thin_sends.at[0], thin_recvs.at[0], p.sibling).wait_recv()

    for d in range(1, n_t):
        remote(thin_send.at[0], thin.at[d], thin_sends.at[0], thin_recvs.at[d], p.sibling).wait_recv()
    rep_ref[...] = rep[...]
    thin_ref[...] = thin[...]

    move(p, tokens_ref, tok, swap_sems, "wait")
    keep = pltpu.make_async_copy(tok, tok_out, out_sem)
    keep.start()
    hat, _ = norm_parts(tok[...].astype(F32))
    normed = (hat * gain_ref[...]).astype(BF)
    normed_ref[...] = normed
    down = rep[:RANK]
    inner[...] = dot(normed, down, 1, 1).astype(BF)
    inner_t_ref[...] = dot(down, normed, 1, 1).astype(BF)

    def load(d):
        return pltpu.make_async_copy(w_full.at[d], stage.at[d % 2], stage_sems.at[d % 2])

    depth = stage.shape[-2] // 3
    gather.done(0)
    load(0).start()
    sent = []
    for d in range(n_t):
        if d == n_t - 2:
            gather.diag(n_t - 1)
        load(d).wait()
        if d + 1 < n_t:
            if d + 1 == n_t - 1:
                gather.share(n_t - 1)
            gather.done(d + 1)
            load(d + 1).start()
        at = p.column(d, cols)
        normed = normed_ref[...]
        for which, out in ((1, k_ref), (2, v_ref), (0, q_ref)):
            weights = stage[d % 2, :, :, which * depth : (which + 1) * depth].reshape(n_dp * depth, cols)
            part = dot(normed, weights, 1, 0)
            part = part + dot(inner[...], thin[d, :, which * cols : (which + 1) * cols], 1, 0)
            if which == 0:
                part = part * (HEAD_DIM**-0.5 * LOG2E)
            out[:, at] = part.astype(BF)
            if which:
                far = (k_far, v_far)[which - 1]
                for m in range(1, p.group):
                    i = (d * 2 + which - 1) * (p.group - 1) + m - 1
                    copy = remote(
                        out.at[:, at], far.at[m - 1, :, at], kv_sends.at[i], kv_recvs.at[i], p.mate(m)
                    )
                    copy.start()
                    sent.append((i, far, m, d))

    for i, far, m, d in sent:
        at = p.column(d, cols)
        remote(k_ref.at[:, at], far.at[m - 1, :, at], kv_sends.at[i], kv_recvs.at[i], p.mate(m)).wait()
    gather.finish()

    @pl.when(p.stays)
    def _():
        remote(rep, rep, rep_sems.at[0], rep_sems.at[1], p.sibling).wait_send()

    for s in range(cap):
        for low in range(p.half):
            to = s * p.group + p.core * p.half + low
            for core in range(2):
                i = (s * p.half + low) * 2 + core
                mine = jnp.logical_and(core == p.core, to == p.t)

                @pl.when(jnp.logical_not(mine))
                def _():
                    remote(
                        thin_send.at[s], thin.at[0], thin_sends.at[i], thin_recvs.at[0], p.sibling
                    ).wait_send()

    keep.wait()


def first_part(cap, choice, count, tokens, w, gain, rep_tables, thin_tables):
    n_dp, n_t = lax.axis_size("dp"), lax.axis_size("tensor")
    rows, width = tokens.shape
    depth3, cols = w.shape
    group = n_t // cap
    thin_width = 4 * cols + 2 * thin_tables[2].shape[-1]
    shape = jax.ShapeDtypeStruct
    n_kv = n_t * 2 * (group - 1)
    return pl.pallas_call(
        functools.partial(first_kernel, n_dp, n_t, cap),
        in_specs=[IN_SMEM, IN_SMEM, ANY, ANY] + [IN_VMEM] * 9,
        out_specs=[IN_VMEM] * 7 + [ANY] * 4,
        out_shape=[shape((rows, width), BF)] * 4
        + [
            shape((RANK, rows), BF),
            shape((n_t, RANK, thin_width), BF),
            shape((5 * RANK, width), BF),
            shape((rows, width), BF),
            shape((group - 1, rows, width), BF),
            shape((group - 1, rows, width), BF),
            shape((n_t, n_dp // 2, 2, depth3, cols), BF),
        ],
        scratch_shapes=[
            pltpu.VMEM((rows, width), BF),
            pltpu.VMEM((n_t, RANK, thin_width), BF),
            pltpu.VMEM((cap, RANK, thin_width), BF),
            pltpu.VMEM((5 * RANK, width), BF),
            pltpu.VMEM((2, n_dp // 2, 2, depth3, cols), BF),
            pltpu.VMEM((rows, RANK), BF),
            *Gather.scratch(n_dp, range(n_t)),
            DMA((3,)), DMA((n_t,)), DMA((n_t,)), DMA((2,)), DMA((2,)), DMA((n_kv,)), DMA((n_kv,)), DMA(()),
        ],
        compiler_params=params(collective_id=0, has_side_effects=True),
        name="first_part",
    )(choice, count, tokens, w, gain, *rep_tables, *thin_tables)


def head_masks(shape):
    lane = lax.broadcasted_iota(jnp.int32, shape, 1)
    return lane < HEAD_DIM, lane >= HEAD_DIM


def ones_lanes(rows, count):
    lane = lax.broadcasted_iota(jnp.int32, (rows, PAIR), 1)
    return jnp.where(lane < count, 1.0, 0.0).astype(BF)


def with_far(near_ref, far_ref):
    return jnp.concatenate([near_ref[...]] + [far_ref[m] for m in range(far_ref.shape[0])], axis=0)


def attend(q_ref, k_ref, k_far, v_ref, v_far, o_ref, lse_ref):
    rows = q_ref.shape[0]
    keys = with_far(k_ref, k_far)
    length = keys.shape[0]
    values = jnp.concatenate([with_far(v_ref, v_far), ones_lanes(length, 1)], axis=1)
    queries = q_ref[...]
    zero = jnp.zeros_like(queries)
    outs, sums = [], []
    for mask in head_masks(queries.shape):
        scores = dot(jnp.where(mask, queries, zero), keys, 1, 1)
        top = jnp.max(scores, axis=1, keepdims=True)
        probs = jnp.exp2(scores - top).astype(BF)
        mixed = dot(probs, values, 1, 0)
        total = mixed[:, PAIR : PAIR + 1]
        outs.append(mixed[:, :PAIR] / total)
        sums.append(top + jnp.log2(total))
    first, _ = head_masks((rows, PAIR))
    o_ref[...] = jnp.where(first, outs[0], outs[1]).astype(BF)
    lse_ref[...] = jnp.where(first, sums[0], sums[1])


def attend_kernel(
    n_dp, n_t, cap,
    q_ref, k_ref, k_far, v_ref, v_far, wo_ref, we_ref, ws_ref, cot_ref,
    o_ref, lse_ref, wo_full, we_full, ws_full, cot_out, *sems,
):
    p = Place(n_dp, n_t, cap)
    step, steps = pl.program_id(0), pl.num_programs(0)
    early = list(range(n_t // 2))
    out_g = Gather(p, wo_ref, wo_full, range(n_t), sems[0:3])
    exp_g = Gather(p, we_ref, we_full, early, sems[3:6])
    shr_g = Gather(p, ws_ref, ws_full, early, sems[6:9])
    swap_sems = [sems[9].at[i] for i in range(3)]

    def starts():
        greet(p.gather_peers() + p.other_core_peers())
        for g in (exp_g, shr_g, out_g):
            g.start()
        move(p, cot_ref, cot_out, swap_sems, "start")

    events = [starts]
    both = (exp_g, shr_g)
    for d in range(n_t):
        if d in early:
            events.append(lambda d=d: [g.diag(d) for g in both])
        events.append(lambda d=d: out_g.diag(d))
        if d + 1 in early:
            events.append(lambda d=d: [g.relay(d + 1) for g in both])
        if d + 1 < n_t:
            events.append(lambda d=d: out_g.relay(d + 1))
        if d in early:
            events.append(lambda d=d: [g.share(d) for g in both])
        events.append(lambda d=d: out_g.share(d))
    places_left = 8
    for i in range(places_left):
        batch = events[:1] if i == 0 else events[1 + (len(events) - 1) * (i - 1) // 7 : 1 + (len(events) - 1) * i // 7]

        @pl.when(step == i)
        def _():
            for event in batch:
                event()

    attend(q_ref, k_ref, k_far, v_ref, v_far, o_ref, lse_ref)

    @pl.when(step == steps - 1)
    def _():
        for g in (exp_g, shr_g, out_g):
            for d in g.ds:
                g.done(d)
            g.finish()
        move(p, cot_ref, cot_out, swap_sems, "wait")


def attention_forward(cap, q, k, k_far, v, v_far, wo, we, ws, cot):
    n_dp, n_t = lax.axis_size("dp"), lax.axis_size("tensor")
    rows, width = q.shape
    pair = pl.BlockSpec((rows, PAIR), lambda h: (0, h))
    far = pl.BlockSpec((k_far.shape[0], rows, PAIR), lambda h: (0, 0, h))
    shape = jax.ShapeDtypeStruct
    early = n_t // 2
    full = lambda n, w: shape((n, n_dp // 2, 2, *w.shape), BF)
    return pl.pallas_call(
        functools.partial(attend_kernel, n_dp, n_t, cap),
        grid=(width // PAIR,),
        in_specs=[pair, pair, far, pair, far] + [ANY] * 4,
        out_specs=[pair, pair] + [ANY] * 4,
        out_shape=[
            shape((rows, width), BF), shape((rows, width), F32),
            full(n_t, wo), full(early, we), full(early, ws), shape((rows, width), BF),
        ],
        scratch_shapes=Gather.scratch(n_dp, range(n_t)) + Gather.scratch(n_dp, range(early)) * 2 + [DMA((3,))],
        compiler_params=params(collective_id=1, has_side_effects=True),
        name="attention_forward",
    )(q, k, k_far, v, v_far, wo, we, ws, cot)


def split_lanes(column):
    column = -column
    high = column.astype(BF)
    rest = column - high.astype(F32)
    mid = rest.astype(BF)
    low = (rest - mid.astype(F32)).astype(BF)
    lane = lax.broadcasted_iota(jnp.int32, (column.shape[0], PAIR), 1)
    zero = jnp.zeros((column.shape[0], PAIR), BF)
    return jnp.where(lane == 0, high, jnp.where(lane == 1, mid, jnp.where(lane == 2, low, zero)))


def attend_back_kernel(
    n_dp, n_t, cap,
    q_ref, k_ref, k_far, v_ref, v_far, o_ref, lse_ref, do_ref, mixed_ref, grads_ref,
    dq_ref, dk_ref, dv_ref, dk_far, dv_far, mixed_out, grads_full,
    dk_send, dv_send, sends, recvs, g_send, g_recv, g_own, swap,
):
    p = Place(n_dp, n_t, cap)
    step, steps = pl.program_id(0), pl.num_programs(0)
    rows = q_ref.shape[0]
    gather = Gather(
        p, grads_ref.at[0], grads_full, range(n_t), (g_send, g_recv, g_own),
        spread=lambda d: grads_ref.at[n_t - d], by_rows=False,
    )
    swap_sems = [swap.at[i] for i in range(3)]

    def starts():
        greet(p.gather_peers() + p.other_core_peers())
        gather.start()
        move(p, mixed_ref, mixed_out, swap_sems, "start")

    events = [starts]
    for d in range(n_t):
        events.append(lambda d=d: gather.diag(d))
        if d + 1 < n_t:
            events.append(lambda d=d: gather.relay(d + 1))
        events.append(lambda d=d: gather.share(d))
    for i in range(8):
        batch = events[:1] if i == 0 else events[1 + (len(events) - 1) * (i - 1) // 7 : 1 + (len(events) - 1) * i // 7]

        @pl.when(step == i)
        def _():
            for event in batch:
                event()

    keys = with_far(k_ref, k_far)
    length = keys.shape[0]
    ones = ones_lanes(length, 3)
    keys_more = jnp.concatenate([keys, ones], axis=1)
    values_more = jnp.concatenate([with_far(v_ref, v_far), ones], axis=1)
    queries, grad = q_ref[...], do_ref[...]
    zero = jnp.zeros_like(queries)
    product = grad.astype(F32) * o_ref[...].astype(F32)
    d_queries, d_keys, d_values = [], 0.0, 0.0
    for head, mask in enumerate(head_masks(queries.shape)):
        query = jnp.where(mask, queries, zero)
        grad_head = jnp.where(mask, grad, zero)
        lse = lse_ref[:, head * HEAD_DIM : head * HEAD_DIM + 1]
        delta = jnp.sum(jnp.where(mask, product, 0.0), axis=1, keepdims=True)
        probs = jnp.exp2(dot(jnp.concatenate([query, split_lanes(lse)], axis=1), keys_more, 1, 1))
        slope = dot(jnp.concatenate([grad_head, split_lanes(delta)], axis=1), values_more, 1, 1)
        score_grad = (probs * slope).astype(BF)
        d_queries.append(dot(score_grad, keys, 1, 0))
        d_values = d_values + dot(grad_head, probs.astype(BF), 0, 0)
        d_keys = d_keys + dot(query, score_grad, 0, 0)
    first, _ = head_masks((rows, PAIR))
    dq_ref[...] = (jnp.where(first, d_queries[0], d_queries[1]) * HEAD_DIM**-0.5).astype(BF)
    d_keys = (d_keys * LN2).T.astype(BF)
    d_values = d_values.T.astype(BF)
    dk_ref[...] = d_keys[:rows]
    dv_ref[...] = d_values[:rows]

    def far_copy(i, m, h):
        at = pl.ds(pl.multiple_of(h * PAIR, PAIR), PAIR)
        source, target = ((dk_send, dk_far), (dv_send, dv_far))[i]
        return remote(
            source.at[m - 1, :, at], target.at[m - 1, :, at],
            sends.at[i, m - 1, h], recvs.at[i, m - 1, h], p.mate(p.group - m),
        )

    at = pl.ds(pl.multiple_of(step * PAIR, PAIR), PAIR)
    for m in range(1, p.group):
        dk_send[m - 1, :, at] = d_keys[m * rows : (m + 1) * rows]
        dv_send[m - 1, :, at] = d_values[m * rows : (m + 1) * rows]
        far_copy(0, m, step).start()
        far_copy(1, m, step).start()

    @pl.when(step == steps - 1)
    def _():
        for d in range(n_t):
            gather.done(d)
        gather.finish()
        move(p, mixed_ref, mixed_out, swap_sems, "wait")

        @pl.loop(0, steps)
        def _(h):
            for m in range(1, p.group):
                far_copy(0, m, h).wait()
                far_copy(1, m, h).wait()


def attention_backward(cap, q, k, k_far, v, v_far, o, lse, do, mixed, grads):
    n_dp, n_t = lax.axis_size("dp"), lax.axis_size("tensor")
    rows, width = q.shape
    others = k_far.shape[0]
    pair = pl.BlockSpec((rows, PAIR), lambda h: (0, h))
    far = pl.BlockSpec((others, rows, PAIR), lambda h: (0, 0, h))
    shape = jax.ShapeDtypeStruct
    count = (2, others, width // PAIR)
    return pl.pallas_call(
        functools.partial(attend_back_kernel, n_dp, n_t, cap),
        grid=(width // PAIR,),
        in_specs=[pair, pair, far, pair, far, pair, pair, pair, ANY, ANY],
        out_specs=[pair] * 3 + [ANY] * 4,
        out_shape=[shape((rows, width), BF)] * 3
        + [shape((others, rows, width), BF)] * 2
        + [shape((rows, width), BF), shape((n_t, n_dp // 2, 2, *grads.shape[1:]), BF)],
        scratch_shapes=[
            pltpu.VMEM((others, rows, width), BF), pltpu.VMEM((others, rows, width), BF),
            DMA(count), DMA(count), *Gather.scratch(n_dp, range(n_t)), DMA((3,)),
        ],
        compiler_params=params(collective_id=3, has_side_effects=True),
        name="attention_backward",
    )(q, k, k_far, v, v_far, o, lse, do, mixed, grads)


def gelu_parts(hidden):
    share = 0.5 * (1.0 + lax.erf(hidden * 0.7071067811865476))
    density = jnp.exp(-0.5 * hidden * hidden) * 0.3989422804014327
    return hidden * share, share + hidden * density


def middle_kernel(
    n_dp, n_t, cap, sub,
    x_ref, att_ref, cot_ref, gain_ref, rep_ref, thin_ref, wo_ref, we_near, ws_near, we_ref, ws_ref,
    mixed_ref, mgrad_ref, agrad_ref, grads_ref, we_full, ws_full,
    middle_ref, second_ref, dy_ref, acc2_ref, acc3_ref, einner_ref, einner_t_ref, sback_ref, sback_t_ref,
    sinner_ref, eback_ref, oinner_ref, we_buf, ws_buf, buf_sems, *sems,
):
    p = Place(n_dp, n_t, cap)
    step, steps = pl.program_id(0), pl.num_programs(0)
    cols = wo_ref.shape[-1]
    width = x_ref.shape[1]
    hid = we_ref.shape[-1]
    size = hid // sub
    near = n_t // 2
    late = list(range(near, n_t))
    exp_g = Gather(p, we_ref, we_full, late, sems[0:3])
    shr_g = Gather(p, ws_ref, ws_full, late, sems[3:6])
    both = (exp_g, shr_g)
    down_e, up_o, up_s = rep_ref[2 * RANK : 3 * RANK], rep_ref[RANK : 2 * RANK], rep_ref[3 * RANK : 4 * RANK]
    alive = rep_ref[4 * RANK : 4 * RANK + 1, 0:1].astype(F32)
    at_od, at_eu = 3 * width, 3 * width + cols
    at_sd, at_id = at_eu + hid, at_eu + 2 * hid

    def load(i):
        d, part = i // sub, i % sub
        at = pl.ds(part * size, size)
        pair = (we_near, ws_near) if d < near else (we_full, ws_full)
        index = d if d < near else d - near
        return [
            pltpu.make_async_copy(src.at[index, :, :, :, at], buf.at[i % 2], buf_sems.at[i % 2, j])
            for j, (src, buf) in enumerate(zip(pair, (we_buf, ws_buf)))
        ]

    @pl.when(step == 0)
    def _():
        greet(p.gather_peers())
        for g in both:
            g.start()
        for copy in load(0):
            copy.start()
        branch, inner = 0.0, 0.0
        for d in range(n_t):
            att = att_ref[:, p.column(d, cols)]
            branch = branch + dot(att, wo_ref[d].reshape(width, cols), 1, 1)
            inner = inner + dot(att, thin_ref[d, :, 3 * cols : 4 * cols], 1, 1)
        inner = inner.astype(BF)
        oinner_ref[...] = inner
        middle = x_ref[...].astype(F32) + (branch + dot(inner, up_o, 1, 0))
        middle_ref[...] = middle
        hat, _ = norm_parts(middle)
        second = (hat * gain_ref[...]).astype(BF)
        second_ref[...] = second
        dy = (cot_ref[...].astype(F32) * alive).astype(BF)
        dy_ref[...] = dy
        einner_ref[...] = dot(second, down_e, 1, 1).astype(BF)
        einner_t_ref[...] = dot(down_e, second, 1, 1).astype(BF)
        sback_ref[...] = dot(dy, up_s, 1, 1).astype(BF)
        sback_t_ref[...] = dot(up_s, dy, 1, 1).astype(BF)
        acc2_ref[...] = jnp.zeros_like(acc2_ref)
        acc3_ref[...] = jnp.zeros_like(acc3_ref)
        sinner_ref[...] = jnp.zeros_like(sinner_ref)
        eback_ref[...] = jnp.zeros_like(eback_ref)

    for i in range(n_t * sub):

        @pl.when(step == i)
        def _():
            for d in late:
                first = (d - 2) * sub if near == 2 else 0
                if i == max(1, first + sub - 1):
                    [g.relay(d) for g in both]
                if i == max(1, first + sub):
                    [g.diag(d) for g in both]
                if i == max(1, first + sub + 1):
                    [g.share(d) for g in both]
            for copy in load(i):
                copy.wait()
            if i + 1 < n_t * sub and (i + 1) // sub < near:
                for copy in load(i + 1):
                    copy.start()

    buf = step % 2
    d, part = step // sub, step % sub
    we, ws = we_buf[buf].reshape(width, size), ws_buf[buf].reshape(width, size)
    at = pl.multiple_of(part * size, size)
    e_up = thin_ref[d, :, pl.ds(4 * cols + at, size)]
    s_down = thin_ref[d, :, pl.ds(4 * cols + hid + at, size)]
    hidden = dot(second_ref[...], we, 1, 0) + dot(einner_ref[...], e_up, 1, 0)
    value, slope = gelu_parts(hidden)
    act = value.astype(BF)
    acc2_ref[...] += dot(act, ws, 1, 1)
    sinner_ref[...] += dot(act, s_down, 1, 1)
    act_grad = dot(dy_ref[...], ws, 1, 0) + dot(sback_ref[...], s_down, 1, 0)
    hid_grad = (act_grad * slope).astype(BF)
    acc3_ref[...] += dot(hid_grad, we, 1, 1)
    eback_ref[...] += dot(hid_grad, e_up, 1, 1)
    grads_ref[d, :, pl.ds(at_eu + at, size)] = dot(einner_t_ref[...], hid_grad, 1, 0).astype(BF)
    grads_ref[d, :, pl.ds(at_sd + at, size)] = dot(sback_t_ref[...], act, 1, 0).astype(BF)

    for i in range(n_t * sub - 1):
        if (i + 1) // sub >= near:

            @pl.when(step == i)
            def _():
                if (i + 1) % sub == 0:
                    for g in both:
                        g.done((i + 1) // sub)
                for copy in load(i + 1):
                    copy.start()

    @pl.when(step == steps - 1)
    def _():
        s_inner, e_back = sinner_ref[...].astype(BF), eback_ref[...].astype(BF)
        middle = middle_ref[...]
        mixed_ref[...] = (alive * (middle + (acc2_ref[...] + dot(s_inner, up_s, 1, 0)))).astype(BF)
        shrink_up = dot(s_inner, dy_ref[...], 0, 0).astype(BF)
        expand_down = dot(e_back, second_ref[...], 0, 0).astype(BF)
        second_grad = acc3_ref[...] + dot(e_back, down_e, 1, 0)
        hat, scale = norm_parts(middle)
        mgrad = cot_ref[...].astype(F32) * alive + norm_back(hat, scale, gain_ref[...], second_grad)
        mgrad_ref[...] = mgrad
        low = mgrad.astype(BF)
        o_back = dot(low, up_o, 1, 1).astype(BF)
        output_up = dot(oinner_ref[...], low, 0, 0).astype(BF)
        for d in range(n_t):
            at = p.column(d, cols)
            agrad_ref[:, at] = (
                dot(low, wo_ref[d].reshape(width, cols), 1, 0)
                + dot(o_back, thin_ref[d, :, 3 * cols : 4 * cols], 1, 0)
            ).astype(BF)
            grads_ref[d, :, :width] = expand_down
            grads_ref[d, :, width : 2 * width] = shrink_up
            grads_ref[d, :, 2 * width : 3 * width] = output_up
            grads_ref[d, :, at_od : at_od + cols] = dot(o_back, att_ref[:, at], 0, 0).astype(BF)
            grads_ref[d, :, at_id:] = rep_ref[4 * RANK :, : grads_ref.shape[2] - at_id]
        for g in both:
            g.finish()


ID_LANES = 128


def middle_both_ways(cap, x, att, cot, gain, rep, thin, wo_full, we_near, ws_near, we, ws):
    n_dp, n_t = lax.axis_size("dp"), lax.axis_size("tensor")
    rows, width = x.shape
    depth, hid = we.shape
    cols = wo_full.shape[-1]
    sub = max(1, hid // 512)
    size = hid // sub
    late = range(n_t // 2, n_t)
    grad_width = 3 * width + cols + 2 * hid + ID_LANES
    whole = lambda a: pl.BlockSpec(a.shape, lambda i: (0,) * len(a.shape))
    shape = jax.ShapeDtypeStruct
    full = shape((len(late), n_dp // 2, 2, depth, hid), BF)
    outs = [
        shape((rows, width), BF), shape((rows, width), F32), shape((rows, width), BF),
        shape((n_t, RANK, grad_width), BF),
    ]
    vmem = pltpu.VMEM
    return pl.pallas_call(
        functools.partial(middle_kernel, n_dp, n_t, cap, sub),
        grid=(n_t * sub,),
        in_specs=[whole(a) for a in (x, att, cot, gain, rep, thin, wo_full)] + [ANY] * 4,
        out_specs=[whole(a) for a in outs] + [ANY] * 2,
        out_shape=outs + [full, full],
        scratch_shapes=[
            vmem((rows, width), F32), vmem((rows, width), BF), vmem((rows, width), BF),
            vmem((rows, width), F32), vmem((rows, width), F32),
            vmem((rows, RANK), BF), vmem((RANK, rows), BF), vmem((rows, RANK), BF), vmem((RANK, rows), BF),
            vmem((rows, RANK), F32), vmem((rows, RANK), F32), vmem((rows, RANK), BF),
            vmem((2, n_dp // 2, 2, depth, size), BF), vmem((2, n_dp // 2, 2, depth, size), BF), DMA((2, 2)),
            *Gather.scratch(n_dp, late), *Gather.scratch(n_dp, late),
        ],
        compiler_params=params(collective_id=2, has_side_effects=True),
        name="middle_both_ways",
    )(x, att, cot, gain, rep, thin, wo_full, we_near, ws_near, we, ws)


def last_kernel(
    n_dp, n_t, cap, tiles,
    gain_ref, rep_ref, thin_ref, inner_t_ref, dq_ref, dk_ref, dv_ref, dk_far, dv_far, w_ref, mgrad_ref, tok_ref, normed_ref,
    tgrad_out, grads_full,
    weights, grad, far, mgrad, tok, normed, back_low, tgrad, grads, load_sems, g_send, g_recv, g_own, swaps,
):
    p = Place(n_dp, n_t, cap)
    cols = w_ref.shape[-1]
    depth = w_ref.shape[-2] // 3
    width = tok_ref.shape[1]
    loads = [
        pltpu.make_async_copy(src, dst, load_sems.at[i])
        for i, (src, dst) in enumerate(
            (
                (dq_ref, grad.at[0]), (dk_ref, grad.at[1]), (dk_far, far.at[0]), (dv_ref, grad.at[2]),
                (dv_far, far.at[1]), (normed_ref, normed), (w_ref, weights), (tok_ref, tok), (mgrad_ref, mgrad),
            )
        )
    ]
    for copy in loads:
        copy.start()
    greet(p.gather_peers() + p.other_core_peers())
    for copy in loads[:5]:
        copy.wait()
    for i in range(2):
        total = grad[1 + i].astype(F32)
        for m in range(far.shape[1]):
            total = total + far[i, m].astype(F32)
        grad[1 + i] = total.astype(BF)
    back = 0.0
    for d in range(n_t):
        at = p.column(d, cols)
        for which in range(3):
            part = grad[which, :, at]
            back = back + dot(part, thin_ref[d, :, which * cols : (which + 1) * cols], 1, 1)
            grads[d, :, which * cols : (which + 1) * cols] = dot(inner_t_ref[...], part, 1, 0).astype(BF)
    back = back.astype(BF)
    back_low[...] = back
    loads[5].wait()
    down_grad = dot(back, normed[...], 0, 0).astype(BF)
    for d in range(n_t):
        grads[d, :, 3 * cols :] = down_grad
    gather = Gather(
        p, grads.at[0], grads_full, range(n_t), (g_send, g_recv, g_own),
        spread=lambda d: grads.at[n_t - d], by_rows=False,
    )
    gather.start()
    for copy in loads[6:]:
        copy.wait()
    events = []
    for d in range(n_t):
        events.append(lambda d=d: gather.diag(d))
        if d + 1 < n_t:
            events.append(lambda d=d: gather.relay(d + 1))
        events.append(lambda d=d: gather.share(d))
    for n, (start, count) in enumerate(tiles):
        rows = pl.ds(start, count)
        total = dot(back_low[rows], rep_ref[:RANK], 1, 0)
        for d in range(n_t):
            at = p.column(d, cols)
            for which in range(3):
                piece = weights[d, :, :, which * depth : (which + 1) * depth].reshape(width, cols)
                total = total + dot(grad[which, rows, at], piece, 1, 1)
        hat, scale = norm_parts(tok[rows].astype(F32))
        tgrad[rows] = (mgrad[rows] + norm_back(hat, scale, gain_ref[...], total)).astype(BF)
        move(p, tgrad, tgrad_out, [swaps.at[n, i] for i in range(3)], "start", rows)
        for event in events[len(events) * n // len(tiles) : len(events) * (n + 1) // len(tiles)]:
            event()
    for d in range(n_t):
        gather.done(d)
    gather.finish()
    for n, (start, count) in enumerate(tiles):
        move(p, tgrad, tgrad_out, [swaps.at[n, i] for i in range(3)], "wait", pl.ds(start, count))


def last_part(cap, gain, rep, thin, inner_t, dq, dk, dv, dk_far, dv_far, w_full, mgrad, tok, normed):
    n_dp, n_t = lax.axis_size("dp"), lax.axis_size("tensor")
    rows, width = tok.shape
    cols = w_full.shape[-1]
    others = dk_far.shape[0]
    count = 3 if rows % 16 == 0 else 1
    step = rows // count // 16 * 16 if count > 1 else rows
    tiles = [(0, rows - step * (count - 1))]
    tiles += [(tiles[0][1] + step * i, step) for i in range(count - 1)]
    grad_width = 3 * cols + width
    shape, vmem = jax.ShapeDtypeStruct, pltpu.VMEM
    return pl.pallas_call(
        functools.partial(last_kernel, n_dp, n_t, cap, tiles),
        in_specs=[IN_VMEM] * 4 + [ANY] * 9,
        out_specs=[ANY] * 2,
        out_shape=[shape((rows, width), BF), shape((n_t, n_dp // 2, 2, RANK, grad_width), BF)],
        scratch_shapes=[
            vmem(w_full.shape, BF), vmem((3, rows, width), BF), vmem((2, others, rows, width), BF),
            vmem((rows, width), F32), vmem((rows, width), BF), vmem((rows, width), BF), vmem((rows, RANK), BF),
            vmem((rows, width), BF), vmem((n_t, RANK, grad_width), BF), DMA((9,)),
            *Gather.scratch(n_dp, range(n_t)), DMA((len(tiles), 3)),
        ],
        compiler_params=params(collective_id=4, has_side_effects=True),
        name="last_part",
    )(gain, rep, thin, inner_t, dq, dk, dv, dk_far, dv_far, w_full, mgrad, tok, normed)


def sum_kernel(
    width, cols, hid, mid_ref, end_ref, entry_down, entry_up, output_down, output_up, expand_down, expand_up,
    shrink_down, shrink_up,
):
    outs = (entry_down, entry_up, output_down, output_up, expand_down, expand_up, shrink_down, shrink_up)
    for out in outs:
        out[...] = jnp.zeros_like(out)
    sources = mid_ref.shape[0]

    @pl.loop(0, sources)
    def _(i):
        tail = mid_ref[i, :, 3 * width + cols + 2 * hid :].astype(F32)
        a = jnp.max(tail[RANK // 2 :]).astype(jnp.int32)
        take = lambda ref, at, size: ref[i, :, at : at + size].astype(F32)
        expand_down[a] += take(mid_ref, 0, width)
        shrink_up[a] += take(mid_ref, width, width)
        output_up[a] += take(mid_ref, 2 * width, width)
        output_down[a] += take(mid_ref, 3 * width, cols)
        expand_up[a] += take(mid_ref, 3 * width + cols, hid)
        shrink_down[a] += take(mid_ref, 3 * width + cols + hid, hid)
        for which in range(3):
            entry_up[a, which] += take(end_ref, which * cols, cols)
        entry_down[a] += take(end_ref, 3 * cols, width)


def sum_gradients(adapters, cols, hid, width, mid, end):
    shape = jax.ShapeDtypeStruct
    wide = shape((adapters, RANK, width), F32)
    flat = lambda a: a.reshape(-1, *a.shape[-2:])
    return pl.pallas_call(
        functools.partial(sum_kernel, width, cols, hid),
        in_specs=[IN_VMEM] * 2,
        out_specs=[IN_VMEM] * 8,
        out_shape=[
            wide, shape((adapters, 3, RANK, cols), F32), shape((adapters, RANK, cols), F32), wide,
            wide, shape((adapters, RANK, hid), F32), shape((adapters, RANK, hid), F32), wide,
        ],
        compiler_params=params(),
        name="sum_gradients",
    )(flat(mid), flat(end))


def local(
    tokens, cotangent, norm_first, norm_second, entry_weight, output_weight, expand_weight, shrink_weight,
    entry_down, entry_up, output_down, output_up, expand_down, expand_up, shrink_down, shrink_up,
    adapter_choice, clip_count,
):
    cap = adapter_choice.shape[0]
    rows, width = tokens.shape
    adapters = entry_down.shape[0]
    cols, hid = output_weight.shape[1], expand_weight.shape[1]
    gain_first, gain_second = norm_first.reshape(1, width), norm_second.reshape(1, width)
    flip = lambda a: a.transpose(0, 2, 1)
    w_entry = entry_weight.transpose(1, 0, 2).reshape(-1, cols)
    q, k, v, normed, inner_t, thin, rep, tok, k_far, v_far, w_full = first_part(
        cap, adapter_choice, clip_count, tokens, w_entry, gain_first,
        (flip(entry_down), output_up, flip(expand_down), shrink_up),
        (entry_up.transpose(0, 2, 1, 3), flip(output_down), expand_up, flip(shrink_down)),
    )
    att, lse, wo_full, we_near, ws_near, cot = attention_forward(
        cap, q, k, k_far, v, v_far, output_weight, expand_weight, shrink_weight, cotangent
    )
    mixed, mgrad, agrad, grads, _, _ = middle_both_ways(
        cap, tok, att, cot, gain_second, rep, thin, wo_full, we_near, ws_near, expand_weight, shrink_weight
    )
    dq, dk, dv, dk_far, dv_far, mixed, mid_grads = attention_backward(
        cap, q, k, k_far, v, v_far, att, lse, agrad, mixed, grads
    )
    token_grad, end_grads = last_part(
        cap, gain_first, rep, thin, inner_t, dq, dk, dv, dk_far, dv_far, w_full, mgrad, tok, normed
    )
    ed, eu, od, ou, xd, xu, sd, su = sum_gradients(adapters, cols, hid, width, mid_grads, end_grads)
    return (
        mixed, token_grad, flip(ed), eu.transpose(0, 2, 1, 3), flip(od), ou, flip(xd), xu, flip(sd), su,
    )


def solution(mesh):
    in_specs = (
        P(BOTH, None), P(BOTH, None), P(), P(),
        P("dp", None, "tensor"), P("dp", "tensor"), P("dp", "tensor"), P("dp", "tensor"),
        P(), P(None, None, None, "tensor"), P(None, "tensor", None), P(),
        P(), P(None, None, "tensor"), P(None, "tensor", None), P(), P("dp"), P("dp"),
    )
    out_specs = (
        P(BOTH, None), P(BOTH, None), P(), P(None, None, None, "tensor"), P(None, "tensor", None), P(),
        P(), P(None, None, "tensor"), P(None, "tensor", None), P(),
    )
    return jax.shard_map(local, mesh=mesh, in_specs=in_specs, out_specs=out_specs, check_vma=False)
```

time: 609 us -> 373 us (0.61)
  waiting for transfers between devices: 309 us -> 0 us
  Pallas kernels: 179 us -> 361 us
  local copies, waits for them, and re-layouts: 42.6 us -> 3.16 us
  starting transfers between devices: 28.6 us -> 0 us
  between operations: 18.9 us -> 1.53 us
  blocking collectives: 10.5 us -> 0 us
    all_gather x5 -> x0, waiting for transfers between devices: 224 us -> none  [the longest x4 165 us: local(): lax.all_gather(w, BOTH, axis=0).reshape(n_dp, n_t, *w.shape)]
    pallas_call x5 -> x6, Pallas kernels: 179 us -> 361 us  [the longest x1 94.1 us: middle_both_ways(): pl.pallas_call(functools.partial(middle_kernel, n_dp, n_t, cap, sub), gri...]
    psum x1 -> x0, waiting for transfers between devices: 48.9 us -> none  [local(): thin_g = lax.psum(thin_g.astype(BF), 'dp').astype(F32)]
    all_to_all x2 -> x0, waiting for transfers between devices: 32.3 us -> none  [the longest x1 20.1 us: local(): got = lax.all_to_all(sent, 'tensor', 0, 0)]
    ppermute x8 -> x0, starting transfers between devices: 21.1 us -> none  [the longest x1 13.8 us: local(): cot = lax.ppermute(cotangent, BOTH, places.swap_pairs())]
    unnamed x63 -> x6, local copies, waits for them, and re-layouts: 22.5 us -> 3.16 us
    unnamed x1 -> x0, blocking collectives: 10.5 us -> none
    slice x5 -> x0, local copies, waits for them, and re-layouts: 7.54 us -> none  [the longest x2 6.17 us: returned(): grad[s * rows:(s + 1) * rows]]
  transfers between devices with their start and end apart: 16 -> 0, of which waited for: 8 -> 0; matrix products, arithmetic and copies ran while one was open for 5% -> 0% of each run, Pallas kernels for 9% -> 0%
where the time goes in v2:
time: 373 us; the launch traced here: 366 us
  Pallas kernels  361 us (97%)
    pallas_call x1, Pallas kernels, middle_both_ways(): pl.pallas_call(functools.partial(middle_kernel, n_dp, n_t, cap, sub), gri...  94.1 us
    pallas_call x1, Pallas kernels, attention_forward(): pl.pallas_call(functools.partial(attend_kernel, n_dp, n_t, cap), grid=(wi...  74.3 us
    pallas_call x1, Pallas kernels, first_part(): pl.pallas_call(functools.partial(first_kernel, n_dp, n_t, cap), in_specs=...  72.3 us
    pallas_call x1, Pallas kernels, attention_backward(): pl.pallas_call(functools.partial(attend_back_kernel, n_dp, n_t, cap), gri...  71.9 us
    pallas_call x1, Pallas kernels, last_part(): pl.pallas_call(functools.partial(last_kernel, n_dp, n_t, cap, tiles), in_...  38.3 us
    pallas_call x1, Pallas kernels, sum_gradients(): pl.pallas_call(functools.partial(sum_kernel, width, cols, hid), in_specs=...  10.4 us

profile of v2, /device:TPU:0, one launch (start us, length us, event | category | flops | bytes accessed | tf_op | source)
XLA Modules:
  0.0 365.8 jit_solution(816260307500942657)
XLA Ops:
  1.3 72.3 %first_part.1 = (bf16[784,1024]{1,0:T(8,128)(2,1)}, bf16[784,1024]{1,0:T(8,128)(2,1)}, bf16[784,1024]{1,0:T(8,128)(2,1)}, bf16[784,1024]{1,0:T(8,128)(2,1)}, bf1...) custom-call(s32[2]{0:T(128)} %choice_ref.1, ...), custom_call_target="tpu_custom_call" | custom-call | tf_op jit(solution)/shard_map/first_part/pallas_call | solution.py:365
  73.6 74.3 %attention_forward.1 = (bf16[784,1024]{1,0:T(8,128)(2,1)}, f32[784,1024]{1,0:T(8,128)}, bf16[4,4,2,128,256]{4,3,2,1,0:T(8,128)(2,1)}, bf16[2,4,2,128,1024]{4,3,2...) custom-call(bf16[784,1024]{1,0:T(8,128)(2,1)} %get-tuple-element.48.q_ref, ...), custom_call_target="tpu_custom_call" | custom-call | tf_op jit(solution)/shard_map/attention_forward/pallas_call | solution.py:489
  147.8 94.1 %middle_both_ways.1 = (bf16[784,1024]{1,0:T(8,128)(2,1)}, f32[784,1024]{1,0:T(8,128)}, bf16[784,1024]{1,0:T(8,128)(2,1)}, bf16[4,16,5504]{2,1,0:T(8,128)(2,1)}, ...) custom-call(bf16[784,1024]{1,0:T(8,128)(2,1)} %get-tuple-element.55.x_ref.tok_ref, ...), custom_call_target="tpu_custom_call" | custom-call | tf_op jit(solution)/shard_map/middle_both_ways/pallas_call | solution.py:795
  241.9 71.9 %attention_backward.1 = (bf16[784,1024]{1,0:T(8,128)(2,1)}, bf16[784,1024]{1,0:T(8,128)(2,1)}, bf16[784,1024]{1,0:T(8,128)(2,1)}, bf16[1,784,1024]{2,1,0:T(8,128...) custom-call(bf16[784,1024]{1,0:T(8,128)(2,1)} %get-tuple-element.48.q_ref, ...), custom_call_target="tpu_custom_call" | custom-call | tf_op jit(solution)/shard_map/attention_backward/pallas_call | solution.py:613
  313.8 38.3 %last_part.1 = (bf16[784,1024]{1,0:T(8,128)(2,1)}, bf16[4,4,2,16,1792]{4,3,2,1,0:T(8,128)(2,1)}) custom-call(f32[1,1024]{1,0:T(1,128)} %bitcast.26, bf16[80,1024]{1,0:T(8,128)(2,1)} %get-tuple-element.57.rep_ref, bf16[4,16,3072]{2,1,0:T(8,128)(2,1)} %get-tuple-element.58.thin_ref, bf16[16,784]{1,0:T(8,128)(2,1)} %get-tuple-element.66.inner_t_ref, ...), custom_call_target="tpu_custom_call" | custom-call | tf_op jit(solution)/shard_map/last_part/pallas_call | solution.py:900
  352.1 0.0 copy-start
  352.1 10.4 %sum_gradients.1 = (f32[8,16,1024]{2,1,0:T(8,128)}, f32[8,3,16,256]{3,2,1,0:T(8,128)}, f32[8,16,256]{2,1,0:T(8,128)}, f32[8,16,1024]{2,1,0:T(8,128)}, f32[8,16,1...) custom-call(bf16[32,16,5504]{2,1,0:T(8,128)(2,1)} %bitcast.17, ...), custom_call_target="tpu_custom_call" | custom-call | tf_op jit(solution)/shard_map/sum_gradients/pallas_call | solution.py:945
  362.5 0.0 copy-done
  362.5 0.0 copy-start.1
  362.5 1.2 copy.31
  363.6 0.8 copy-done.1
  364.5 1.2 copy.32
Async XLA Ops:
  352.1 10.4 %copy-start = (bf16[784,1024]{1,0:T(8,128)(2,1)S(1)}, bf16[784,1024]{1,0:T(8,128)(2,1)}, u32[]{:S(2)}) copy-start(bf16[784,1024]{1,0:T(8,128)(2,1)} %get-tuple-element.96) | copy-start | bytes 4816900
  362.5 2.0 copy-start.1

commit v3 on v2

v3 whole, which is shorter than its diff:
```python
import functools

import jax
import jax.numpy as jnp
from jax import lax
from jax.experimental import pallas as pl
from jax.experimental.pallas import tpu as pltpu
from jax.sharding import PartitionSpec as P

HEAD_DIM = 64
PAIR = 2 * HEAD_DIM
RANK = 16
LOG2E = 1.4426950408889634
LN2 = 0.6931471805599453
F32, BF = jnp.float32, jnp.bfloat16
VMEM_LIMIT = 60 * 2**20


def dot(a, b, ca, cb):
    return lax.dot_general(a, b, (((ca,), (cb,)), ((), ())), preferred_element_type=F32)


def params(**more):
    return pltpu.CompilerParams(vmem_limit_bytes=VMEM_LIMIT, **more)


def merge_rows(block):
    return block.reshape(block.shape[0] * block.shape[1], block.shape[2])


def norm_parts(values):
    centre = jnp.mean(values, axis=-1, keepdims=True)
    shifted = values - centre
    scale = lax.rsqrt(jnp.mean(shifted * shifted, axis=-1, keepdims=True) + 1e-05)
    return shifted * scale, scale


def norm_back(hat, scale, gain, grad):
    inner = grad * gain
    mean_one = jnp.mean(inner, axis=-1, keepdims=True)
    mean_two = jnp.mean(inner * hat, axis=-1, keepdims=True)
    return scale * (inner - mean_one - hat * mean_two)


MESH = pl.DeviceIdType.MESH
BOTH = ("dp", "tensor")
ANY = pl.BlockSpec(memory_space=pl.ANY)
IN_VMEM = pl.BlockSpec(memory_space=pltpu.VMEM)
IN_SMEM = pl.BlockSpec(memory_space=pltpu.SMEM)
DMA = pltpu.SemaphoreType.DMA


class Place:
    def __init__(self, n_dp, n_t, cap):
        self.n_dp, self.n_t, self.cap = n_dp, n_t, cap
        self.dp, self.t = lax.axis_index("dp"), lax.axis_index("tensor")
        self.core, self.q = self.dp % 2, self.dp // 2
        self.n_q, self.n_hi = n_dp // 2, n_dp // 4
        self.lo, self.hi = self.q % 2, self.q // 2
        self.group = n_t // cap
        self.half = self.group // 2
        self.slot, block = self.t // self.group, self.t % self.group
        self.high, self.low = block // self.half, block % self.half
        self.stays = self.core == self.high
        self.sibling = (self.dp + 1 - 2 * self.core, self.t)
        self.partner = (self.dp - self.core + self.high, self.t - block + self.core * self.half + self.low)

    def along(self, d):
        return (self.t + d) % self.n_t

    def column(self, d, cols):
        return pl.ds(pl.multiple_of(((self.t + self.n_t - d) % self.n_t) * cols, cols), cols)

    def lo_q(self):
        return self.q + 1 - 2 * self.lo

    def hi_q(self, m, lo=None):
        return ((self.hi + m) % self.n_hi) * 2 + (self.lo if lo is None else lo)

    def device(self, q, core=None, t=None):
        return (q * 2 + (self.core if core is None else core), self.t if t is None else t)

    def mate(self, shift):
        block = (self.core * self.half + self.low + shift) % self.group
        return (self.dp - self.core + block // self.half, self.t - self.low + block % self.half)

    def gather_peers(self):
        return (
            [(self.dp, self.along(d)) for d in range(1, self.n_t)]
            + [self.sibling, self.device(self.lo_q())]
            + [self.device(self.hi_q(m)) for m in range(1, self.n_hi)]
        )

    def other_core_peers(self):
        return [(self.sibling[0], self.along(d)) for d in range(1, self.n_t)]


def greet(peers):
    barrier = pltpu.get_barrier_semaphore()
    for peer in peers:
        pl.semaphore_signal(barrier, inc=1, device_id=peer, device_id_type=MESH)
    pl.semaphore_wait(barrier, len(peers))


def remote(src, dst, send, recv, device):
    return pltpu.make_async_remote_copy(
        src_ref=src, dst_ref=dst, send_sem=send, recv_sem=recv, device_id=device, device_id_type=MESH
    )


class Gather:
    @staticmethod
    def keys(n_hi, ds, here):
        found = []
        for d in ds:
            found += [] if d in here else [("z", d)]
            found += [("x", d), ("s", d)]
            for m in range(1, n_hi):
                found += [("y", m, d), ("dy", m, d), ("dx", m, d)]
        return found

    @staticmethod
    def scratch(n_dp, ds, here=(0,)):
        count = len(Gather.keys(n_dp // 4, ds, here))
        return [DMA((count,)), DMA((count,)), DMA((len(here),))]

    def __init__(self, place, sources, full, ds, sems, spread=None, by_rows=True):
        self.place, self.sources, self.full, self.ds = place, sources, full, list(ds)
        self.send, self.recv, self.own = sems
        self.index = {k: i for i, k in enumerate(Gather.keys(place.n_hi, self.ds, sources))}
        self.spread, self.by_rows = spread, by_rows
        self.ms = range(1, place.n_hi)

    def block(self, d, q, half=None):
        ref = self.full.at[self.ds.index(d), q, self.place.core]
        if half is None:
            return ref
        rows, cols = self.full.shape[-2:]
        if self.by_rows:
            return ref.at[pl.ds(half * (rows // 2), rows // 2)]
        first = cols // 2 // 128 * 128
        return ref.at[:, pl.ds(half * first, cols - first if half else first)]

    def copy(self, key):
        p, kind, d = self.place, key[0], key[-1]
        i = self.index[key]
        if kind == "z":
            src = self.sources[0] if self.spread is None else self.spread(d)
            dst, device = self.block(d, p.q), (p.dp, p.along(d))
        elif kind == "s":
            src = dst = self.full.at[self.ds.index(d), :, p.core]
            device = p.sibling
        elif kind in "xy":
            src = self.sources[d] if d in self.sources else self.block(d, p.q)
            dst = self.block(d, p.q)
            device = p.device(p.lo_q() if kind == "x" else p.hi_q(key[1]))
        elif kind == "dy":
            src = dst = self.block(d, p.lo_q(), 0)
            device = p.device(p.hi_q(key[1]))
        else:
            src = dst = self.block(d, p.hi_q(p.n_hi - key[1]), 1)
            device = p.device(p.lo_q())
        return remote(src, dst, self.send.at[i], self.recv.at[i], device)

    def own_copy(self, d):
        i = list(self.sources).index(d)
        return pltpu.make_async_copy(self.sources[d], self.block(d, self.place.q), self.own.at[i])

    def along(self, d):
        self.copy(("z", d)).start()

    def relay(self, d):
        if d in self.sources:
            self.own_copy(d).start()
        else:
            self.copy(("z", d)).wait_recv()
        self.copy(("x", d)).start()
        for m in self.ms:
            self.copy(("y", m, d)).start()

    def diag(self, d):
        self.copy(("x", d)).wait_recv()
        for m in self.ms:
            self.copy(("dy", m, d)).start()
        for m in self.ms:
            self.copy(("y", m, d)).wait_recv()
            self.copy(("dx", m, d)).start()

    def share(self, d):
        if d in self.sources:
            self.own_copy(d).wait()
        for m in self.ms:
            self.copy(("dy", m, d)).wait_recv()
            self.copy(("dx", m, d)).wait_recv()
        self.copy(("s", d)).start()

    def done(self, d):
        self.copy(("s", d)).wait_recv()

    def finish(self):
        for key in self.index:
            self.copy(key).wait_send()


def run_events(step, batches):
    for i, batch in enumerate(batches):
        if batch:

            @pl.when(step == i)
            def _():
                for event in batch:
                    event()


def cut(names, word):
    parts = [[]]
    for name in names:
        if name.startswith(word):
            parts.append([])
        else:
            parts[-1].append(name)
    return parts


def orders(n_t, pairs, sub, group):
    if (n_t, pairs, sub, group) == (4, 2, 2, 2):
        return FRONT, MIDDLE
    near = n_t // 2
    late = list(reversed(range(near, n_t)))
    front = ["greet", "tok", "e.relay.0", "x.relay.0", "h.relay.0", "o.relay.0"]
    for d in range(1, n_t):
        front += [f"e.along.{d}", f"o.along.{d}"] + ([f"x.along.{d}", f"h.along.{d}"] if d < near else [])
    front += ["lx", "lh", "cot"]
    every = lambda g, d: ([f"{g}.relay.{d}"] if d else []) + [f"{g}.diag.{d}", f"{g}.share.{d}"]
    for d in range(n_t):
        front += every("e", d)
    front += ["wtok", "go", "ln"]
    for d in range(n_t):
        front += [f"ready.{d}", f"proj.{d}"]
    for d in range(n_t):
        front += every("o", d) + (every("x", d) + every("h", d) if d < near else [])
    for d in range(n_t):
        front += [f"arrive.{d}"] + [f"attn.{d * pairs + i}" for i in range(pairs)]
    middle = []
    for g in "xh":
        middle += [f"{g}.relay.{late[0]}"] + [f"{g}.along.{d}" for d in late[1:]]
    middle += ["pre"]
    for i in range(n_t * sub):
        middle += [f"ffn.{i}"]
        if i == 0:
            for d in late:
                for g in "xh":
                    middle += ([f"{g}.relay.{d}"] if d != late[0] else []) + [f"{g}.diag.{d}", f"{g}.share.{d}"]
        if (i + 1) % sub == 0 and near <= (i + 1) // sub < n_t:
            middle += [f"cr.{late[(i + 1) // sub - near]}"]
    return front, middle


FRONT = (
    "greet", "e.along.1", "h.relay.0", "e.relay.0", "x.relay.0", "tok", "e.diag.0", "e.along.2",
    "h.diag.0", "e.share.0", "e.relay.1", "wtok", "e.diag.1", "x.diag.0", "e.along.3", "o.along.3",
    "ln", "e.share.1", "o.relay.0", "o.along.2", "e.relay.2", "ready.0", "go", "x.along.1",
    "proj.0", "h.along.1", "ready.1", "e.relay.3", "arrive.0", "o.diag.0", "attn.0", "o.along.1",
    "x.share.0", "e.diag.2", "e.diag.3", "o.relay.2", "proj.1", "x.relay.1", "attn.1", "e.share.2",
    "h.relay.1", "cot", "arrive.1", "attn.2", "h.share.0", "ready.2", "proj.2", "o.relay.1",
    "e.share.3", "attn.3", "h.diag.1", "o.diag.2", "ready.3", "o.relay.3", "lx", "o.diag.1",
    "proj.3", "arrive.2", "attn.4", "arrive.3", "o.share.0", "h.share.1", "o.diag.3", "o.share.2",
    "x.diag.1", "attn.5", "o.share.1", "lh", "o.share.3", "attn.6", "x.share.1", "attn.7",
)
MIDDLE = (
    "x.along.2", "x.relay.3", "pre", "h.relay.3", "ffn.0", "x.diag.3", "x.relay.2", "h.along.2",
    "ffn.1", "h.diag.3", "ffn.2", "x.diag.2", "x.share.3", "h.share.3", "h.relay.2", "ffn.3",
    "cr.3", "x.share.2", "h.diag.2", "ffn.4", "h.share.2", "ffn.5", "cr.2", "ffn.6",
    "ffn.7",
)


def move(place, source, target, sems, kind, rows=None):
    if rows is not None:
        source, target = source.at[rows], target.at[rows]

    @pl.when(place.stays)
    def _():
        here = pltpu.make_async_copy(source, target, sems[2])
        here.start() if kind == "start" else here.wait()

    @pl.when(jnp.logical_not(place.stays))
    def _():
        there = remote(source, target, sems[0], sems[1], place.partner)
        there.start() if kind == "start" else there.wait()


def head_masks(shape):
    lane = lax.broadcasted_iota(jnp.int32, shape, 1)
    return lane < HEAD_DIM, lane >= HEAD_DIM


def ones_lanes(rows, count):
    lane = lax.broadcasted_iota(jnp.int32, (rows, PAIR), 1)
    return jnp.where(lane < count, 1.0, 0.0).astype(BF)


def attend(queries, keys, values, o_ref, lse_ref):
    rows, length = queries.shape[0], keys.shape[0]
    values = jnp.concatenate([values, ones_lanes(length, 1)], axis=1)
    zero = jnp.zeros_like(queries)
    outs, sums = [], []
    both = [dot(jnp.where(mask, queries, zero), keys, 1, 1) for mask in head_masks(queries.shape)]
    for scores in both:
        top = jnp.max(scores, axis=1, keepdims=True)
        probs = jnp.exp2(scores - top).astype(BF)
        mixed = dot(probs, values, 1, 0)
        total = mixed[:, PAIR : PAIR + 1]
        outs.append(mixed[:, :PAIR] / total)
        sums.append(top + jnp.log2(total))
    first, _ = head_masks((rows, PAIR))
    o_ref[...] = jnp.where(first, outs[0], outs[1]).astype(BF)
    lse_ref[...] = jnp.where(first, sums[0], sums[1])


def front_kernel(
    n_dp, n_t, cap,
    choice_ref, count_ref, gain_ref, ed_tab, ou_tab, xd_tab, su_tab, eu_tab, od_tab, xu_tab, sd_tab,
    tokens_ref, cot_ref, w_ref, wo_ref, we_ref, ws_ref,
    o_ref, lse_ref, inner_t_ref, thin_out, rep_out,
    q_out, k_out, v_out, k_far_out, v_far_out, normed_out, tok_out, cot_out, w_full, wo_full, we_full, ws_full,
    we_land, ws_land,
    q, k, v, k_far, v_far, tok, cot, normed, thin, rep, thin_send, stage, inner,
    tok_sems, cot_sems, thin_sends, thin_recvs, rep_sems, stage_sems, kv_sends, kv_recvs, keep_sems, kept_sems,
    land_sems, go_sem, *sems,
):
    p = Place(n_dp, n_t, cap)
    step, steps = pl.program_id(0), pl.num_programs(0)
    cols, hid = od_tab.shape[-1], xu_tab.shape[-1]
    pairs = cols // PAIR
    depth = w_ref.shape[0] // 3
    early = list(range(n_t // 2))
    entry = Gather(p, {0: w_ref}, w_full, range(n_t), sems[0:3])
    out_g = Gather(p, {0: wo_ref}, wo_full, range(n_t), sems[3:6])
    exp_g = Gather(p, {0: we_ref}, we_full, early, sems[6:9])
    shr_g = Gather(p, {0: ws_ref}, ws_full, early, sems[9:12])
    both = (exp_g, shr_g)
    tok_three = [tok_sems.at[i] for i in range(3)]
    cot_three = [cot_sems.at[i] for i in range(3)]

    def thin_targets():
        for s in range(cap):
            for low in range(p.half):
                to = s * p.group + p.core * p.half + low
                for core in range(2):
                    i = (s * p.half + low) * 2 + core
                    elsewhere = jnp.logical_or(core != p.core, to != p.t)
                    yield s, to, core, i, elsewhere

    def send_thin(near):
        for s, to, core, i, elsewhere in thin_targets():
            d = (to + n_t - p.t) % n_t

            @pl.when(jnp.logical_and(elsewhere, (to == p.t) == near))
            def _():
                remote(
                    thin_send.at[s], thin.at[d], thin_sends.at[i], thin_recvs.at[d], (p.dp - p.core + core, to)
                ).start()

    def send_adapters():
        for s in range(cap):
            a = choice_ref[s]
            for i in range(3):
                thin_send[s, :, i * cols : (i + 1) * cols] = eu_tab[a, i]
            thin_send[s, :, 3 * cols : 4 * cols] = od_tab[a]
            thin_send[s, :, 4 * cols : 4 * cols + hid] = xu_tab[a]
            thin_send[s, :, 4 * cols + hid :] = sd_tab[a]
        send_thin(True)

        @pl.when(p.stays)
        def _():
            a = choice_ref[p.slot]
            for i, table in enumerate((ed_tab, ou_tab, xd_tab, su_tab)):
                rep[i * RANK : (i + 1) * RANK] = table[a]
            row = lax.broadcasted_iota(jnp.int32, (RANK, rep.shape[1]), 0)
            alive = jnp.where(p.slot < count_ref[0], 1.0, 0.0)
            rep[4 * RANK :] = jnp.where(row < RANK // 2, alive, a.astype(F32)).astype(BF)
            remote(rep, rep, rep_sems.at[0], rep_sems.at[1], p.sibling).start()
            thin[0] = thin_send[p.slot]

    def take_near():
        @pl.when(jnp.logical_not(p.stays))
        def _():
            remote(rep, rep, rep_sems.at[0], rep_sems.at[1], p.sibling).wait_recv()
            remote(thin_send.at[0], thin.at[0], thin_sends.at[0], thin_recvs.at[0], p.sibling).wait_recv()

        rep_out[...] = rep[...]
        thin_out[0] = thin[0]

    def take_thin(d):
        remote(thin_send.at[0], thin.at[d], thin_sends.at[0], thin_recvs.at[d], p.sibling).wait_recv()
        thin_out[d] = thin[d]

    def load(d):
        return pltpu.make_async_copy(w_full.at[d], stage.at[d % 2], stage_sems.at[d % 2])

    def kept():
        return [pltpu.make_async_copy(tok, tok_out, keep_sems.at[0]), pltpu.make_async_copy(normed, normed_out, keep_sems.at[1])]

    def first_norm():
        hat, _ = norm_parts(tok[...].astype(F32))
        value = (hat * gain_ref[...]).astype(BF)
        normed[...] = value
        down = rep[:RANK]
        inner[...] = dot(value, down, 1, 1).astype(BF)
        inner_t_ref[...] = dot(down, value, 1, 1).astype(BF)
        for copy in kept():
            copy.start()

    def far_copy(d, which, m):
        source, target = ((k, k_far), (v, v_far))[which]
        device = p.mate(m)
        there = (d + device[1] + n_t - p.t) % n_t
        return remote(
            source.at[pl.ds(d * pairs, pairs)], target.at[m - 1, pl.ds(there * pairs, pairs)],
            kv_sends.at[d, which, m - 1], kv_recvs.at[there, which, m - 1], device,
        )

    def far_arrival(d, which, m):
        source, target = ((k, k_far), (v, v_far))[which]
        return remote(
            source.at[pl.ds(d * pairs, pairs)], target.at[m - 1, pl.ds(d * pairs, pairs)],
            kv_sends.at[d, which, m - 1], kv_recvs.at[d, which, m - 1], p.mate(m),
        )

    def project(d):
        if d:
            take_thin(d)
        load(d).wait()
        for which, out in ((1, k), (2, v), (0, q)):
            weights = stage[d % 2, :, :, which * depth : (which + 1) * depth].reshape(n_dp * depth, cols)
            part = dot(normed[...], weights, 1, 0)
            part = part + dot(inner[...], thin[d, :, which * cols : (which + 1) * cols], 1, 0)
            if which == 0:
                part = part * (HEAD_DIM**-0.5 * LOG2E)
            part = part.astype(BF)
            for i in range(pairs):
                out[d * pairs + i] = part[:, i * PAIR : (i + 1) * PAIR]
            if which:
                for m in range(1, p.group):
                    far_copy(d, which - 1, m).start()

    def copies_out(d):
        at = pl.ds(d * pairs, pairs)
        found = [(a.at[at], b.at[at]) for a, b in ((q, q_out), (k, k_out), (v, v_out))]
        for a, b in ((k_far, k_far_out), (v_far, v_far_out)):
            found += [(a.at[m, at], b.at[m, at]) for m in range(p.group - 1)]
        return [pltpu.make_async_copy(a, b, kept_sems.at[d, i]) for i, (a, b) in enumerate(found)]

    def arrive(d):
        for m in range(1, p.group):
            far_arrival(d, 0, m).wait_recv()
            far_arrival(d, 1, m).wait_recv()
        for copy in copies_out(d):
            copy.start()

    def land(i):
        source, target = ((we_ref, we_land), (ws_ref, ws_land))[i]
        return remote(source, target, land_sems.at[0, i], land_sems.at[1, i], (p.dp, p.along(n_t - 1)))

    def ready(d):
        entry.done(d)
        load(d).start()

    def go():
        @pl.when(jnp.logical_not(p.stays))
        def _():
            pl.semaphore_signal(go_sem, inc=1, device_id=p.sibling, device_id_type=MESH)

        @pl.when(p.stays)
        def _():
            pl.semaphore_wait(go_sem, 1)

    def arrived():
        move(p, tokens_ref, tok, tok_three, "wait")
        send_thin(False)

    def norm():
        take_near()
        first_norm()

    def opened():
        greet(p.gather_peers() + p.other_core_peers())

    gathers = {"e": entry, "x": exp_g, "h": shr_g, "o": out_g}
    plain = {
        "greet": opened, "go": go, "wtok": arrived, "ln": norm,
        "tok": lambda: move(p, tokens_ref, tok, tok_three, "start"),
        "cot": lambda: move(p, cot_ref, cot, cot_three, "start"),
        "lx": lambda: land(0).start(), "lh": lambda: land(1).start(),
        "adapters": send_adapters,
    }
    counted = {"ready": ready, "proj": project, "arrive": arrive}

    def event(name):
        word = name.split(".")
        if len(word) == 1:
            return plain[name]
        if len(word) == 2:
            return lambda: counted[word[0]](int(word[1]))
        return lambda: getattr(gathers[word[0]], word[1])(int(word[2]))

    names = list(orders(n_t, pairs, max(1, hid // 512), p.group)[0])
    names.insert(names.index("e.diag.0"), "adapters")
    batches = [[event(name) for name in part] for part in cut(names, "attn")]
    closing = batches.pop()
    run_events(step, batches)
    keys = jnp.concatenate([k[step]] + [k_far[m, step] for m in range(p.group - 1)], axis=0)
    values = jnp.concatenate([v[step]] + [v_far[m, step] for m in range(p.group - 1)], axis=0)
    attend(q[step], keys, values, o_ref, lse_ref)

    @pl.when(step == steps - 1)
    def _():
        for call in closing:
            call()
        for g in (exp_g, shr_g, out_g):
            for d in g.ds:
                g.done(d)
        for g in (entry, exp_g, shr_g, out_g):
            g.finish()
        for i in range(2):
            land(i).wait()
        move(p, cot_ref, cot, cot_three, "wait")
        keep_cot = pltpu.make_async_copy(cot, cot_out, keep_sems.at[2])
        keep_cot.start()

        @pl.when(p.stays)
        def _():
            remote(rep, rep, rep_sems.at[0], rep_sems.at[1], p.sibling).wait_send()

        for s, to, core, i, elsewhere in thin_targets():

            @pl.when(elsewhere)
            def _():
                remote(thin_send.at[s], thin.at[0], thin_sends.at[i], thin_recvs.at[0], p.sibling).wait_send()

        for copy in [keep_cot, *kept()]:
            copy.wait()
        for d in range(n_t):
            for m in range(1, p.group):
                far_copy(d, 0, m).wait_send()
                far_copy(d, 1, m).wait_send()
            for copy in copies_out(d):
                copy.wait()


def front_part(cap, choice, count, gain, rep_tables, thin_tables, tokens, cot, w, wo, we, ws):
    n_dp, n_t = lax.axis_size("dp"), lax.axis_size("tensor")
    rows, width = tokens.shape
    cols = wo.shape[-1]
    others = n_t // cap - 1
    count_pairs = width // PAIR
    early = n_t // 2
    thin_width = 4 * cols + 2 * we.shape[-1]
    shape, vmem = jax.ShapeDtypeStruct, pltpu.VMEM
    whole = lambda *s: pl.BlockSpec(s, lambda h: (0,) * len(s))
    pair = pl.BlockSpec((None, rows, PAIR), lambda h: (h, 0, 0))
    full = lambda n, a: shape((n, n_dp // 2, 2, *a.shape), BF)
    heads, far = (count_pairs, rows, PAIR), (others, count_pairs, rows, PAIR)
    small = [(RANK, rows), (n_t, RANK, thin_width), (5 * RANK, width)]
    return pl.pallas_call(
        functools.partial(front_kernel, n_dp, n_t, cap),
        grid=(count_pairs,),
        in_specs=[IN_SMEM, IN_SMEM] + [whole(*a.shape) for a in (gain, *rep_tables, *thin_tables)]
        + [ANY] * 2 + [whole(*a.shape) for a in (w, wo, we, ws)],
        out_specs=[pair, pair] + [whole(*s) for s in small] + [ANY] * 14,
        out_shape=[shape(heads, BF), shape(heads, F32)] + [shape(s, BF) for s in small]
        + [shape(heads, BF)] * 3 + [shape(far, BF)] * 2 + [shape((rows, width), BF)] * 3
        + [full(n_t, w), full(n_t, wo), full(early, we), full(early, ws), shape(we.shape, BF), shape(ws.shape, BF)],
        scratch_shapes=[
            vmem(heads, BF), vmem(heads, BF), vmem(heads, BF), vmem(far, BF), vmem(far, BF),
            vmem((rows, width), BF), vmem((rows, width), BF), vmem((rows, width), BF), vmem(small[1], BF), vmem(small[2], BF),
            vmem((cap, RANK, thin_width), BF),
            vmem((2, n_dp // 2, 2, *w.shape), BF), vmem((rows, RANK), BF),
            DMA((3,)), DMA((3,)), DMA((n_t,)), DMA((n_t,)), DMA((2,)), DMA((2,)),
            DMA((n_t, 2, others)), DMA((n_t, 2, others)), DMA((3,)), DMA((n_t, 3 + 2 * others)), DMA((2, 2)),
            pltpu.SemaphoreType.REGULAR,
            *Gather.scratch(n_dp, range(n_t)), *Gather.scratch(n_dp, range(n_t)),
            *Gather.scratch(n_dp, range(early)), *Gather.scratch(n_dp, range(early)),
        ],
        compiler_params=params(collective_id=0, has_side_effects=True),
        name="front_part",
    )(choice, count, gain, *rep_tables, *thin_tables, tokens, cot, w, wo, we, ws)


def split_lanes(column):
    column = -column
    high = column.astype(BF)
    rest = column - high.astype(F32)
    mid = rest.astype(BF)
    low = (rest - mid.astype(F32)).astype(BF)
    lane = lax.broadcasted_iota(jnp.int32, (column.shape[0], PAIR), 1)
    zero = jnp.zeros((column.shape[0], PAIR), BF)
    return jnp.where(lane == 0, high, jnp.where(lane == 1, mid, jnp.where(lane == 2, low, zero)))


def back_kernel(
    n_dp, n_t, cap, tiles,
    q_ref, k_ref, k_far, v_ref, v_far, o_ref, lse_ref, do_ref, gain_ref, rep_ref, thin_ref, inner_t_ref, grads_ref,
    mixed_ref, w_ref, mgrad_ref, tok_ref, normed_ref,
    mixed_out, mid_full, tgrad_out, end_full,
    grad, send, far, mixed, weights, mgrad, tok, normed, back_low, tgrad, end, sends, recvs, swap, swaps, load_sems,
    *sems,
):
    p = Place(n_dp, n_t, cap)
    step, steps = pl.program_id(0), pl.num_programs(0)
    rows = q_ref.shape[0]
    pairs = grad.shape[1] // n_t
    cols = w_ref.shape[-1]
    depth = w_ref.shape[-2] // 3
    width = tok_ref.shape[1]
    mid_g = Gather(
        p, {0: grads_ref.at[0]}, mid_full, range(n_t), sems[0:3],
        spread=lambda d: grads_ref.at[n_t - d], by_rows=False,
    )
    end_g = Gather(
        p, {0: end.at[0]}, end_full, range(n_t), sems[3:6], spread=lambda d: end.at[n_t - d], by_rows=False
    )
    swap_sems = [swap.at[i] for i in range(3)]
    loads = [
        pltpu.make_async_copy(src, dst, load_sems.at[i])
        for i, (src, dst) in enumerate(((w_ref, weights), (normed_ref, normed), (tok_ref, tok), (mgrad_ref, mgrad)))
    ]
    relay, diag, share = ((lambda d, f=f: lambda: f(d)) for f in (mid_g.relay, mid_g.diag, mid_g.share))
    start_swap = lambda: move(p, mixed_ref, mixed, swap_sems, "start")
    start_loads = lambda: [copy.start() for copy in loads]

    def opening():
        greet(p.gather_peers() + p.other_core_peers())
        mid_g.relay(0)
        for d in range(1, n_t):
            mid_g.along(d)

    if n_t == 4:
        table = {
            0: [opening], 1: [diag(0), relay(1)], 2: [share(0), diag(1), relay(2), start_swap],
            3: [share(1), diag(2), relay(3)], 4: [share(2), diag(3), start_loads], 5: [share(3)],
        }
    else:
        table = {0: [opening, start_swap, start_loads, diag(0), share(0)]}
        for d in range(1, n_t):
            table[0] += [relay(d), diag(d), share(d)]
    run_events(step, [table.get(i, []) for i in range(max(table) + 1)])

    with_far = lambda near, far: jnp.concatenate([near[...]] + [far[m] for m in range(p.group - 1)], axis=0)
    keys = with_far(k_ref, k_far)
    length = keys.shape[0]
    ones = ones_lanes(length, 3)
    keys_more = jnp.concatenate([keys, ones], axis=1)
    values_more = jnp.concatenate([with_far(v_ref, v_far), ones], axis=1)
    queries, grad_out = q_ref[...], do_ref[...]
    zero = jnp.zeros_like(queries)
    product = grad_out.astype(F32) * o_ref[...].astype(F32)
    d_queries, d_keys, d_values = [], 0.0, 0.0
    for head, mask in enumerate(head_masks(queries.shape)):
        query = jnp.where(mask, queries, zero)
        grad_head = jnp.where(mask, grad_out, zero)
        lse = lse_ref[:, head * HEAD_DIM : head * HEAD_DIM + 1]
        delta = jnp.sum(jnp.where(mask, product, 0.0), axis=1, keepdims=True)
        probs = jnp.exp2(dot(jnp.concatenate([query, split_lanes(lse)], axis=1), keys_more, 1, 1))
        slope = dot(jnp.concatenate([grad_head, split_lanes(delta)], axis=1), values_more, 1, 1)
        score_grad = (probs * slope).astype(BF)
        d_queries.append(dot(score_grad, keys, 1, 0))
        d_values = d_values + dot(grad_head, probs.astype(BF), 0, 0)
        d_keys = d_keys + dot(query, score_grad, 0, 0)
    first, _ = head_masks((rows, PAIR))
    grad[0, step] = (jnp.where(first, d_queries[0], d_queries[1]) * HEAD_DIM**-0.5).astype(BF)
    d_keys = (d_keys * LN2).T.astype(BF)
    d_values = d_values.T.astype(BF)
    grad[1, step] = d_keys[:rows]
    grad[2, step] = d_values[:rows]

    def far_copy(i, m, h):
        device = p.mate(p.group - m)
        there = (h // pairs + device[1] + n_t - p.t) % n_t * pairs + h % pairs
        return remote(
            send.at[i, m - 1, h], far.at[i, m - 1, there], sends.at[i, m - 1, h], recvs.at[i, m - 1, there], device
        )

    for m in range(1, p.group):
        send[0, m - 1, step] = d_keys[m * rows : (m + 1) * rows]
        send[1, m - 1, step] = d_values[m * rows : (m + 1) * rows]
        far_copy(0, m, step).start()
        far_copy(1, m, step).start()

    @pl.when(step == steps - 1)
    def _():
        move(p, mixed_ref, mixed, swap_sems, "wait")
        keep = pltpu.make_async_copy(mixed, mixed_out, swap.at[3])
        keep.start()
        for i in range(2):
            for m in range(1, p.group):
                for h in range(n_t * pairs):
                    remote(
                        send.at[i, m - 1, h], far.at[i, m - 1, h], sends.at[i, m - 1, h], recvs.at[i, m - 1, h], p.sibling
                    ).wait_recv()
            for h in range(n_t * pairs):
                total = grad[1 + i, h].astype(F32)
                for m in range(p.group - 1):
                    total = total + far[i, m, h].astype(F32)
                grad[1 + i, h] = total.astype(BF)
        columns = lambda which, d, rows: jnp.concatenate(
            [grad[which, d * pairs + i, rows] for i in range(pairs)], axis=1
        )
        back = 0.0
        for d in range(n_t):
            for which in range(3):
                up = thin_ref[d, :, which * cols : (which + 1) * cols]
                back = back + dot(columns(which, d, slice(None)), up, 1, 1)
        back_low[...] = back.astype(BF)
        for copy in loads:
            copy.wait()

        def tile(n):
            start, count = tiles[n]
            rows = pl.ds(start, count)
            total = dot(back_low[rows], rep_ref[:RANK], 1, 0)
            for d in range(n_t):
                for which in range(3):
                    piece = weights[d, :, :, which * depth : (which + 1) * depth].reshape(width, cols)
                    total = total + dot(columns(which, d, rows), piece, 1, 1)
            hat, scale = norm_parts(tok[rows].astype(F32))
            tgrad[rows] = (mgrad[rows] + norm_back(hat, scale, gain_ref[...], total)).astype(BF)
            move(p, tgrad, tgrad_out, [swaps.at[n, i] for i in range(3)], "start", rows)

        tile(0)
        down_grad = dot(back_low[...], normed[...], 0, 0).astype(BF)
        for d in range(n_t):
            for which in range(3):
                end[d, :, which * cols : (which + 1) * cols] = dot(
                    inner_t_ref[...], columns(which, d, slice(None)), 1, 0
                ).astype(BF)
            end[d, :, 3 * cols :] = down_grad
        end_g.relay(0)
        for d in range(1, n_t):
            end_g.along(d)
        for n in range(1, len(tiles)):
            tile(n)
            if n == 1:
                end_g.diag(0)
        if len(tiles) == 1:
            end_g.diag(0)
        for d in range(1, n_t):
            end_g.relay(d)
            end_g.share(d - 1)
            end_g.diag(d)
        end_g.share(n_t - 1)
        for d in range(n_t):
            mid_g.done(d)
            end_g.done(d)
        mid_g.finish()
        end_g.finish()
        for n, (start, count) in enumerate(tiles):
            move(p, tgrad, tgrad_out, [swaps.at[n, i] for i in range(3)], "wait", pl.ds(start, count))

        @pl.loop(0, steps)
        def _(h):
            for m in range(1, p.group):
                for i in range(2):
                    far_copy(i, m, h).wait_send()

        keep.wait()


def back_part(cap, q, k, k_far, v, v_far, o, lse, do, gain, rep, thin, inner_t, grads, mixed, w_full, mgrad, tok, normed):
    n_dp, n_t = lax.axis_size("dp"), lax.axis_size("tensor")
    heads, rows, _ = q.shape
    width, cols = tok.shape[1], w_full.shape[-1]
    others = k_far.shape[0]
    pair = pl.BlockSpec((None, rows, PAIR), lambda h: (h, 0, 0))
    far = pl.BlockSpec((others, None, rows, PAIR), lambda h: (0, h, 0, 0))
    whole = lambda a: pl.BlockSpec(a.shape, lambda h: (0,) * len(a.shape))
    shape, vmem = jax.ShapeDtypeStruct, pltpu.VMEM
    count = (2, others, heads)
    number = 3 if rows % 16 == 0 else 1
    size = rows // number // 16 * 16 if number > 1 else rows
    tiles = [(0, rows - size * (number - 1))]
    tiles += [(tiles[0][1] + size * i, size) for i in range(number - 1)]
    end_width = 3 * cols + width
    full = lambda n: shape((n_t, n_dp // 2, 2, RANK, n), BF)
    return pl.pallas_call(
        functools.partial(back_kernel, n_dp, n_t, cap, tiles),
        grid=(heads,),
        in_specs=[pair, pair, far, pair, far, pair, pair, pair]
        + [whole(a) for a in (gain, rep, thin, inner_t, grads)] + [ANY] * 5,
        out_specs=[ANY] * 4,
        out_shape=[shape(mixed.shape, BF), full(grads.shape[-1]), shape(tok.shape, BF), full(end_width)],
        scratch_shapes=[
            vmem((3, heads, rows, PAIR), BF), vmem((2, *k_far.shape), BF), vmem((2, *k_far.shape), BF),
            vmem(mixed.shape, BF), vmem(w_full.shape, BF), vmem(mgrad.shape, F32), vmem(tok.shape, BF),
            vmem(tok.shape, BF), vmem((rows, RANK), BF), vmem(tok.shape, BF), vmem((n_t, RANK, end_width), BF),
            DMA(count), DMA(count), DMA((4,)), DMA((len(tiles), 3)), DMA((4,)),
            *Gather.scratch(n_dp, range(n_t)), *Gather.scratch(n_dp, range(n_t)),
        ],
        compiler_params=params(collective_id=1, has_side_effects=True),
        name="back_part",
    )(q, k, k_far, v, v_far, o, lse, do, gain, rep, thin, inner_t, grads, mixed, w_full, mgrad, tok, normed)


def gelu_parts(hidden):
    share = 0.5 * (1.0 + lax.erf(hidden * 0.7071067811865476))
    density = jnp.exp(-0.5 * hidden * hidden) * 0.3989422804014327
    return hidden * share, share + hidden * density


def middle_kernel(
    n_dp, n_t, cap, sub,
    x_ref, att_ref, cot_ref, gain_ref, rep_ref, thin_ref, wo_ref, we_near, ws_near, we_land, ws_land, we_ref, ws_ref,
    mixed_ref, mgrad_ref, agrad_ref, grads_ref, we_full, ws_full,
    middle_ref, second_ref, dy_ref, acc2_ref, acc3_ref, einner_ref, einner_t_ref, sback_ref, sback_t_ref,
    sinner_ref, eback_ref, oinner_ref, we_buf, ws_buf, buf_sems, *sems,
):
    p = Place(n_dp, n_t, cap)
    step, steps = pl.program_id(0), pl.num_programs(0)
    cols = wo_ref.shape[-1]
    width = x_ref.shape[1]
    hid = we_ref.shape[-1]
    size = hid // sub
    near = n_t // 2
    late = list(reversed(range(near, n_t)))
    exp_g = Gather(p, {n_t - 1: we_land}, we_full, late, sems[0:3], spread=lambda d: we_ref)
    shr_g = Gather(p, {n_t - 1: ws_land}, ws_full, late, sems[3:6], spread=lambda d: ws_ref)
    pairs = cols // PAIR
    both = (exp_g, shr_g)
    down_e, up_o, up_s = rep_ref[2 * RANK : 3 * RANK], rep_ref[RANK : 2 * RANK], rep_ref[3 * RANK : 4 * RANK]
    alive = rep_ref[4 * RANK : 4 * RANK + 1, 0:1].astype(F32)
    at_od, at_eu = 3 * width, 3 * width + cols
    at_sd, at_id = at_eu + hid, at_eu + 2 * hid

    def load(i):
        index, part = i // sub, i % sub
        at = pl.ds(part * size, size)
        pair = (we_near, ws_near) if index < near else (we_full, ws_full)
        index = index if index < near else index - near
        return [
            pltpu.make_async_copy(src.at[index, :, :, :, at], buf.at[i % 3], buf_sems.at[i % 3, j])
            for j, (src, buf) in enumerate(zip(pair, (we_buf, ws_buf)))
        ]

    gathers = {"x": exp_g, "h": shr_g}

    def bring(d):
        exp_g.done(d)
        shr_g.done(d)
        for i in range(sub):
            for copy in load((near + late.index(d)) * sub + i):
                copy.start()

    def event(name):
        word = name.split(".")
        if len(word) == 2:
            return lambda: bring(int(word[1]))
        return lambda: getattr(gathers[word[0]], word[1])(int(word[2]))

    names = orders(n_t, pairs, sub, p.group)[1]
    begun = names.index("pre")
    start = [event(name) for name in names[:begun]]
    opening, *after = [[event(name) for name in part] for part in cut(names[begun + 1 :], "ffn")]
    columns = lambda d: jnp.concatenate([att_ref[d * pairs + i] for i in range(pairs)], axis=1)

    @pl.when(step == 0)
    def _():
        greet(p.gather_peers())
        for call in start:
            call()
        for i in range(2):
            for copy in load(i):
                copy.start()
        branch, inner = 0.0, 0.0
        for d in range(n_t):
            att = columns(d)
            branch = branch + dot(att, wo_ref[d].reshape(width, cols), 1, 1)
            inner = inner + dot(att, thin_ref[d, :, 3 * cols : 4 * cols], 1, 1)
        inner = inner.astype(BF)
        oinner_ref[...] = inner
        middle = x_ref[...].astype(F32) + (branch + dot(inner, up_o, 1, 0))
        middle_ref[...] = middle
        hat, _ = norm_parts(middle)
        second = (hat * gain_ref[...]).astype(BF)
        second_ref[...] = second
        dy = (cot_ref[...].astype(F32) * alive).astype(BF)
        dy_ref[...] = dy
        einner_ref[...] = dot(second, down_e, 1, 1).astype(BF)
        einner_t_ref[...] = dot(down_e, second, 1, 1).astype(BF)
        sback_ref[...] = dot(dy, up_s, 1, 1).astype(BF)
        sback_t_ref[...] = dot(up_s, dy, 1, 1).astype(BF)
        acc2_ref[...] = jnp.zeros_like(acc2_ref)
        acc3_ref[...] = jnp.zeros_like(acc3_ref)
        sinner_ref[...] = jnp.zeros_like(sinner_ref)
        eback_ref[...] = jnp.zeros_like(eback_ref)

    run_events(step, [opening])
    for i in range(n_t * sub):

        @pl.when(step == i)
        def _():
            for copy in load(i):
                copy.wait()
            if i + 2 < near * sub:
                for copy in load(i + 2):
                    copy.start()

    buf = step % 3
    d, part = step // sub, step % sub
    d = jnp.where(d < near, d, n_t - 1 + near - d)
    we, ws = we_buf[buf].reshape(width, size), ws_buf[buf].reshape(width, size)
    at = pl.multiple_of(part * size, size)
    e_up = thin_ref[d, :, pl.ds(4 * cols + at, size)]
    s_down = thin_ref[d, :, pl.ds(4 * cols + hid + at, size)]
    hidden = dot(second_ref[...], we, 1, 0) + dot(einner_ref[...], e_up, 1, 0)
    value, slope = gelu_parts(hidden)
    act = value.astype(BF)
    acc2_ref[...] += dot(act, ws, 1, 1)
    sinner_ref[...] += dot(act, s_down, 1, 1)
    act_grad = dot(dy_ref[...], ws, 1, 0) + dot(sback_ref[...], s_down, 1, 0)
    hid_grad = (act_grad * slope).astype(BF)
    acc3_ref[...] += dot(hid_grad, we, 1, 1)
    eback_ref[...] += dot(hid_grad, e_up, 1, 1)
    grads_ref[d, :, pl.ds(at_eu + at, size)] = dot(einner_t_ref[...], hid_grad, 1, 0).astype(BF)
    grads_ref[d, :, pl.ds(at_sd + at, size)] = dot(sback_t_ref[...], act, 1, 0).astype(BF)

    run_events(step, after)
    @pl.when(step == steps - 1)
    def _():
        s_inner, e_back = sinner_ref[...].astype(BF), eback_ref[...].astype(BF)
        middle = middle_ref[...]
        mixed_ref[...] = (alive * (middle + (acc2_ref[...] + dot(s_inner, up_s, 1, 0)))).astype(BF)
        shrink_up = dot(s_inner, dy_ref[...], 0, 0).astype(BF)
        expand_down = dot(e_back, second_ref[...], 0, 0).astype(BF)
        second_grad = acc3_ref[...] + dot(e_back, down_e, 1, 0)
        hat, scale = norm_parts(middle)
        mgrad = cot_ref[...].astype(F32) * alive + norm_back(hat, scale, gain_ref[...], second_grad)
        mgrad_ref[...] = mgrad
        low = mgrad.astype(BF)
        o_back = dot(low, up_o, 1, 1).astype(BF)
        output_up = dot(oinner_ref[...], low, 0, 0).astype(BF)
        for d in range(n_t):
            agrad = dot(low, wo_ref[d].reshape(width, cols), 1, 0)
            agrad = (agrad + dot(o_back, thin_ref[d, :, 3 * cols : 4 * cols], 1, 0)).astype(BF)
            for i in range(pairs):
                agrad_ref[d * pairs + i] = agrad[:, i * PAIR : (i + 1) * PAIR]
            grads_ref[d, :, :width] = expand_down
            grads_ref[d, :, width : 2 * width] = shrink_up
            grads_ref[d, :, 2 * width : 3 * width] = output_up
            grads_ref[d, :, at_od : at_od + cols] = dot(o_back, columns(d), 0, 0).astype(BF)
            grads_ref[d, :, at_id:] = rep_ref[4 * RANK :, : grads_ref.shape[2] - at_id]
        for g in both:
            g.finish()


ID_LANES = 128


def middle_both_ways(cap, x, att, cot, gain, rep, thin, wo_full, we_near, ws_near, we_land, ws_land, we, ws):
    n_dp, n_t = lax.axis_size("dp"), lax.axis_size("tensor")
    rows, width = x.shape
    depth, hid = we.shape
    cols = wo_full.shape[-1]
    sub = max(1, hid // 512)
    size = hid // sub
    late = list(reversed(range(n_t // 2, n_t)))
    grad_width = 3 * width + cols + 2 * hid + ID_LANES
    whole = lambda a: pl.BlockSpec(a.shape, lambda i: (0,) * len(a.shape))
    shape = jax.ShapeDtypeStruct
    full = shape((len(late), n_dp // 2, 2, depth, hid), BF)
    outs = [
        shape((rows, width), BF), shape((rows, width), F32), shape(att.shape, BF),
        shape((n_t, RANK, grad_width), BF),
    ]
    vmem = pltpu.VMEM
    return pl.pallas_call(
        functools.partial(middle_kernel, n_dp, n_t, cap, sub),
        grid=(n_t * sub,),
        in_specs=[whole(a) for a in (x, att, cot, gain, rep, thin, wo_full)]
        + [ANY] * 2 + [whole(we_land), whole(ws_land)] + [ANY] * 2,
        out_specs=[whole(a) for a in outs] + [ANY] * 2,
        out_shape=outs + [full, full],
        scratch_shapes=[
            vmem((rows, width), F32), vmem((rows, width), BF), vmem((rows, width), BF),
            vmem((rows, width), F32), vmem((rows, width), F32),
            vmem((rows, RANK), BF), vmem((RANK, rows), BF), vmem((rows, RANK), BF), vmem((RANK, rows), BF),
            vmem((rows, RANK), F32), vmem((rows, RANK), F32), vmem((rows, RANK), BF),
            vmem((3, n_dp // 2, 2, depth, size), BF), vmem((3, n_dp // 2, 2, depth, size), BF), DMA((3, 2)),
            *Gather.scratch(n_dp, late, late[:1]), *Gather.scratch(n_dp, late, late[:1]),
        ],
        compiler_params=params(collective_id=2, has_side_effects=True),
        name="middle_both_ways",
    )(x, att, cot, gain, rep, thin, wo_full, we_near, ws_near, we_land, ws_land, we, ws)


def sum_kernel(
    width, cols, hid, mid_ref, end_ref, entry_down, entry_up, output_down, output_up, expand_down, expand_up,
    shrink_down, shrink_up,
):
    outs = (entry_down, entry_up, output_down, output_up, expand_down, expand_up, shrink_down, shrink_up)

    @pl.when(pl.program_id(0) == 0)
    def _():
        for out in outs:
            out[...] = jnp.zeros_like(out)

    sources = range(mid_ref.shape[0])
    at_id = 3 * width + cols + 2 * hid
    chosen = [jnp.max(mid_ref[i, RANK // 2 :, at_id : at_id + 128].astype(F32)).astype(jnp.int32) for i in sources]
    for i in sources:
        a = chosen[i]
        take = lambda ref, at, size: ref[i, :, at : at + size].astype(F32)
        expand_down[a] += take(mid_ref, 0, width)
        shrink_up[a] += take(mid_ref, width, width)
        output_up[a] += take(mid_ref, 2 * width, width)
        output_down[a] += take(mid_ref, 3 * width, cols)
        expand_up[a] += take(mid_ref, 3 * width + cols, hid)
        shrink_down[a] += take(mid_ref, 3 * width + cols + hid, hid)
        for which in range(3):
            entry_up[a, which] += take(end_ref, which * cols, cols)
        entry_down[a] += take(end_ref, 3 * cols, width)


def sum_gradients(adapters, cols, hid, width, mid, end):
    shape = jax.ShapeDtypeStruct
    wide = shape((adapters, RANK, width), F32)
    flat = lambda a: a.reshape(a.shape[0], -1, *a.shape[-2:])
    mid, end = flat(mid), flat(end)
    outs = [
        wide, shape((adapters, 3, RANK, cols), F32), shape((adapters, RANK, cols), F32), wide,
        wide, shape((adapters, RANK, hid), F32), shape((adapters, RANK, hid), F32), wide,
    ]
    part = lambda a: pl.BlockSpec((None, *a.shape[1:]), lambda i: (i, 0, 0, 0))
    return pl.pallas_call(
        functools.partial(sum_kernel, width, cols, hid),
        grid=(mid.shape[0],),
        in_specs=[part(mid), part(end)],
        out_specs=[pl.BlockSpec(a.shape, lambda i, n=len(a.shape): (0,) * n) for a in outs],
        out_shape=outs,
        compiler_params=params(),
        name="sum_gradients",
    )(mid, end)


def local(
    tokens, cotangent, norm_first, norm_second, entry_weight, output_weight, expand_weight, shrink_weight,
    entry_down, entry_up, output_down, output_up, expand_down, expand_up, shrink_down, shrink_up,
    adapter_choice, clip_count,
):
    cap = adapter_choice.shape[0]
    rows, width = tokens.shape
    adapters = entry_down.shape[0]
    cols, hid = output_weight.shape[1], expand_weight.shape[1]
    gain_first, gain_second = norm_first.reshape(1, width), norm_second.reshape(1, width)
    flip = lambda a: a.transpose(0, 2, 1)
    w_entry = entry_weight.transpose(1, 0, 2).reshape(-1, cols)
    (
        att, lse, inner_t, thin, rep, q, k, v, k_far, v_far, normed, tok, cot, w_full, wo_full, we_near, ws_near,
        we_land, ws_land,
    ) = front_part(
        cap, adapter_choice, clip_count, gain_first,
        (flip(entry_down), output_up, flip(expand_down), shrink_up),
        (entry_up.transpose(0, 2, 1, 3), flip(output_down), expand_up, flip(shrink_down)),
        tokens, cotangent, w_entry, output_weight, expand_weight, shrink_weight,
    )
    mixed, mgrad, agrad, grads, _, _ = middle_both_ways(
        cap, tok, att, cot, gain_second, rep, thin, wo_full, we_near, ws_near, we_land, ws_land,
        expand_weight, shrink_weight,
    )
    mixed, mid_grads, token_grad, end_grads = back_part(
        cap, q, k, k_far, v, v_far, att, lse, agrad, gain_first, rep, thin, inner_t, grads, mixed, w_full, mgrad, tok,
        normed,
    )
    ed, eu, od, ou, xd, xu, sd, su = sum_gradients(adapters, cols, hid, width, mid_grads, end_grads)
    return (
        mixed, token_grad, flip(ed), eu.transpose(0, 2, 1, 3), flip(od), ou, flip(xd), xu, flip(sd), su,
    )


def solution(mesh):
    in_specs = (
        P(BOTH, None), P(BOTH, None), P(), P(),
        P("dp", None, "tensor"), P("dp", "tensor"), P("dp", "tensor"), P("dp", "tensor"),
        P(), P(None, None, None, "tensor"), P(None, "tensor", None), P(),
        P(), P(None, None, "tensor"), P(None, "tensor", None), P(), P("dp"), P("dp"),
    )
    out_specs = (
        P(BOTH, None), P(BOTH, None), P(), P(None, None, None, "tensor"), P(None, "tensor", None), P(),
        P(), P(None, None, "tensor"), P(None, "tensor", None), P(),
    )
    return jax.shard_map(local, mesh=mesh, in_specs=in_specs, out_specs=out_specs, check_vma=False)
```

time: 373 us -> 303 us (0.81); the launches traced: 366 us -> 300 us
  Pallas kernels: 361 us -> 295 us
    pallas_call x5 -> x3, Pallas kernels: 267 us -> 225 us  [the longest x1 112 us: back_part(): pl.pallas_call(functools.partial(back_kernel, n_dp, n_t, cap, tiles), gri...]
    pallas_call x1, Pallas kernels: 94.1 us -> 70.2 us  [middle_both_ways(): pl.pallas_call(functools.partial(middle_kernel, n_dp, n_t, cap, sub), gri...]
where the time goes in v3:
time: 303 us; the launch traced here: 300 us
  Pallas kernels  295 us (97%)
  local copies, waits for them, and re-layouts  3.15 us (1%)
    pallas_call x1, Pallas kernels, back_part(): pl.pallas_call(functools.partial(back_kernel, n_dp, n_t, cap, tiles), gri...  112 us
    pallas_call x1, Pallas kernels, front_part(): pl.pallas_call(functools.partial(front_kernel, n_dp, n_t, cap), grid=(cou...  107 us
    pallas_call x1, Pallas kernels, middle_both_ways(): pl.pallas_call(functools.partial(middle_kernel, n_dp, n_t, cap, sub), gri...  70.2 us
    pallas_call x1, Pallas kernels, sum_gradients(): pl.pallas_call(functools.partial(sum_kernel, width, cols, hid), grid=(mid...  6.46 us

profile of v3, /device:TPU:0, one launch (start us, length us, event | category | flops | bytes accessed | tf_op | source)
XLA Modules:
  0.0 299.6 jit_solution(3687376205242589465)
XLA Ops:
  1.3 106.5 %front_part.1 = (bf16[8,784,128]{2,1,0:T(8,128)(2,1)}, f32[8,784,128]{2,1,0:T(8,128)}, bf16[16,784]{1,0:T(8,128)(2,1)}, bf16[4,16,3072]{2,1,0:T(8,128)(2,1)}, bf...) custom-call(s32[2]{0:T(128)} %choice_ref.1, ...), custom_call_target="tpu_custom_call" | custom-call | tf_op jit(solution)/shard_map/front_part/pallas_call | solution.py:566
  107.8 70.2 %middle_both_ways.1 = (bf16[784,1024]{1,0:T(8,128)(2,1)}, f32[784,1024]{1,0:T(8,128)}, bf16[8,784,128]{2,1,0:T(8,128)(2,1)}, bf16[4,16,5504]{2,1,0:T(8,128)(2,1)...) custom-call(bf16[784,1024]{1,0:T(8,128)(2,1)} %get-tuple-element.52.x_ref.tok_ref, ...), custom_call_target="tpu_custom_call" | custom-call | tf_op jit(solution)/shard_map/middle_both_ways/pallas_call | solution.py:976
  178.0 111.8 %back_part.1 = (bf16[784,1024]{1,0:T(8,128)(2,1)}, bf16[4,4,2,16,5504]{4,3,2,1,0:T(8,128)(2,1)}, bf16[784,1024]{1,0:T(8,128)(2,1)}, bf16[4,4,2,16,1792]{4,3,2,1,0:T(8,128)(2,1)}) custom-call(bf16[8,784,128]{2,1,0:T(8,128)(2,1)} %get-tuple-element.45.q_ref, bf16[8,784,128]{2,1,0:T(8,128)(2,1)} %get-tuple-element.46.k_ref, ...), custom_call_target="tpu_custom_call" | custom-call | tf_op jit(solution)/shard_map/back_part/pallas_call | solution.py:786
  289.8 0.0 copy-start.1
  289.8 6.5 %sum_gradients.1 = (f32[8,16,1024]{2,1,0:T(8,128)}, f32[8,3,16,256]{3,2,1,0:T(8,128)}, f32[8,16,256]{2,1,0:T(8,128)}, f32[8,16,1024]{2,1,0:T(8,128)}, f32[8,16,1...) custom-call(bf16[4,8,16,5504]{3,2,1,0:T(8,128)(2,1)} %bitcast.17, ...), custom_call_target="tpu_custom_call" | custom-call | tf_op jit(solution)/shard_map/sum_gradients/pallas_call | solution.py:1034
  296.3 0.0 copy-done.1
  296.3 0.0 copy-start
  296.3 1.2 copy.31
  297.5 0.8 copy-done
  298.3 1.2 copy.32
Async XLA Ops:
  289.8 6.5 %copy-start.1 = (bf16[784,1024]{1,0:T(8,128)(2,1)S(1)}, bf16[784,1024]{1,0:T(8,128)(2,1)}, u32[]{:S(2)}) copy-start(bf16[784,1024]{1,0:T(8,128)(2,1)} %get-tuple-element.90) | copy-start | bytes 4816900
  296.3 2.0 copy-start

commit v4 on v3

--- a/solution.py
+++ b/solution.py
@@ -212,10 +212,10 @@
                     event()
 
 
-def cut(names, word):
+def cut(names, letter):
     parts = [[]]
     for name in names:
-        if name.startswith(word):
+        if name[0] == letter:
             parts.append([])
         else:
             parts[-1].append(name)
@@ -227,67 +227,63 @@
         return FRONT, MIDDLE
     near = n_t // 2
     late = list(reversed(range(near, n_t)))
-    front = ["greet", "tok", "e.relay.0", "x.relay.0", "h.relay.0", "o.relay.0"]
+    name = lambda letters, d: letters + str(d)
+    front = ["G", "T", "er0", "xr0", "hr0", "or0", "A"]
     for d in range(1, n_t):
-        front += [f"e.along.{d}", f"o.along.{d}"] + ([f"x.along.{d}", f"h.along.{d}"] if d < near else [])
-    front += ["lx", "lh", "cot"]
-    every = lambda g, d: ([f"{g}.relay.{d}"] if d else []) + [f"{g}.diag.{d}", f"{g}.share.{d}"]
+        front += [name(g, d) for g in (("ea", "oa", "xa", "ha") if d < near else ("ea", "oa"))]
+    front += ["X", "H", "C"]
+    every = lambda g, d: [name(g + a, d) for a in ("rds" if d else "ds")]
     for d in range(n_t):
         front += every("e", d)
-    front += ["wtok", "go", "ln"]
+    front += ["W", "g", "N"]
     for d in range(n_t):
-        front += [f"ready.{d}", f"proj.{d}"]
+        front += [name("R", d), name("P", d)]
     for d in range(n_t):
         front += every("o", d) + (every("x", d) + every("h", d) if d < near else [])
     for d in range(n_t):
-        front += [f"arrive.{d}"] + [f"attn.{d * pairs + i}" for i in range(pairs)]
+        front += [name("V", d)] + [name("K", d * pairs + i) for i in range(pairs)]
     middle = []
     for g in "xh":
-        middle += [f"{g}.relay.{late[0]}"] + [f"{g}.along.{d}" for d in late[1:]]
-    middle += ["pre"]
+        middle += [name(g + "r", late[0])] + [name(g + "a", d) for d in late[1:]]
+    middle += ["I"]
     for i in range(n_t * sub):
-        middle += [f"ffn.{i}"]
+        middle += [name("F", i)]
         if i == 0:
             for d in late:
                 for g in "xh":
-                    middle += ([f"{g}.relay.{d}"] if d != late[0] else []) + [f"{g}.diag.{d}", f"{g}.share.{d}"]
+                    middle += every(g, d)[1 if d == late[0] else 0 :]
         if (i + 1) % sub == 0 and near <= (i + 1) // sub < n_t:
-            middle += [f"cr.{late[(i + 1) // sub - near]}"]
+            middle += [name("B", late[(i + 1) // sub - near])]
     return front, middle
 
 
 FRONT = (
-    "greet", "e.along.1", "h.relay.0", "e.relay.0", "x.relay.0", "tok", "e.diag.0", "e.along.2",
-    "h.diag.0", "e.share.0", "e.relay.1", "wtok", "e.diag.1", "x.diag.0", "e.along.3", "o.along.3",
-    "ln", "e.share.1", "o.relay.0", "o.along.2", "e.relay.2", "ready.0", "go", "x.along.1",
-    "proj.0", "h.along.1", "ready.1", "e.relay.3", "arrive.0", "o.diag.0", "attn.0", "o.along.1",
-    "x.share.0", "e.diag.2", "e.diag.3", "o.relay.2", "proj.1", "x.relay.1", "attn.1", "e.share.2",
-    "h.relay.1", "cot", "arrive.1", "attn.2", "h.share.0", "ready.2", "proj.2", "o.relay.1",
-    "e.share.3", "attn.3", "h.diag.1", "o.diag.2", "ready.3", "o.relay.3", "lx", "o.diag.1",
-    "proj.3", "arrive.2", "attn.4", "arrive.3", "o.share.0", "h.share.1", "o.diag.3", "o.share.2",
-    "x.diag.1", "attn.5", "o.share.1", "lh", "o.share.3", "attn.6", "x.share.1", "attn.7",
+    "G", "ea1", "hr0", "er0", "xr0", "T", "A", "ed0", "ea2", "hd0", "es0", "er1", "W", "ed1", "xd0", "ea3",
+    "oa3", "N", "es1", "or0", "oa2", "er2", "R0", "g", "xa1", "P0", "ha1", "R1", "er3", "V0", "od0", "K0",
+    "oa1", "xs0", "ed2", "ed3", "or2", "P1", "xr1", "K1", "es2", "hr1", "C", "V1", "K2", "hs0", "R2", "P2",
+    "or1", "es3", "K3", "hd1", "od2", "R3", "or3", "X", "od1", "P3", "V2", "K4", "V3", "os0", "hs1", "od3",
+    "os2", "xd1", "K5", "os1", "H", "os3", "K6", "xs1", "K7",
 )
 MIDDLE = (
-    "x.along.2", "x.relay.3", "pre", "h.relay.3", "ffn.0", "x.diag.3", "x.relay.2", "h.along.2",
-    "ffn.1", "h.diag.3", "ffn.2", "x.diag.2", "x.share.3", "h.share.3", "h.relay.2", "ffn.3",
-    "cr.3", "x.share.2", "h.diag.2", "ffn.4", "h.share.2", "ffn.5", "cr.2", "ffn.6",
-    "ffn.7",
+    "xa2", "xr3", "I", "hr3", "F0", "xd3", "xr2", "ha2", "F1", "hd3", "F2", "xd2", "xs3", "hs3", "hr2", "F3",
+    "B3", "xs2", "hd2", "F4", "hs2", "F5", "B2", "F6", "F7",
 )
-
-
-def move(place, source, target, sems, kind, rows=None):
+STEPS = {"a": Gather.along, "r": Gather.relay, "d": Gather.diag, "s": Gather.share}
+
+
+def move(place, source, target, sems, begin, rows=None):
     if rows is not None:
         source, target = source.at[rows], target.at[rows]
 
     @pl.when(place.stays)
     def _():
         here = pltpu.make_async_copy(source, target, sems[2])
-        here.start() if kind == "start" else here.wait()
+        here.start() if begin else here.wait()
 
     @pl.when(jnp.logical_not(place.stays))
     def _():
         there = remote(source, target, sems[0], sems[1], place.partner)
-        there.start() if kind == "start" else there.wait()
+        there.start() if begin else there.wait()
 
 
 def head_masks(shape):
@@ -477,7 +473,7 @@
             pl.semaphore_wait(go_sem, 1)
 
     def arrived():
-        move(p, tokens_ref, tok, tok_three, "wait")
+        move(p, tokens_ref, tok, tok_three, False)
         send_thin(False)
 
     def norm():
@@ -489,25 +485,21 @@
 
     gathers = {"e": entry, "x": exp_g, "h": shr_g, "o": out_g}
     plain = {
-        "greet": opened, "go": go, "wtok": arrived, "ln": norm,
-        "tok": lambda: move(p, tokens_ref, tok, tok_three, "start"),
-        "cot": lambda: move(p, cot_ref, cot, cot_three, "start"),
-        "lx": lambda: land(0).start(), "lh": lambda: land(1).start(),
-        "adapters": send_adapters,
+        "G": opened, "g": go, "W": arrived, "N": norm, "A": send_adapters,
+        "T": lambda: move(p, tokens_ref, tok, tok_three, True), "C": lambda: move(p, cot_ref, cot, cot_three, True),
+        "X": lambda: land(0).start(), "H": lambda: land(1).start(),
     }
-    counted = {"ready": ready, "proj": project, "arrive": arrive}
+    counted = {"R": ready, "P": project, "V": arrive}
 
     def event(name):
-        word = name.split(".")
-        if len(word) == 1:
+        if len(name) == 1:
             return plain[name]
-        if len(word) == 2:
-            return lambda: counted[word[0]](int(word[1]))
-        return lambda: getattr(gathers[word[0]], word[1])(int(word[2]))
-
-    names = list(orders(n_t, pairs, max(1, hid // 512), p.group)[0])
-    names.insert(names.index("e.diag.0"), "adapters")
-    batches = [[event(name) for name in part] for part in cut(names, "attn")]
+        if len(name) == 2:
+            return lambda: counted[name[0]](int(name[1]))
+        return lambda: STEPS[name[1]](gathers[name[0]], int(name[2]))
+
+    names = orders(n_t, pairs, max(1, hid // 512), p.group)[0]
+    batches = [[event(name) for name in part] for part in cut(names, "K")]
     closing = batches.pop()
     run_events(step, batches)
     keys = jnp.concatenate([k[step]] + [k_far[m, step] for m in range(p.group - 1)], axis=0)
@@ -525,7 +517,7 @@
             g.finish()
         for i in range(2):
             land(i).wait()
-        move(p, cot_ref, cot, cot_three, "wait")
+        move(p, cot_ref, cot, cot_three, False)
         keep_cot = pltpu.make_async_copy(cot, cot_out, keep_sems.at[2])
         keep_cot.start()
 
@@ -627,7 +619,7 @@
         for i, (src, dst) in enumerate(((w_ref, weights), (normed_ref, normed), (tok_ref, tok), (mgrad_ref, mgrad)))
     ]
     relay, diag, share = ((lambda d, f=f: lambda: f(d)) for f in (mid_g.relay, mid_g.diag, mid_g.share))
-    start_swap = lambda: move(p, mixed_ref, mixed, swap_sems, "start")
+    start_swap = lambda: move(p, mixed_ref, mixed, swap_sems, True)
     start_loads = lambda: [copy.start() for copy in loads]
 
     def opening():
@@ -656,7 +648,7 @@
     queries, grad_out = q_ref[...], do_ref[...]
     zero = jnp.zeros_like(queries)
     product = grad_out.astype(F32) * o_ref[...].astype(F32)
-    d_queries, d_keys, d_values = [], 0.0, 0.0
+    d_queries, both = [], [[], [], [], []]
     for head, mask in enumerate(head_masks(queries.shape)):
         query = jnp.where(mask, queries, zero)
         grad_head = jnp.where(mask, grad_out, zero)
@@ -666,8 +658,11 @@
         slope = dot(jnp.concatenate([grad_head, split_lanes(delta)], axis=1), values_more, 1, 1)
         score_grad = (probs * slope).astype(BF)
         d_queries.append(dot(score_grad, keys, 1, 0))
-        d_values = d_values + dot(grad_head, probs.astype(BF), 0, 0)
-        d_keys = d_keys + dot(query, score_grad, 0, 0)
+        for kept, one in zip(both, (grad_head, probs.astype(BF), query, score_grad)):
+            kept.append(one)
+    grad_heads, probs, query, score_grad = [jnp.concatenate(kept, axis=0) for kept in both]
+    d_values = dot(grad_heads, probs, 0, 0)
+    d_keys = dot(query, score_grad, 0, 0)
     first, _ = head_masks((rows, PAIR))
     grad[0, step] = (jnp.where(first, d_queries[0], d_queries[1]) * HEAD_DIM**-0.5).astype(BF)
     d_keys = (d_keys * LN2).T.astype(BF)
@@ -690,7 +685,7 @@
 
     @pl.when(step == steps - 1)
     def _():
-        move(p, mixed_ref, mixed, swap_sems, "wait")
+        move(p, mixed_ref, mixed, swap_sems, False)
         keep = pltpu.make_async_copy(mixed, mixed_out, swap.at[3])
         keep.start()
         for i in range(2):
@@ -713,7 +708,18 @@
                 up = thin_ref[d, :, which * cols : (which + 1) * cols]
                 back = back + dot(columns(which, d, slice(None)), up, 1, 1)
         back_low[...] = back.astype(BF)
-        for copy in loads:
+        loads[1].wait()
+        down_grad = dot(back_low[...], normed[...], 0, 0).astype(BF)
+        for d in range(n_t):
+            for which in range(3):
+                end[d, :, which * cols : (which + 1) * cols] = dot(
+                    inner_t_ref[...], columns(which, d, slice(None)), 1, 0
+                ).astype(BF)
+            end[d, :, 3 * cols :] = down_grad
+        end_g.relay(0)
+        for d in range(1, n_t):
+            end_g.along(d)
+        for copy in (loads[0], *loads[2:]):
             copy.wait()
 
         def tile(n):
@@ -726,29 +732,21 @@
                     total = total + dot(columns(which, d, rows), piece, 1, 1)
             hat, scale = norm_parts(tok[rows].astype(F32))
             tgrad[rows] = (mgrad[rows] + norm_back(hat, scale, gain_ref[...], total)).astype(BF)
-            move(p, tgrad, tgrad_out, [swaps.at[n, i] for i in range(3)], "start", rows)
-
-        tile(0)
-        down_grad = dot(back_low[...], normed[...], 0, 0).astype(BF)
-        for d in range(n_t):
-            for which in range(3):
-                end[d, :, which * cols : (which + 1) * cols] = dot(
-                    inner_t_ref[...], columns(which, d, slice(None)), 1, 0
-                ).astype(BF)
-            end[d, :, 3 * cols :] = down_grad
-        end_g.relay(0)
-        for d in range(1, n_t):
-            end_g.along(d)
-        for n in range(1, len(tiles)):
+            move(p, tgrad, tgrad_out, [swaps.at[n, i] for i in range(3)], True, rows)
+
+        for n in range(len(tiles)):
             tile(n)
-            if n == 1:
+            if n == 0:
                 end_g.diag(0)
-        if len(tiles) == 1:
-            end_g.diag(0)
-        for d in range(1, n_t):
-            end_g.relay(d)
+                end_g.relay(1)
+            if n == min(1, len(tiles) - 1):
+                for d in range(2, n_t):
+                    end_g.relay(d)
+                end_g.share(0)
+                end_g.diag(1)
+        for d in range(2, n_t):
+            end_g.diag(d)
             end_g.share(d - 1)
-            end_g.diag(d)
         end_g.share(n_t - 1)
         for d in range(n_t):
             mid_g.done(d)
@@ -756,7 +754,7 @@
         mid_g.finish()
         end_g.finish()
         for n, (start, count) in enumerate(tiles):
-            move(p, tgrad, tgrad_out, [swaps.at[n, i] for i in range(3)], "wait", pl.ds(start, count))
+            move(p, tgrad, tgrad_out, [swaps.at[n, i] for i in range(3)], False, pl.ds(start, count))
 
         @pl.loop(0, steps)
         def _(h):
@@ -852,15 +850,14 @@
                 copy.start()
 
     def event(name):
-        word = name.split(".")
-        if len(word) == 2:
-            return lambda: bring(int(word[1]))
-        return lambda: getattr(gathers[word[0]], word[1])(int(word[2]))
+        if len(name) == 2:
+            return lambda: bring(int(name[1]))
+        return lambda: STEPS[name[1]](gathers[name[0]], int(name[2]))
 
     names = orders(n_t, pairs, sub, p.group)[1]
-    begun = names.index("pre")
+    begun = names.index("I")
     start = [event(name) for name in names[:begun]]
-    opening, *after = [[event(name) for name in part] for part in cut(names[begun + 1 :], "ffn")]
+    opening, *after = [[event(name) for name in part] for part in cut(names[begun + 1 :], "F")]
     columns = lambda d: jnp.concatenate([att_ref[d * pairs + i] for i in range(pairs)], axis=1)
 
     @pl.when(step == 0)

time: 303 us -> 292 us (0.964)
  the two profiles are of different devices: /device:TPU:0 before, /device:TPU:17 now
where the time goes in v4:
time: 292 us; the launch traced here: 289 us
  Pallas kernels  284 us (97%)
  local copies, waits for them, and re-layouts  3.15 us (1%)
    pallas_call x1, Pallas kernels, back_part(): pl.pallas_call(functools.partial(back_kernel, n_dp, n_t, cap, tiles), gri...  104 us
    pallas_call x1, Pallas kernels, front_part(): pl.pallas_call(functools.partial(front_kernel, n_dp, n_t, cap), grid=(cou...  95 us
    pallas_call x1, Pallas kernels, middle_both_ways(): pl.pallas_call(functools.partial(middle_kernel, n_dp, n_t, cap, sub), gri...  78.9 us
    pallas_call x1, Pallas kernels, sum_gradients(): pl.pallas_call(functools.partial(sum_kernel, width, cols, hid), grid=(mid...  6.46 us

profile of v4, /device:TPU:17, one launch (start us, length us, event | category | flops | bytes accessed | tf_op | source)
XLA Modules:
  0.0 288.8 jit_solution(1240608917489162733)
XLA Ops:
  1.3 95.0 %front_part.1 = (bf16[8,784,128]{2,1,0:T(8,128)(2,1)}, f32[8,784,128]{2,1,0:T(8,128)}, bf16[16,784]{1,0:T(8,128)(2,1)}, bf16[4,16,3072]{2,1,0:T(8,128)(2,1)}, bf...) custom-call(s32[2]{0:T(128)} %choice_ref.1, ...), custom_call_target="tpu_custom_call" | custom-call | tf_op jit(solution)/shard_map/front_part/pallas_call | solution.py:558
  96.3 78.9 %middle_both_ways.1 = (bf16[784,1024]{1,0:T(8,128)(2,1)}, f32[784,1024]{1,0:T(8,128)}, bf16[8,784,128]{2,1,0:T(8,128)(2,1)}, bf16[4,16,5504]{2,1,0:T(8,128)(2,1)...) custom-call(bf16[784,1024]{1,0:T(8,128)(2,1)} %get-tuple-element.52.x_ref.tok_ref, ...), custom_call_target="tpu_custom_call" | custom-call | tf_op jit(solution)/shard_map/middle_both_ways/pallas_call | solution.py:973
  175.2 103.8 %back_part.1 = (bf16[784,1024]{1,0:T(8,128)(2,1)}, bf16[4,4,2,16,5504]{4,3,2,1,0:T(8,128)(2,1)}, bf16[784,1024]{1,0:T(8,128)(2,1)}, bf16[4,4,2,16,1792]{4,3,2,1,0:T(8,128)(2,1)}) custom-call(bf16[8,784,128]{2,1,0:T(8,128)(2,1)} %get-tuple-element.45.q_ref, bf16[8,784,128]{2,1,0:T(8,128)(2,1)} %get-tuple-element.46.k_ref, ...), custom_call_target="tpu_custom_call" | custom-call | tf_op jit(solution)/shard_map/back_part/pallas_call | solution.py:784
  279.0 0.0 copy-start.1
  279.0 6.5 %sum_gradients.1 = (f32[8,16,1024]{2,1,0:T(8,128)}, f32[8,3,16,256]{3,2,1,0:T(8,128)}, f32[8,16,256]{2,1,0:T(8,128)}, f32[8,16,1024]{2,1,0:T(8,128)}, f32[8,16,1...) custom-call(bf16[4,8,16,5504]{3,2,1,0:T(8,128)(2,1)} %bitcast.17, ...), custom_call_target="tpu_custom_call" | custom-call | tf_op jit(solution)/shard_map/sum_gradients/pallas_call | solution.py:1031
  285.5 0.0 copy-done.1
  285.5 0.0 copy-start
  285.5 1.2 copy.31
  286.6 0.8 copy-done
  287.5 1.2 copy.32
Async XLA Ops:
  279.0 6.5 %copy-start.1 = (bf16[784,1024]{1,0:T(8,128)(2,1)S(1)}, bf16[784,1024]{1,0:T(8,128)(2,1)}, u32[]{:S(2)}) copy-start(bf16[784,1024]{1,0:T(8,128)(2,1)} %get-tuple-element.90) | copy-start | bytes 4816900
  285.5 2.0 copy-start

commit v5 on v4

--- a/solution.py
+++ b/solution.py
@@ -425,8 +425,6 @@
         )
 
     def project(d):
-        if d:
-            take_thin(d)
         load(d).wait()
         for which, out in ((1, k), (2, v), (0, q)):
             weights = stage[d % 2, :, :, which * depth : (which + 1) * depth].reshape(n_dp * depth, cols)
@@ -460,6 +458,8 @@
         return remote(source, target, land_sems.at[0, i], land_sems.at[1, i], (p.dp, p.along(n_t - 1)))
 
     def ready(d):
+        if d:
+            take_thin(d)
         entry.done(d)
         load(d).start()
 
@@ -499,9 +499,27 @@
         return lambda: STEPS[name[1]](gathers[name[0]], int(name[2]))
 
     names = orders(n_t, pairs, max(1, hid // 512), p.group)[0]
-    batches = [[event(name) for name in part] for part in cut(names, "K")]
-    closing = batches.pop()
-    run_events(step, batches)
+    parts = cut(names, "K")
+    closing = [event(name) for name in parts.pop()]
+    first = ["P0" in part or sum(name[0] == "P" for name in part) > 1 for part in parts]
+    single = {}
+    before, after = [], []
+    for i, part in enumerate(parts):
+        places = [] if first[i] else [j for j, name in enumerate(part) if name[0] == "P"]
+        at = places[0] if places else len(part)
+        if places:
+            single[i] = int(part[at][1])
+        before.append([event(name) for name in part[:at]])
+        after.append([event(name) for name in part[at + 1 :]])
+    run_events(step, before)
+    if single:
+        chunk = sum(jnp.where(step == i, d, 0) for i, d in single.items())
+
+        @pl.when(chunk > 0)
+        def _():
+            project(chunk)
+
+    run_events(step, after)
     keys = jnp.concatenate([k[step]] + [k_far[m, step] for m in range(p.group - 1)], axis=0)
     values = jnp.concatenate([v[step]] + [v_far[m, step] for m in range(p.group - 1)], axis=0)
     attend(q[step], keys, values, o_ref, lse_ref)
@@ -596,7 +614,7 @@
     q_ref, k_ref, k_far, v_ref, v_far, o_ref, lse_ref, do_ref, gain_ref, rep_ref, thin_ref, inner_t_ref, grads_ref,
     mixed_ref, w_ref, mgrad_ref, tok_ref, normed_ref,
     mixed_out, mid_full, tgrad_out, end_full,
-    grad, send, far, mixed, weights, mgrad, tok, normed, back_low, tgrad, end, sends, recvs, swap, swaps, load_sems,
+    grad, send, far, mixed, weights, mgrad, tok, normed, back_sum, row_sum, back_low, tgrad, end, sends, recvs, swap, swaps, load_sems,
     *sems,
 ):
     p = Place(n_dp, n_t, cap)
@@ -694,27 +712,31 @@
                     remote(
                         send.at[i, m - 1, h], far.at[i, m - 1, h], sends.at[i, m - 1, h], recvs.at[i, m - 1, h], p.sibling
                     ).wait_recv()
-            for h in range(n_t * pairs):
+
+            @pl.loop(0, steps)
+            def _(h):
                 total = grad[1 + i, h].astype(F32)
                 for m in range(p.group - 1):
                     total = total + far[i, m, h].astype(F32)
                 grad[1 + i, h] = total.astype(BF)
+
         columns = lambda which, d, rows: jnp.concatenate(
             [grad[which, d * pairs + i, rows] for i in range(pairs)], axis=1
         )
-        back = 0.0
-        for d in range(n_t):
-            for which in range(3):
-                up = thin_ref[d, :, which * cols : (which + 1) * cols]
-                back = back + dot(columns(which, d, slice(None)), up, 1, 1)
-        back_low[...] = back.astype(BF)
+        chunks = n_t * 3
+        back_sum[...] = jnp.zeros_like(back_sum)
+
+        @pl.loop(0, chunks)
+        def _(j):
+            d, at = j // 3, pl.ds(pl.multiple_of(j % 3 * cols, cols), cols)
+            part = columns(j % 3, d, slice(None))
+            back_sum[...] += dot(part, thin_ref[d, :, at], 1, 1)
+            end[d, :, at] = dot(inner_t_ref[...], part, 1, 0).astype(BF)
+
+        back_low[...] = back_sum[...].astype(BF)
         loads[1].wait()
         down_grad = dot(back_low[...], normed[...], 0, 0).astype(BF)
         for d in range(n_t):
-            for which in range(3):
-                end[d, :, which * cols : (which + 1) * cols] = dot(
-                    inner_t_ref[...], columns(which, d, slice(None)), 1, 0
-                ).astype(BF)
             end[d, :, 3 * cols :] = down_grad
         end_g.relay(0)
         for d in range(1, n_t):
@@ -725,11 +747,16 @@
         def tile(n):
             start, count = tiles[n]
             rows = pl.ds(start, count)
-            total = dot(back_low[rows], rep_ref[:RANK], 1, 0)
-            for d in range(n_t):
-                for which in range(3):
-                    piece = weights[d, :, :, which * depth : (which + 1) * depth].reshape(width, cols)
-                    total = total + dot(columns(which, d, rows), piece, 1, 1)
+            acc = row_sum.at[pl.ds(0, count)]
+            acc[...] = dot(back_low[rows], rep_ref[:RANK], 1, 0)
+
+            @pl.loop(0, chunks)
+            def _(j):
+                at = pl.ds(pl.multiple_of(j % 3 * depth, depth), depth)
+                piece = weights[j // 3, :, :, at].reshape(width, cols)
+                acc[...] += dot(columns(j % 3, j // 3, rows), piece, 1, 1)
+
+            total = acc[...]
             hat, scale = norm_parts(tok[rows].astype(F32))
             tgrad[rows] = (mgrad[rows] + norm_back(hat, scale, gain_ref[...], total)).astype(BF)
             move(p, tgrad, tgrad_out, [swaps.at[n, i] for i in range(3)], True, rows)
@@ -791,7 +818,8 @@
         scratch_shapes=[
             vmem((3, heads, rows, PAIR), BF), vmem((2, *k_far.shape), BF), vmem((2, *k_far.shape), BF),
             vmem(mixed.shape, BF), vmem(w_full.shape, BF), vmem(mgrad.shape, F32), vmem(tok.shape, BF),
-            vmem(tok.shape, BF), vmem((rows, RANK), BF), vmem(tok.shape, BF), vmem((n_t, RANK, end_width), BF),
+            vmem(tok.shape, BF), vmem((rows, RANK), F32), vmem((tiles[0][1], width), F32), vmem((rows, RANK), BF),
+            vmem(tok.shape, BF), vmem((n_t, RANK, end_width), BF),
             DMA(count), DMA(count), DMA((4,)), DMA((len(tiles), 3)), DMA((4,)),
             *Gather.scratch(n_dp, range(n_t)), *Gather.scratch(n_dp, range(n_t)),
         ],

time: 292 us -> 278 us (0.952)
  the two profiles are of different devices: /device:TPU:17 before, /device:TPU:0 now
where the time goes in v5:
time: 278 us; the launch traced here: 276 us
  Pallas kernels  271 us (97%)
  local copies, waits for them, and re-layouts  3.15 us (1%)
    pallas_call x1, Pallas kernels, front_part(): pl.pallas_call(functools.partial(front_kernel, n_dp, n_t, cap), grid=(cou...  107 us
    pallas_call x1, Pallas kernels, back_part(): pl.pallas_call(functools.partial(back_kernel, n_dp, n_t, cap, tiles), gri...  88 us
    pallas_call x1, Pallas kernels, middle_both_ways(): pl.pallas_call(functools.partial(middle_kernel, n_dp, n_t, cap, sub), gri...  70.2 us
    pallas_call x1, Pallas kernels, sum_gradients(): pl.pallas_call(functools.partial(sum_kernel, width, cols, hid), grid=(mid...  6.46 us

profile of v5, /device:TPU:0, one launch (start us, length us, event | category | flops | bytes accessed | tf_op | source)
XLA Modules:
  0.0 275.8 jit_solution(12678654446713466247)
XLA Ops:
  1.3 106.7 %front_part.1 = (bf16[8,784,128]{2,1,0:T(8,128)(2,1)}, f32[8,784,128]{2,1,0:T(8,128)}, bf16[16,784]{1,0:T(8,128)(2,1)}, bf16[4,16,3072]{2,1,0:T(8,128)(2,1)}, bf...) custom-call(s32[2]{0:T(128)} %choice_ref.1, ...), custom_call_target="tpu_custom_call" | custom-call | tf_op jit(solution)/shard_map/front_part/pallas_call | solution.py:576
  108.0 70.2 %middle_both_ways.1 = (bf16[784,1024]{1,0:T(8,128)(2,1)}, f32[784,1024]{1,0:T(8,128)}, bf16[8,784,128]{2,1,0:T(8,128)(2,1)}, bf16[4,16,5504]{2,1,0:T(8,128)(2,1)...) custom-call(bf16[784,1024]{1,0:T(8,128)(2,1)} %get-tuple-element.52.x_ref.tok_ref, ...), custom_call_target="tpu_custom_call" | custom-call | tf_op jit(solution)/shard_map/middle_both_ways/pallas_call | solution.py:1001
  178.2 88.0 %back_part.1 = (bf16[784,1024]{1,0:T(8,128)(2,1)}, bf16[4,4,2,16,5504]{4,3,2,1,0:T(8,128)(2,1)}, bf16[784,1024]{1,0:T(8,128)(2,1)}, bf16[4,4,2,16,1792]{4,3,2,1,0:T(8,128)(2,1)}) custom-call(bf16[8,784,128]{2,1,0:T(8,128)(2,1)} %get-tuple-element.45.q_ref, bf16[8,784,128]{2,1,0:T(8,128)(2,1)} %get-tuple-element.46.k_ref, ...), custom_call_target="tpu_custom_call" | custom-call | tf_op jit(solution)/shard_map/back_part/pallas_call | solution.py:811
  266.2 0.0 copy-start.1
  266.2 6.5 %sum_gradients.1 = (f32[8,16,1024]{2,1,0:T(8,128)}, f32[8,3,16,256]{3,2,1,0:T(8,128)}, f32[8,16,256]{2,1,0:T(8,128)}, f32[8,16,1024]{2,1,0:T(8,128)}, f32[8,16,1...) custom-call(bf16[4,8,16,5504]{3,2,1,0:T(8,128)(2,1)} %bitcast.17, ...), custom_call_target="tpu_custom_call" | custom-call | tf_op jit(solution)/shard_map/sum_gradients/pallas_call | solution.py:1059
  272.6 0.0 copy-done.1
  272.6 0.0 copy-start
  272.6 1.2 copy.31
  273.8 0.8 copy-done
  274.6 1.2 copy.32
Async XLA Ops:
  266.2 6.5 %copy-start.1 = (bf16[784,1024]{1,0:T(8,128)(2,1)S(1)}, bf16[784,1024]{1,0:T(8,128)(2,1)}, u32[]{:S(2)}) copy-start(bf16[784,1024]{1,0:T(8,128)(2,1)} %get-tuple-element.90) | copy-start | bytes 4816900
  272.6 2.0 copy-start

commit v6 on v5

--- a/solution.py
+++ b/solution.py
@@ -258,8 +258,8 @@
 
 
 FRONT = (
-    "G", "ea1", "hr0", "er0", "xr0", "T", "A", "ed0", "ea2", "hd0", "es0", "er1", "W", "ed1", "xd0", "ea3",
-    "oa3", "N", "es1", "or0", "oa2", "er2", "R0", "g", "xa1", "P0", "ha1", "R1", "er3", "V0", "od0", "K0",
+    "G", "ea1", "hr0", "er0", "xr0", "T", "A", "ed0", "ea2", "ea3", "hd0", "es0", "er1", "W", "g", "ed1",
+    "xd0", "oa3", "N", "es1", "or0", "oa2", "er2", "R0", "xa1", "P0", "ha1", "R1", "er3", "V0", "od0", "K0",
     "oa1", "xs0", "ed2", "ed3", "or2", "P1", "xr1", "K1", "es2", "hr1", "C", "V1", "K2", "hs0", "R2", "P2",
     "or1", "es3", "K3", "hd1", "od2", "R3", "or3", "X", "od1", "P3", "V2", "K4", "V3", "os0", "hs1", "od3",
     "os2", "xd1", "K5", "os1", "H", "os3", "K6", "xs1", "K7",

time: 278 us -> 268 us (0.964)
  Pallas kernels: 271 us -> 260 us
    pallas_call x1, Pallas kernels: 107 us -> 98.3 us  [front_part(): pl.pallas_call(functools.partial(front_kernel, n_dp, n_t, cap), grid=(cou...]
where the time goes in v6:
time: 268 us; the launch traced here: 265 us
  Pallas kernels  260 us (97%)
  local copies, waits for them, and re-layouts  3.15 us (1%)
    pallas_call x1, Pallas kernels, front_part(): pl.pallas_call(functools.partial(front_kernel, n_dp, n_t, cap), grid=(cou...  98.3 us
    pallas_call x1, Pallas kernels, back_part(): pl.pallas_call(functools.partial(back_kernel, n_dp, n_t, cap, tiles), gri...  87.8 us
    pallas_call x1, Pallas kernels, middle_both_ways(): pl.pallas_call(functools.partial(middle_kernel, n_dp, n_t, cap, sub), gri...  67.7 us
    pallas_call x1, Pallas kernels, sum_gradients(): pl.pallas_call(functools.partial(sum_kernel, width, cols, hid), grid=(mid...  6.46 us

profile of v6, /device:TPU:0, one launch (start us, length us, event | category | flops | bytes accessed | tf_op | source)
XLA Modules:
  0.0 264.8 jit_solution(3829596805539875996)
XLA Ops:
  1.3 98.3 %front_part.1 = (bf16[8,784,128]{2,1,0:T(8,128)(2,1)}, f32[8,784,128]{2,1,0:T(8,128)}, bf16[16,784]{1,0:T(8,128)(2,1)}, bf16[4,16,3072]{2,1,0:T(8,128)(2,1)}, bf...) custom-call(s32[2]{0:T(128)} %choice_ref.1, ...), custom_call_target="tpu_custom_call" | custom-call | tf_op jit(solution)/shard_map/front_part/pallas_call | solution.py:576
  99.6 67.7 %middle_both_ways.1 = (bf16[784,1024]{1,0:T(8,128)(2,1)}, f32[784,1024]{1,0:T(8,128)}, bf16[8,784,128]{2,1,0:T(8,128)(2,1)}, bf16[4,16,5504]{2,1,0:T(8,128)(2,1)...) custom-call(bf16[784,1024]{1,0:T(8,128)(2,1)} %get-tuple-element.52.x_ref.tok_ref, ...), custom_call_target="tpu_custom_call" | custom-call | tf_op jit(solution)/shard_map/middle_both_ways/pallas_call | solution.py:1001
  167.4 87.8 %back_part.1 = (bf16[784,1024]{1,0:T(8,128)(2,1)}, bf16[4,4,2,16,5504]{4,3,2,1,0:T(8,128)(2,1)}, bf16[784,1024]{1,0:T(8,128)(2,1)}, bf16[4,4,2,16,1792]{4,3,2,1,0:T(8,128)(2,1)}) custom-call(bf16[8,784,128]{2,1,0:T(8,128)(2,1)} %get-tuple-element.45.q_ref, bf16[8,784,128]{2,1,0:T(8,128)(2,1)} %get-tuple-element.46.k_ref, ...), custom_call_target="tpu_custom_call" | custom-call | tf_op jit(solution)/shard_map/back_part/pallas_call | solution.py:811
  255.2 0.0 copy-start.1
  255.2 6.5 %sum_gradients.1 = (f32[8,16,1024]{2,1,0:T(8,128)}, f32[8,3,16,256]{3,2,1,0:T(8,128)}, f32[8,16,256]{2,1,0:T(8,128)}, f32[8,16,1024]{2,1,0:T(8,128)}, f32[8,16,1...) custom-call(bf16[4,8,16,5504]{3,2,1,0:T(8,128)(2,1)} %bitcast.17, ...), custom_call_target="tpu_custom_call" | custom-call | tf_op jit(solution)/shard_map/sum_gradients/pallas_call | solution.py:1059
  261.7 0.0 copy-done.1
  261.7 0.0 copy-start
  261.7 1.2 copy.31
  262.8 0.8 copy-done
  263.7 1.2 copy.32
Async XLA Ops:
  255.2 6.5 %copy-start.1 = (bf16[784,1024]{1,0:T(8,128)(2,1)S(1)}, bf16[784,1024]{1,0:T(8,128)(2,1)}, u32[]{:S(2)}) copy-start(bf16[784,1024]{1,0:T(8,128)(2,1)} %get-tuple-element.90) | copy-start | bytes 4816900
  261.7 2.0 copy-start

commit v7 on v6

--- a/solution.py
+++ b/solution.py
@@ -836,10 +836,11 @@
 
 def middle_kernel(
     n_dp, n_t, cap, sub,
-    x_ref, att_ref, cot_ref, gain_ref, rep_ref, thin_ref, wo_ref, we_near, ws_near, we_land, ws_land, we_ref, ws_ref,
-    mixed_ref, mgrad_ref, agrad_ref, grads_ref, we_full, ws_full,
+    x_in, att_in, cot_in, gain_ref, rep_ref, thin_ref, wo_in, we_near, ws_near, we_land, ws_land, we_ref, ws_ref,
+    mixed_out, mgrad_out, agrad_out, grads_ref, we_full, ws_full,
     middle_ref, second_ref, dy_ref, acc2_ref, acc3_ref, einner_ref, einner_t_ref, sback_ref, sback_t_ref,
-    sinner_ref, eback_ref, oinner_ref, we_buf, ws_buf, buf_sems, *sems,
+    sinner_ref, eback_ref, oinner_ref, we_buf, ws_buf, x_ref, att_ref, cot_ref, wo_ref, mixed_ref, mgrad_ref, agrad_ref,
+    buf_sems, in_sems, out_sems, *sems,
 ):
     p = Place(n_dp, n_t, cap)
     step, steps = pl.program_id(0), pl.num_programs(0)
@@ -868,6 +869,14 @@
             for j, (src, buf) in enumerate(zip(pair, (we_buf, ws_buf)))
         ]
 
+    inputs = [
+        pltpu.make_async_copy(src, dst, in_sems.at[i])
+        for i, (src, dst) in enumerate(((att_in, att_ref), (wo_in, wo_ref), (x_in, x_ref), (cot_in, cot_ref)))
+    ]
+    outputs = [
+        pltpu.make_async_copy(src, dst, out_sems.at[i])
+        for i, (src, dst) in enumerate(((mixed_ref, mixed_out), (mgrad_ref, mgrad_out), (agrad_ref, agrad_out)))
+    ]
     gathers = {"x": exp_g, "h": shr_g}
 
     def bring(d):
@@ -890,12 +899,16 @@
 
     @pl.when(step == 0)
     def _():
+        for copy in inputs:
+            copy.start()
+        for i in range(2):
+            for copy in load(i):
+                copy.start()
         greet(p.gather_peers())
         for call in start:
             call()
-        for i in range(2):
-            for copy in load(i):
-                copy.start()
+        for copy in inputs:
+            copy.wait()
         branch, inner = 0.0, 0.0
         for d in range(n_t):
             att = columns(d)
@@ -955,12 +968,14 @@
         s_inner, e_back = sinner_ref[...].astype(BF), eback_ref[...].astype(BF)
         middle = middle_ref[...]
         mixed_ref[...] = (alive * (middle + (acc2_ref[...] + dot(s_inner, up_s, 1, 0)))).astype(BF)
+        outputs[0].start()
         shrink_up = dot(s_inner, dy_ref[...], 0, 0).astype(BF)
         expand_down = dot(e_back, second_ref[...], 0, 0).astype(BF)
         second_grad = acc3_ref[...] + dot(e_back, down_e, 1, 0)
         hat, scale = norm_parts(middle)
         mgrad = cot_ref[...].astype(F32) * alive + norm_back(hat, scale, gain_ref[...], second_grad)
         mgrad_ref[...] = mgrad
+        outputs[1].start()
         low = mgrad.astype(BF)
         o_back = dot(low, up_o, 1, 1).astype(BF)
         output_up = dot(oinner_ref[...], low, 0, 0).astype(BF)
@@ -969,6 +984,8 @@
             agrad = (agrad + dot(o_back, thin_ref[d, :, 3 * cols : 4 * cols], 1, 0)).astype(BF)
             for i in range(pairs):
                 agrad_ref[d * pairs + i] = agrad[:, i * PAIR : (i + 1) * PAIR]
+        outputs[2].start()
+        for d in range(n_t):
             grads_ref[d, :, :width] = expand_down
             grads_ref[d, :, width : 2 * width] = shrink_up
             grads_ref[d, :, 2 * width : 3 * width] = output_up
@@ -976,6 +993,8 @@
             grads_ref[d, :, at_id:] = rep_ref[4 * RANK :, : grads_ref.shape[2] - at_id]
         for g in both:
             g.finish()
+        for copy in outputs:
+            copy.wait()
 
 
 ID_LANES = 128
@@ -1001,16 +1020,18 @@
     return pl.pallas_call(
         functools.partial(middle_kernel, n_dp, n_t, cap, sub),
         grid=(n_t * sub,),
-        in_specs=[whole(a) for a in (x, att, cot, gain, rep, thin, wo_full)]
-        + [ANY] * 2 + [whole(we_land), whole(ws_land)] + [ANY] * 2,
-        out_specs=[whole(a) for a in outs] + [ANY] * 2,
+        in_specs=[ANY] * 3 + [whole(a) for a in (gain, rep, thin)]
+        + [ANY] * 3 + [whole(we_land), whole(ws_land)] + [ANY] * 2,
+        out_specs=[ANY] * 3 + [whole(outs[3])] + [ANY] * 2,
         out_shape=outs + [full, full],
         scratch_shapes=[
             vmem((rows, width), F32), vmem((rows, width), BF), vmem((rows, width), BF),
             vmem((rows, width), F32), vmem((rows, width), F32),
             vmem((rows, RANK), BF), vmem((RANK, rows), BF), vmem((rows, RANK), BF), vmem((RANK, rows), BF),
             vmem((rows, RANK), F32), vmem((rows, RANK), F32), vmem((rows, RANK), BF),
-            vmem((3, n_dp // 2, 2, depth, size), BF), vmem((3, n_dp // 2, 2, depth, size), BF), DMA((3, 2)),
+            vmem((3, n_dp // 2, 2, depth, size), BF), vmem((3, n_dp // 2, 2, depth, size), BF),
+            vmem(x.shape, BF), vmem(att.shape, BF), vmem(cot.shape, BF), vmem(wo_full.shape, BF),
+            vmem(x.shape, BF), vmem(x.shape, F32), vmem(att.shape, BF), DMA((3, 2)), DMA((4,)), DMA((3,)),
             *Gather.scratch(n_dp, late, late[:1]), *Gather.scratch(n_dp, late, late[:1]),
         ],
         compiler_params=params(collective_id=2, has_side_effects=True),

time: 268 us -> 267 us (level)
  no operation moved by 1% of the time
where the time goes in v7:
time: 267 us; the launch traced here: 264 us
  Pallas kernels  260 us (97%)
  local copies, waits for them, and re-layouts  3.15 us (1%)
    pallas_call x1, Pallas kernels, front_part(): pl.pallas_call(functools.partial(front_kernel, n_dp, n_t, cap), grid=(cou...  98.3 us
    pallas_call x1, Pallas kernels, back_part(): pl.pallas_call(functools.partial(back_kernel, n_dp, n_t, cap, tiles), gri...  88 us
    pallas_call x1, Pallas kernels, middle_both_ways(): pl.pallas_call(functools.partial(middle_kernel, n_dp, n_t, cap, sub), gri...  67 us
    pallas_call x1, Pallas kernels, sum_gradients(): pl.pallas_call(functools.partial(sum_kernel, width, cols, hid), grid=(mid...  6.46 us

profile of v7, /device:TPU:0, one launch (start us, length us, event | category | flops | bytes accessed | tf_op | source)
XLA Modules:
  0.0 264.3 jit_solution(8591434333683522260)
XLA Ops:
  1.3 98.3 %front_part.1 = (bf16[8,784,128]{2,1,0:T(8,128)(2,1)}, f32[8,784,128]{2,1,0:T(8,128)}, bf16[16,784]{1,0:T(8,128)(2,1)}, bf16[4,16,3072]{2,1,0:T(8,128)(2,1)}, bf...) custom-call(s32[2]{0:T(128)} %choice_ref.1, ...), custom_call_target="tpu_custom_call" | custom-call | tf_op jit(solution)/shard_map/front_part/pallas_call | solution.py:576
  99.6 67.0 %middle_both_ways.1 = (bf16[784,1024]{1,0:T(8,128)(2,1)}, f32[784,1024]{1,0:T(8,128)}, bf16[8,784,128]{2,1,0:T(8,128)(2,1)}, bf16[4,16,5504]{2,1,0:T(8,128)(2,1)...) custom-call(bf16[784,1024]{1,0:T(8,128)(2,1)} %get-tuple-element.52.x_in.tok_ref, ...), custom_call_target="tpu_custom_call" | custom-call | tf_op jit(solution)/shard_map/middle_both_ways/pallas_call | solution.py:1020
  166.6 88.0 %back_part.1 = (bf16[784,1024]{1,0:T(8,128)(2,1)}, bf16[4,4,2,16,5504]{4,3,2,1,0:T(8,128)(2,1)}, bf16[784,1024]{1,0:T(8,128)(2,1)}, bf16[4,4,2,16,1792]{4,3,2,1,0:T(8,128)(2,1)}) custom-call(bf16[8,784,128]{2,1,0:T(8,128)(2,1)} %get-tuple-element.45.q_ref, bf16[8,784,128]{2,1,0:T(8,128)(2,1)} %get-tuple-element.46.k_ref, ...), custom_call_target="tpu_custom_call" | custom-call | tf_op jit(solution)/shard_map/back_part/pallas_call | solution.py:811
  254.7 0.0 copy-start.1
  254.7 6.5 %sum_gradients.1 = (f32[8,16,1024]{2,1,0:T(8,128)}, f32[8,3,16,256]{3,2,1,0:T(8,128)}, f32[8,16,256]{2,1,0:T(8,128)}, f32[8,16,1024]{2,1,0:T(8,128)}, f32[8,16,1...) custom-call(bf16[4,8,16,5504]{3,2,1,0:T(8,128)(2,1)} %bitcast.17, ...), custom_call_target="tpu_custom_call" | custom-call | tf_op jit(solution)/shard_map/sum_gradients/pallas_call | solution.py:1080
  261.1 0.0 copy-done.1
  261.1 0.0 copy-start
  261.2 1.2 copy.31
  262.3 0.8 copy-done
  263.1 1.2 copy.32
Async XLA Ops:
  254.7 6.5 %copy-start.1 = (bf16[784,1024]{1,0:T(8,128)(2,1)S(1)}, bf16[784,1024]{1,0:T(8,128)(2,1)}, u32[]{:S(2)}) copy-start(bf16[784,1024]{1,0:T(8,128)(2,1)} %get-tuple-element.90) | copy-start | bytes 4816900
  261.1 2.0 copy-start
